TPU v7x, 32 devices: a whole 2x2x4 slice. The times are simulated.
32 devices in a mesh: fsdp: 16 (over z, y, core), tp: 2 (over x).
Axes of the slice: x: 2, y: 2, z: 4, core: 2. Of those that a mesh axis runs over, the one named last changes fastest.
Arguments:
- tokens: bfloat16 [16384, 1024], P(('fsdp', 'tp')), may hold values from -6 to 6
- out_cotangent: bfloat16 [16384, 1024], P(('fsdp', 'tp')), may hold values from -6 to 6
- attn_gain: float32 [1024], replicated, may hold values from 0.5 to 1.5
- query_weight: bfloat16 [1024, 1024], P('fsdp', 'tp'), may hold values from -0.1875 to 0.1875
- key_weight: bfloat16 [1024, 512], P('fsdp', 'tp'), may hold values from -0.1875 to 0.1875
- value_weight: bfloat16 [1024, 512], P('fsdp', 'tp'), may hold values from -0.1875 to 0.1875
- query_gain: float32 [64], replicated, may hold values from 0.5 to 1.5
- key_gain: float32 [64], replicated, may hold values from 0.5 to 1.5
- out_weight: bfloat16 [1024, 1024], P('tp', 'fsdp'), may hold values from -1.5 to 1.5
- ffn_gain: float32 [1024], replicated, may hold values from 0.5 to 1.5
- gate_weight: bfloat16 [1024, 4608], P('fsdp', 'tp'), may hold values from -0.1875 to 0.1875
- up_weight: bfloat16 [1024, 4608], P('fsdp', 'tp'), may hold values from -0.1875 to 0.1875
- down_weight: bfloat16 [4608, 1024], P('tp', 'fsdp'), may hold values from -0.09375 to 0.09375
Outputs:
- output: bfloat16 [16384, 1024], P(('fsdp', 'tp'))
- tokens_grad: float32 [16384, 1024], P(('fsdp', 'tp'))
- attn_gain_grad: float32 [1024], replicated
- query_weight_grad: float32 [1024, 1024], P('fsdp', 'tp')
- key_weight_grad: float32 [1024, 512], P('fsdp', 'tp')
- value_weight_grad: float32 [1024, 512], P('fsdp', 'tp')
- query_gain_grad: float32 [64], replicated
- key_gain_grad: float32 [64], replicated
- out_weight_grad: float32 [1024, 1024], P('tp', 'fsdp')
- ffn_gain_grad: float32 [1024], replicated
- gate_weight_grad: float32 [1024, 4608], P('fsdp', 'tp')
- up_weight_grad: float32 [1024, 4608], P('fsdp', 'tp')
- down_weight_grad: float32 [4608, 1024], P('tp', 'fsdp')
All inputs are finite; a program needn't handle non-finite values.
Results may differ from a plain program's by a relative error of at most 0.02.
Values may be sent and summed in bfloat16 or wider, within the bound.
No kernel may reach another device: no remote copies, remote signals or barrier semaphores. Data moves between devices by JAX's collectives and lax.ppermute only.
A program may use at most 256 MiB of HBM per device.

v0:
```python
from functools import partial

import jax
import jax.numpy as jnp
from jax import lax
from jax.sharding import PartitionSpec as P

HD = 64


eps = 1e-05
theta_base = 1000000.0


def rms_norm(values, gain):
    return values * lax.rsqrt(jnp.mean(values * values, axis=-1, keepdims=True) + eps) * gain


def rotary_tables(length):
    half_size = HD // 2
    frequency = theta_base ** (-jnp.arange(half_size, dtype=jnp.float32) * 2.0 / HD)
    angles = jnp.arange(length, dtype=jnp.float32)[:, None] * frequency[None, :]
    cosine = jnp.concatenate([jnp.cos(angles), jnp.cos(angles)], axis=-1)
    sine_table = jnp.concatenate([jnp.sin(angles), jnp.sin(angles)], axis=-1)
    return (cosine, sine_table)


def rotate(values, cosine, sine_table):
    half_size = values.shape[-1] // 2
    turned = jnp.concatenate([-values[..., half_size:], values[..., :half_size]], axis=-1)
    return values * cosine[:, None, :] + turned * sine_table[:, None, :]


def prepare(cosine, sine_table, query_raw, key_raw, query_gain, key_gain):
    length = query_raw.shape[0]
    query_rows = rotate(rms_norm(query_raw.reshape(length, -1, HD), query_gain), cosine, sine_table)
    key_rows = rotate(rms_norm(key_raw.reshape(length, -1, HD), key_gain), cosine, sine_table)
    return (query_rows, key_rows)


def swiglu(gate_rows, up_rows):
    return jax.nn.silu(gate_rows) * up_rows


def dot_transposed(former, latter):
    return lax.dot_general(
        former, latter, (((1,), (1,)), ((), ())), preferred_element_type=jnp.float32
    )


def dot_leading(former, latter):
    return lax.dot_general(
        former, latter, (((0,), (0,)), ((), ())), preferred_element_type=jnp.float32
    )


def widen(rows):
    return lax.all_gather(rows, "tp", axis=0, tiled=True)


def narrow(terms):
    return lax.psum_scatter(terms, "tp", scatter_dimension=0, tiled=True)


def widen_grad(rows):
    return lax.all_gather(rows, "tp", axis=0, tiled=True)


def narrow_grad(terms):
    return lax.psum_scatter(
        terms.astype(jnp.bfloat16), "tp", scatter_dimension=0, tiled=True
    ).astype(jnp.float32)


def block_scores(query_block, key_rows, row_start, finish):
    block_rows = query_block.shape[0]
    scores = jnp.einsum(
        "qkgd,skd->kgqs", query_block, key_rows[:finish], preferred_element_type=jnp.float32
    ) * HD ** (-0.5)
    causal = (row_start + jnp.arange(block_rows))[:, None] >= jnp.arange(finish)[None, :]
    return jnp.where(causal, scores, -1e30)


def attend(query_rows, key_rows, value_rows):
    length = query_rows.shape[0]
    heads_local = query_rows.shape[1]
    kv_local = key_rows.shape[1]
    grouped = query_rows.reshape(length, kv_local, heads_local // kv_local, HD)
    block_rows = min(512, length)
    outputs = []
    log_totals = []
    for block_index in range(length // block_rows):
        row_start = block_index * block_rows
        finish = row_start + block_rows
        scores = block_scores(grouped[row_start:finish], key_rows, row_start, finish)
        largest = jnp.max(scores, axis=-1, keepdims=True)
        exponent = jnp.exp(scores - largest)
        row_total = jnp.sum(exponent, axis=-1, keepdims=True)
        probability = (exponent / row_total).astype(jnp.bfloat16)
        attended = jnp.einsum(
            "kgqs,skd->qkgd", probability, value_rows[:finish], preferred_element_type=jnp.float32
        )
        outputs.append(attended.astype(jnp.bfloat16).reshape(block_rows, heads_local * HD))
        log_totals.append(largest + jnp.log(row_total))
    return (jnp.concatenate(outputs, axis=0), log_totals)


def attend_back(query_rows, key_rows, value_rows, log_totals, attended_grad):
    length = query_rows.shape[0]
    heads_local = query_rows.shape[1]
    kv_local = key_rows.shape[1]
    group_size = heads_local // kv_local
    grouped = query_rows.reshape(length, kv_local, group_size, HD)
    grad_grouped = attended_grad.reshape(length, kv_local, group_size, HD)
    block_rows = min(512, length)
    key_grad = jnp.zeros(key_rows.shape, jnp.float32)
    value_grad = jnp.zeros(value_rows.shape, jnp.float32)
    query_parts = []
    for block_index in range(length // block_rows):
        row_start = block_index * block_rows
        finish = row_start + block_rows
        query_block = grouped[row_start:finish]
        grad_block = grad_grouped[row_start:finish]
        scores = block_scores(query_block, key_rows, row_start, finish)
        probability = jnp.exp(scores - log_totals[block_index])
        prob_grad = jnp.einsum(
            "qkgd,skd->kgqs", grad_block, value_rows[:finish], preferred_element_type=jnp.float32
        )
        inner_sum = jnp.sum(probability * prob_grad, axis=-1, keepdims=True)
        score_grad = (probability * (prob_grad - inner_sum)).astype(jnp.bfloat16)
        query_parts.append(
            jnp.einsum(
                "kgqs,skd->qkgd", score_grad, key_rows[:finish], preferred_element_type=jnp.float32
            )
            * HD ** (-0.5)
        )
        key_grad = key_grad.at[:finish].add(
            jnp.einsum(
                "kgqs,qkgd->skd", score_grad, query_block, preferred_element_type=jnp.float32
            )
            * HD ** (-0.5)
        )
        value_grad = value_grad.at[:finish].add(
            jnp.einsum(
                "kgqs,qkgd->skd",
                probability.astype(jnp.bfloat16),
                grad_block,
                preferred_element_type=jnp.float32,
            )
        )
    query_grad = jnp.concatenate(query_parts, axis=0).reshape(length, heads_local, HD)
    return (query_grad, key_grad, value_grad)


def on_device(
    tokens,
    out_cotangent,
    attn_gain,
    query_weight,
    key_weight,
    value_weight,
    query_gain,
    key_gain,
    out_weight,
    ffn_gain,
    gate_weight,
    up_weight,
    down_weight,
):
    query_full, key_full, value_full, gate_full, up_full = (
        lax.all_gather(query_weight, "fsdp", axis=0, tiled=True),
        lax.all_gather(key_weight, "fsdp", axis=0, tiled=True),
        lax.all_gather(value_weight, "fsdp", axis=0, tiled=True),
        lax.all_gather(gate_weight, "fsdp", axis=0, tiled=True),
        lax.all_gather(up_weight, "fsdp", axis=0, tiled=True),
    )
    out_full, down_full = (
        lax.all_gather(out_weight, "fsdp", axis=1, tiled=True),
        lax.all_gather(down_weight, "fsdp", axis=1, tiled=True),
    )
    residual = tokens.astype(jnp.float32)
    normed, attn_norm_pull = jax.vjp(rms_norm, residual, attn_gain)
    normed_rows = widen(normed.astype(jnp.bfloat16))
    length = normed_rows.shape[0]
    cosine, sine_table = rotary_tables(length)
    query_raw = jnp.dot(normed_rows, query_full, preferred_element_type=jnp.float32)
    key_raw = jnp.dot(normed_rows, key_full, preferred_element_type=jnp.float32)
    value_raw = jnp.dot(normed_rows, value_full, preferred_element_type=jnp.float32)
    (query_rows, key_rows), prepare_pull = jax.vjp(
        partial(prepare, cosine, sine_table), query_raw, key_raw, query_gain, key_gain
    )
    query_rows = query_rows.astype(jnp.bfloat16)
    key_rows = key_rows.astype(jnp.bfloat16)
    value_rows = value_raw.astype(jnp.bfloat16).reshape(length, -1, HD)
    attended, log_totals = attend(query_rows, key_rows, value_rows)
    middle = residual + narrow(jnp.dot(attended, out_full, preferred_element_type=jnp.float32))
    normed_ffn, ffn_norm_pull = jax.vjp(rms_norm, middle, ffn_gain)
    ffn_rows = widen(normed_ffn.astype(jnp.bfloat16))
    gate_rows = jnp.dot(ffn_rows, gate_full, preferred_element_type=jnp.float32)
    up_rows = jnp.dot(ffn_rows, up_full, preferred_element_type=jnp.float32)
    hidden, swiglu_pull = jax.vjp(swiglu, gate_rows, up_rows)
    hidden = hidden.astype(jnp.bfloat16)
    output = (
        middle + narrow(jnp.dot(hidden, down_full, preferred_element_type=jnp.float32))
    ).astype(jnp.bfloat16)
    query_full, key_full, value_full, gate_full, up_full = (
        lax.all_gather(query_weight, "fsdp", axis=0, tiled=True),
        lax.all_gather(key_weight, "fsdp", axis=0, tiled=True),
        lax.all_gather(value_weight, "fsdp", axis=0, tiled=True),
        lax.all_gather(gate_weight, "fsdp", axis=0, tiled=True),
        lax.all_gather(up_weight, "fsdp", axis=0, tiled=True),
    )
    out_full, down_full = (
        lax.all_gather(out_weight, "fsdp", axis=1, tiled=True),
        lax.all_gather(down_weight, "fsdp", axis=1, tiled=True),
    )
    upstream = out_cotangent.astype(jnp.float32)
    cotangent_rows = widen_grad(out_cotangent)
    down_grad = dot_leading(hidden, cotangent_rows)
    hidden_grad = dot_transposed(cotangent_rows, down_full)
    gate_grad, up_grad = swiglu_pull(hidden_grad)
    gate_grad = gate_grad.astype(jnp.bfloat16)
    up_grad = up_grad.astype(jnp.bfloat16)
    gate_weight_grad = dot_leading(ffn_rows, gate_grad)
    up_weight_grad = dot_leading(ffn_rows, up_grad)
    ffn_normed_grad = narrow_grad(
        dot_transposed(gate_grad, gate_full) + dot_transposed(up_grad, up_full)
    )
    middle_piece, ffn_gain_local = ffn_norm_pull(ffn_normed_grad)
    middle_grad = upstream + middle_piece
    branch_rows = widen_grad(middle_grad.astype(jnp.bfloat16))
    out_weight_grad = dot_leading(attended, branch_rows)
    attended_grad = dot_transposed(branch_rows, out_full).astype(jnp.bfloat16)
    query_grad, key_grad, value_grad = attend_back(
        query_rows, key_rows, value_rows, log_totals, attended_grad
    )
    query_raw_grad, key_raw_grad, query_gain_local, key_gain_local = prepare_pull(
        (query_grad, key_grad)
    )
    query_raw_grad = query_raw_grad.astype(jnp.bfloat16)
    key_raw_grad = key_raw_grad.astype(jnp.bfloat16)
    value_raw_grad = value_grad.reshape(length, -1).astype(jnp.bfloat16)
    query_weight_grad = dot_leading(normed_rows, query_raw_grad)
    key_weight_grad = dot_leading(normed_rows, key_raw_grad)
    value_weight_grad = dot_leading(normed_rows, value_raw_grad)
    normed_grad = narrow_grad(
        dot_transposed(query_raw_grad, query_full)
        + dot_transposed(key_raw_grad, key_full)
        + dot_transposed(value_raw_grad, value_full)
    )
    tokens_piece, attn_gain_local = attn_norm_pull(normed_grad)
    tokens_grad = middle_grad + tokens_piece
    gain_totals = lax.psum(
        (attn_gain_local, query_gain_local, key_gain_local, ffn_gain_local), ("fsdp", "tp")
    )
    inner_grads = (
        lax.psum_scatter(
            query_weight_grad.astype(jnp.bfloat16), "fsdp", scatter_dimension=0, tiled=True
        ).astype(jnp.float32),
        lax.psum_scatter(
            key_weight_grad.astype(jnp.bfloat16), "fsdp", scatter_dimension=0, tiled=True
        ).astype(jnp.float32),
        lax.psum_scatter(
            value_weight_grad.astype(jnp.bfloat16), "fsdp", scatter_dimension=0, tiled=True
        ).astype(jnp.float32),
        lax.psum_scatter(
            gate_weight_grad.astype(jnp.bfloat16), "fsdp", scatter_dimension=0, tiled=True
        ).astype(jnp.float32),
        lax.psum_scatter(
            up_weight_grad.astype(jnp.bfloat16), "fsdp", scatter_dimension=0, tiled=True
        ).astype(jnp.float32),
    )
    outer_grads = (
        lax.psum_scatter(
            out_weight_grad.astype(jnp.bfloat16), "fsdp", scatter_dimension=1, tiled=True
        ).astype(jnp.float32),
        lax.psum_scatter(
            down_grad.astype(jnp.bfloat16), "fsdp", scatter_dimension=1, tiled=True
        ).astype(jnp.float32),
    )
    return (
        output,
        tokens_grad,
        gain_totals[0],
        inner_grads[0],
        inner_grads[1],
        inner_grads[2],
        gain_totals[1],
        gain_totals[2],
        outer_grads[0],
        gain_totals[3],
        inner_grads[3],
        inner_grads[4],
        outer_grads[1],
    )


def solution(mesh):
    placed = (
        P(("fsdp", "tp"), None),
        P(("fsdp", "tp"), None),
        P(),
        P("fsdp", "tp"),
        P("fsdp", "tp"),
        P("fsdp", "tp"),
        P(),
        P(),
        P("tp", "fsdp"),
        P(),
        P("fsdp", "tp"),
        P("fsdp", "tp"),
        P("tp", "fsdp"),
    )
    return jax.shard_map(
        on_device,
        mesh=mesh,
        in_specs=placed,
        out_specs=(
            P(("fsdp", "tp"), None),
            P(("fsdp", "tp"), None),
            P(),
            P("fsdp", "tp"),
            P("fsdp", "tp"),
            P("fsdp", "tp"),
            P(),
            P(),
            P("tp", "fsdp"),
            P(),
            P("fsdp", "tp"),
            P("fsdp", "tp"),
            P("tp", "fsdp"),
        ),
        check_vma=False,
    )
```

profile of v0, /device:TPU:0, one launch (start us, length us, event | category | flops | bytes accessed | tf_op | source)
XLA Modules:
  0.0 1099.7 jit_solution(16615849046763055739)
XLA Ops:
  14.8 24.6 %all_gather.42 = bf16[1024,256]{1,0:T(8,128)(2,1)S(1)} all-gather(bf16[64,256]{1,0:T(8,128)(2,1)S(1)} %copy-done.50), channel_id=1, replica_groups=mesh['fsdp'=16,'tp'=2] {'fsdp'}, dimensions={0}, use_global_device_ids=true | all-gather | bytes 557056 | tf_op jit(solution)/shard_map/all_gather | solution.py:172
  39.3 19.0 %all_gather.41 = bf16[1024,256]{1,0:T(8,128)(2,1)S(1)} all-gather(bf16[64,256]{1,0:T(8,128)(2,1)S(1)} %copy-done.51), channel_id=1, replica_groups=mesh['fsdp'=16,'tp'=2] {'fsdp'}, dimensions={0}, use_global_device_ids=true | all-gather | bytes 557056 | tf_op jit(solution)/shard_map/all_gather | solution.py:173
  64.2 23.2 %all-gather.12.cloned.1.call-done = bf16[1024,512]{1,0:T(8,128)(2,1)} async-done(((bf16[64,512]{1,0:T(8,128)(2,1)}), bf16[1024,512]{1,0:T(8,128)(2,1)}) %all-gather.12.cloned.1.call-update) | async-done | bytes 1048592 | tf_op jit(solution)/shard_map/all_gather | solution.py:171
  87.4 3.2 multiply_reduce_fusion.3
  99.6 7.5 fusion.80
  107.1 8.2 fusion.3
  115.3 7.4 fusion.54
  122.8 3.7 all-gather.14.cloned.1.call-done
  126.5 4.5 fusion.63
  131.7 52.7 %reduce-scatter.12.cloned.1.call-done = f32[512,1024]{1,0:T(8,128)} async-done(((f32[1024,1024]{1,0:T(8,128)}), f32[512,1024]{1,0:T(8,128)}) %reduce-scatter.12.cloned.1.call-update) | async-done | bytes 2097168 | tf_op jit(solution)/shard_map/reduce_scatter | solution.py:62
  190.1 50.1 %all-gather.20.cloned.1.call-done = bf16[1024,2304]{1,0:T(8,128)(2,1)} async-done(((bf16[64,2304]{1,0:T(8,128)(2,1)}), bf16[1024,2304]{1,0:T(8,128)(2,1)}) %all-gather.20.cloned.1.call-update) | async-done | bytes 4718608 | tf_op jit(solution)/shard_map/all_gather | solution.py:175
  240.2 33.7 %all-gather.16.cloned.1.call-done = bf16[1024,1024]{1,0:T(8,128)(2,1)} async-done(((bf16[512,1024]{1,0:T(8,128)(2,1)}), bf16[1024,1024]{1,0:T(8,128)(2,1)}) %all-gather.16.cloned.1.call-update) | async-done | bytes 2097168 | tf_op jit(solution)/shard_map/all_gather | solution.py:58
  274.0 10.2 fusion.83
  284.2 45.7 %all-gather.18.cloned.1.call-done = bf16[1024,2304]{1,0:T(8,128)(2,1)} async-done(((bf16[64,2304]{1,0:T(8,128)(2,1)}), bf16[1024,2304]{1,0:T(8,128)(2,1)}) %all-gather.18.cloned.1.call-update) | async-done | bytes 4718608 | tf_op jit(solution)/shard_map/all_gather | solution.py:174
  329.9 10.1 fusion.82
  340.0 23.3 %all-gather.24.cloned.1.call-done = bf16[1024,1024]{1,0:T(8,128)(2,1)} async-done(((bf16[512,1024]{1,0:T(8,128)(2,1)}), bf16[1024,1024]{1,0:T(8,128)(2,1)}) %all-gather.24.cloned.1.call-update) | async-done | bytes 2097168 | tf_op jit(solution)/shard_map/all_gather | solution.py:66
  363.2 56.0 %all-gather.22.cloned.1.call-done = bf16[2304,1024]{0,1:T(8,128)(2,1)} async-done(((bf16[2304,64]{0,1:T(8,128)(2,1)}), bf16[2304,1024]{0,1:T(8,128)(2,1)}) %all-gather.22.cloned.1.call-update) | async-done | bytes 4718608 | tf_op jit(solution)/shard_map/all_gather | solution.py:179
  419.2 18.0 %multiply_convert_fusion = (bf16[1024,2304]{1,0:T(8,128)(2,1)}, bf16[1024,2304]{1,0:T(8,128)(2,1)}, bf16[1024,2304]{1,0:T(8,128)(2,1)}) fusion(f32[1024,2304]{1,0:T(8,128)} %fusion.82, f32[1024,2304]{1,0:T(8,128)} %fusion.83, bf16[1024,1024]{1,0:T(8,128)(2,1)} %all-gather.24.cloned.1.call-done, bf16[2304,1024]{0,1:T(8,128)(2,1)} %all-gather.22.cloned.1.call-done), kind=kOutput, calls=%fused_computation.15 | convolution fusion | flops 4869586944 | bytes 39845888 | tf_op jit(solution)/shard_map/dot_general | solution.py:46
  437.2 7.1 fusion.85
  444.3 8.6 add_convert_fusion.1
  453.3 30.2 %reduce-scatter.16.cloned.1.call-done = bf16[512,1024]{1,0:T(8,128)(2,1)} async-done(((bf16[1024,1024]{1,0:T(8,128)(2,1)}), bf16[512,1024]{1,0:T(8,128)(2,1)}) %reduce-scatter.16.cloned.1.call-update) | async-done | bytes 1048592 | tf_op jit(solution)/shard_map/reduce_scatter | solution.py:70
  486.1 3.2 fusion.74
  489.3 9.5 convolution_convert_fusion.1
  498.9 9.4 convolution_convert_fusion.2
  508.9 13.6 %all-gather.26.cloned.1.call-done = bf16[1024,1024]{1,0:T(8,128)(2,1)} async-done(((bf16[512,1024]{1,0:T(8,128)(2,1)}), bf16[1024,1024]{1,0:T(8,128)(2,1)}) %all-gather.26.cloned.1.call-update) | async-done | bytes 2097168 | tf_op jit(solution)/shard_map/all_gather | solution.py:66
  522.5 3.1 convolution_convert_fusion.5
  525.8 5.0 fusion.55
  530.8 9.5 fusion.50
  542.7 9.8 convolution_convert_fusion
  553.4 6.0 fusion.11
  559.5 5.0 fusion.13
  568.6 10.5 fusion
  579.2 11.2 %fusion.2 = bf16[4,2,512,1024]{2,3,1,0:T(8,128)(2,1)} fusion(f32[4,1024,512,2]{2,1,3,0:T(8,128)} %get-tuple-element.121, f32[4,2,512,1024]{2,3,1,0:T(8,128)S(1)} %bitcast.187, f32[4,2,512]{2,1,0:T(2,128)S(1)} %get-tuple-element.120, f32[4,2,512]{2,1,0:T(2,128)S(1)} %bitcast.210), kind=kLoop, calls=%fused_computation.4 | loop fusion | flops 16777216 | bytes 41975808 | tf_op jit(solution)/shard_map/convert_element_type | solution.py:130
  590.4 6.2 broadcast_multiply_fusion
  600.0 4.0 fusion.46
  604.0 5.9 fusion.45
  629.0 2.7 add_convert_fusion
  631.8 9.7 fusion.84
  643.4 37.5 %reduce-scatter.28.cloned.1.call-done = bf16[64,2304]{1,0:T(8,128)(2,1)} async-done(((bf16[1024,2304]{1,0:T(8,128)(2,1)}), bf16[64,2304]{1,0:T(8,128)(2,1)}) %reduce-scatter.28.cloned.1.call-update) | async-done | bytes 294928 | tf_op jit(solution)/shard_map/reduce_scatter | solution.py:266
  682.7 56.5 %reduce-scatter.24.cloned.1.call-done = bf16[64,256]{1,0:T(8,128)(2,1)} async-done(((bf16[1024,256]{1,0:T(8,128)(2,1)}), bf16[64,256]{1,0:T(8,128)(2,1)}) %reduce-scatter.24.cloned.1.call-update) | async-done | bytes 32784 | tf_op jit(solution)/shard_map/reduce_scatter | solution.py:263
  740.5 77.4 %reduce-scatter.32.cloned.1.call-done = bf16[2304,64]{0,1:T(8,128)(2,1)} async-done(((bf16[2304,1024]{0,1:T(8,128)(2,1)}), bf16[2304,64]{0,1:T(8,128)(2,1)}) %reduce-scatter.32.cloned.1.call-update) | async-done | bytes 294928 | tf_op jit(solution)/shard_map/reduce_scatter | solution.py:277
  819.8 56.5 %reduce-scatter.22.cloned.1.call-done = bf16[64,256]{1,0:T(8,128)(2,1)} async-done(((bf16[1024,256]{1,0:T(8,128)(2,1)}), bf16[64,256]{1,0:T(8,128)(2,1)}) %reduce-scatter.22.cloned.1.call-update) | async-done | bytes 32784 | tf_op jit(solution)/shard_map/reduce_scatter | solution.py:260
  877.6 58.9 %reduce-scatter.26.cloned.1.call-done = bf16[512,64]{0,1:T(8,128)(2,1)} async-done(((bf16[512,1024]{0,1:T(8,128)(2,1)}), bf16[512,64]{0,1:T(8,128)(2,1)}) %reduce-scatter.26.cloned.1.call-update) | async-done | bytes 65552 | tf_op jit(solution)/shard_map/reduce_scatter | solution.py:274
  938.0 58.4 %reduce-scatter.20.cloned.1.call-done = bf16[64,512]{1,0:T(8,128)(2,1)} async-done(((bf16[1024,512]{1,0:T(8,128)(2,1)}), bf16[64,512]{1,0:T(8,128)(2,1)}) %reduce-scatter.20.cloned.1.call-update) | async-done | bytes 65552 | tf_op jit(solution)/shard_map/reduce_scatter | solution.py:257
  998.0 32.3 %reduce-scatter.18.cloned.1.call-done = bf16[512,1024]{1,0:T(8,128)(2,1)} async-done(((bf16[1024,1024]{1,0:T(8,128)(2,1)}), bf16[512,1024]{1,0:T(8,128)(2,1)}) %reduce-scatter.18.cloned.1.call-update) | async-done | bytes 1048592 | tf_op jit(solution)/shard_map/reduce_scatter | solution.py:70
  1032.8 40.0 %all-reduce.6 = (f32[1024]{0:T(1024)}, f32[64]{0:T(128)}, f32[64]{0:T(128)}, f32[1024]{0:T(1024)}) all-reduce(f32[1024]{0:T(1024)S(1)} %get-tuple-element.81, f32[64]{0:T(128)S(1)} %get-tuple-element.79, f32[64]{0:T(128)S(1)} %get-tuple-element.83, f32[1024]{0:T(1024)S(1)} %copy-done.58), channel_id=1, replica_groups=mesh['fsdp'=16,'tp'=2] {'fsdp','tp'}, use_global_device_ids=true, to_apply=%region_19.20 | all-reduce | flops 2176 | bytes 17408 | tf_op jit(solution)/shard_map/psum | solution.py:253
  1072.8 15.2 %reduce-scatter.14.cloned.1.call-done = f32[512,1024]{1,0:T(8,128)} async-done(((f32[1024,1024]{1,0:T(8,128)}), f32[512,1024]{1,0:T(8,128)}) %reduce-scatter.14.cloned.1.call-update) | async-done | bytes 2097168 | tf_op jit(solution)/shard_map/reduce_scatter | solution.py:62
  1088.0 4.6 fusion.32
  (250 shorter events, 75.6 us)
Async XLA Ops:
  7.2 32.1 %copy-start.51 = (bf16[64,256]{1,0:T(8,128)(2,1)S(1)}, bf16[64,256]{1,0:T(8,128)(2,1)}, u32[]{:S(2)}) copy-start(bf16[64,256]{1,0:T(8,128)(2,1)} %param.30) | copy-start | bytes 98308
  7.2 51.1 %all-gather.10.cloned.1.call-start = ((), (), s32[]{:S(2)}) async-start(), calls=%async_computation.11 | async-start | bytes 3145728 | tf_op jit(solution)/shard_map/all_gather | solution.py:58
  11.3 76.1 %all-gather.12.cloned.1.call-start = ((), (), s32[]{:S(2)}) async-start(), calls=%async_computation.12 | async-start | bytes 1114112 | tf_op jit(solution)/shard_map/all_gather | solution.py:171
  12.1 114.4 %all-gather.14.cloned.1.call-start = ((), (), s32[]{:S(2)}) async-start(), calls=%async_computation.13 | async-start | bytes 1114112 | tf_op jit(solution)/shard_map/all_gather | solution.py:178
  12.8 171.6 %reduce-scatter.12.cloned.1.call-start = ((), (), s32[]{:S(2)}) async-start(), calls=%async_computation.14 | async-start | bytes 6291456 | tf_op jit(solution)/shard_map/reduce_scatter | solution.py:62
  13.5 79.3 %copy-start.12 = (f32[1024,64]{0,1:T(8,128)}, f32[1024,64]{0,1:T(8,128)S(1)}, u32[]{:S(2)}) copy-start(f32[1024,64]{0,1:T(8,128)S(1)} %pad_maximum_fusion.4) | copy-start | bytes 786436
  13.6 79.2 %copy-start.8 = (f32[1024,64]{0,1:T(8,128)}, f32[1024,64]{0,1:T(8,128)S(1)}, u32[]{:S(2)}) copy-start(f32[1024,64]{0,1:T(8,128)S(1)} %pad_maximum_fusion.5) | copy-start | bytes 786436
  39.3 24.7 %copy-start.17 = (bf16[1024,256]{1,0:T(8,128)(2,1)}, bf16[1024,256]{1,0:T(8,128)(2,1)S(1)}, u32[]{:S(2)}) copy-start(bf16[1024,256]{1,0:T(8,128)(2,1)S(1)} %all_gather.42) | copy-start | bytes 1572868
  39.3 24.5 %copy-start.61 = (f32[64]{0:T(128)S(1)}, f32[64]{0:T(128)}, u32[]{:S(2)}) copy-start(f32[64]{0:T(128)} %param.32) | copy-start | bytes 772
  63.2 29.6 %copy-start.4 = (f32[1024,256]{0,1:T(8,128)}, f32[1024,256]{0,1:T(8,128)S(1)}, u32[]{:S(2)}) copy-start(f32[1024,256]{0,1:T(8,128)S(1)} %get-tuple-element.115) | copy-start | bytes 3145732
  63.3 29.5 %copy-start.41 = (f32[1024,4]{0,1:T(4,128)}, f32[1024,4]{0,1:T(4,128)S(1)}, u32[]{:S(2)}) copy-start(f32[1024,4]{0,1:T(4,128)S(1)} %fusion.69) | copy-start | bytes 49156
  64.1 26.6 %copy-start.59 = (f32[64]{0:T(128)S(1)}, f32[64]{0:T(128)}, u32[]{:S(2)}) copy-start(f32[64]{0:T(128)} %param.31) | copy-start | bytes 772
  99.6 26.9 %copy-start.65 = (bf16[4,64,2,512]{3,1,2,0:T(8,128)(2,1)}, bf16[4,64,2,512]{3,1,2,0:T(8,128)(2,1)S(1)}, u32[]{:S(2)}) copy-start(bf16[4,64,2,512]{3,1,2,0:T(8,128)(2,1)S(1)} %fusion.53) | copy-start | bytes 1572868
  107.1 8.2 copy-start.36
  122.8 8.2 copy-start.67
  131.0 55.6 %copy-start.48 = (f32[1024]{0:T(1024)S(1)}, f32[1024]{0:T(1024)}, u32[]{:S(2)}) copy-start(f32[1024]{0:T(1024)} %param.34) | copy-start | bytes 12292
  131.0 109.2 %all-gather.20.cloned.1.call-start = ((), (), s32[]{:S(2)}) async-start(), calls=%async_computation.17 | async-start | bytes 5013504 | tf_op jit(solution)/shard_map/all_gather | solution.py:175
  131.6 142.3 %all-gather.16.cloned.1.call-start = ((), (), s32[]{:S(2)}) async-start(), calls=%async_computation.15 | async-start | bytes 3145728 | tf_op jit(solution)/shard_map/all_gather | solution.py:58
  187.8 142.1 %all-gather.18.cloned.1.call-start = ((), (), s32[]{:S(2)}) async-start(), calls=%async_computation.16 | async-start | bytes 5013504 | tf_op jit(solution)/shard_map/all_gather | solution.py:174
  188.6 174.7 %all-gather.24.cloned.1.call-start = ((), (), s32[]{:S(2)}) async-start(), calls=%async_computation.20 | async-start | bytes 3145728 | tf_op jit(solution)/shard_map/all_gather | solution.py:66
  189.3 229.9 %all-gather.22.cloned.1.call-start = ((), (), s32[]{:S(2)}) async-start(), calls=%async_computation.18 | async-start | bytes 5013504 | tf_op jit(solution)/shard_map/all_gather | solution.py:179
  190.1 293.4 %reduce-scatter.16.cloned.1.call-start = ((), (), s32[]{:S(2)}) async-start(), calls=%async_computation.21 | async-start | bytes 3145728 | tf_op jit(solution)/shard_map/reduce_scatter | solution.py:70
  419.2 18.0 %copy-start.63 = (bf16[1024,2304]{1,0:T(8,128)(2,1)S(1)}, bf16[1024,2304]{1,0:T(8,128)(2,1)}, u32[]{:S(2)}) copy-start(bf16[1024,2304]{1,0:T(8,128)(2,1)} %all-gather.18.cloned.1.call-done) | copy-start | bytes 14155780
  453.0 69.6 %all-gather.26.cloned.1.call-start = ((), (), s32[]{:S(2)}) async-start(), calls=%async_computation.22 | async-start | bytes 3145728 | tf_op jit(solution)/shard_map/all_gather | solution.py:66
  486.1 12.8 %copy-start.56 = (f32[512]{0:T(512)}, f32[512]{0:T(512)S(1)}, u32[]{:S(2)}) copy-start(f32[512]{0:T(512)S(1)} %multiply_multiply_fusion.5) | copy-start | bytes 6148
  489.3 152.3 %reduce-scatter.30.cloned.1.call-start = ((), (), s32[]{:S(2)}) async-start(), calls=%async_computation.29 | async-start | bytes 5013504 | tf_op jit(solution)/shard_map/reduce_scatter | solution.py:269
  498.8 182.0 %reduce-scatter.28.cloned.1.call-start = ((), (), s32[]{:S(2)}) async-start(), calls=%async_computation.28 | async-start | bytes 5013504 | tf_op jit(solution)/shard_map/reduce_scatter | solution.py:266
  508.3 230.8 %reduce-scatter.24.cloned.1.call-start = ((), (), s32[]{:S(2)}) async-start(), calls=%async_computation.26 | async-start | bytes 557056 | tf_op jit(solution)/shard_map/reduce_scatter | solution.py:263
  508.9 43.7 %copy-start.43 = (f32[1,8,512]{2,1,0:T(8,128)}, f32[1,8,512]{2,1,0:T(8,128)S(1)}, u32[]{:S(2)}) copy-start(f32[1,8,512]{2,1,0:T(8,128)S(1)} %log_add_fusion.1) | copy-start | bytes 49156
  530.8 10.3 copy-start.25
  542.7 275.3 %reduce-scatter.32.cloned.1.call-start = ((), (), s32[]{:S(2)}) async-start(), calls=%async_computation.30 | async-start | bytes 5013504 | tf_op jit(solution)/shard_map/reduce_scatter | solution.py:277
  552.5 323.7 %reduce-scatter.22.cloned.1.call-start = ((), (), s32[]{:S(2)}) async-start(), calls=%async_computation.25 | async-start | bytes 557056 | tf_op jit(solution)/shard_map/reduce_scatter | solution.py:260
  553.4 15.1 %slice-start = ((s8[16777216]{0:T(1024)(128)(4,1)}), s8[4194304]{0:T(1024)(128)(4,1)S(1)}, s32[]{:S(2)}) async-start(s8[16777216]{0:T(1024)(128)(4,1)} %bitcast.186), calls=%async_computation.31 | async-start | bytes 8388608
  553.4 15.1 %slice-start.1 = ((s8[16777216]{0:T(1024)(128)(4,1)}), s8[4194304]{0:T(1024)(128)(4,1)S(1)}, s32[]{:S(2)}) async-start(s8[16777216]{0:T(1024)(128)(4,1)} %bitcast.186), calls=%async_computation.32 | async-start | bytes 8388608
  559.4 9.1 slice-start.2
  559.5 9.1 slice-start.3
  579.2 11.2 %copy-start.9 = (f32[1024,64]{0,1:T(8,128)S(1)}, f32[1024,64]{0,1:T(8,128)}, u32[]{:S(2)}) copy-start(f32[1024,64]{0,1:T(8,128)} %copy-done.8) | copy-start | bytes 786436
  579.2 11.2 %copy-start.23 = (f32[512,4,64]{0,2,1:T(8,128)S(1)}, f32[512,4,64]{0,2,1:T(8,128)}, u32[]{:S(2)}) copy-start(f32[512,4,64]{0,2,1:T(8,128)} %fusion.59) | copy-start | bytes 1572868
  579.2 11.2 %copy-start.30 = (bf16[512,8,64]{0,2,1:T(8,128)(2,1)S(1)}, bf16[512,8,64]{0,2,1:T(8,128)(2,1)}, u32[]{:S(2)}) copy-start(bf16[512,8,64]{0,2,1:T(8,128)(2,1)} %copy-done.29) | copy-start | bytes 1572868
  609.9 326.6 %reduce-scatter.26.cloned.1.call-start = ((), (), s32[]{:S(2)}) async-start(), calls=%async_computation.27 | async-start | bytes 1114112 | tf_op jit(solution)/shard_map/reduce_scatter | solution.py:274
  617.3 379.1 %reduce-scatter.20.cloned.1.call-start = ((), (), s32[]{:S(2)}) async-start(), calls=%async_computation.24 | async-start | bytes 1114112 | tf_op jit(solution)/shard_map/reduce_scatter | solution.py:257
  626.2 404.1 %reduce-scatter.18.cloned.1.call-start = ((), (), s32[]{:S(2)}) async-start(), calls=%async_computation.23 | async-start | bytes 3145728 | tf_op jit(solution)/shard_map/reduce_scatter | solution.py:70
  631.7 456.3 %reduce-scatter.14.cloned.1.call-start = ((), (), s32[]{:S(2)}) async-start(), calls=%async_computation.19 | async-start | bytes 6291456 | tf_op jit(solution)/shard_map/reduce_scatter | solution.py:62
  641.5 388.8 %copy-start.49 = (f32[1024]{0:T(1024)S(1)}, f32[1024]{0:T(1024)}, u32[]{:S(2)}) copy-start(f32[1024]{0:T(1024)} %param.27) | copy-start | bytes 12292
  641.5 388.8 %copy-start.53 = (f32[512]{0:T(512)S(1)}, f32[512]{0:T(512)}, u32[]{:S(2)}) copy-start(f32[512]{0:T(512)} %copy-done.52) | copy-start | bytes 6148
  641.5 391.2 %copy-start.58 = (f32[1024]{0:T(1024)S(1)}, f32[1024]{0:T(1024)}, u32[]{:S(2)}) copy-start(f32[1024]{0:T(1024)} %get-tuple-element.77) | copy-start | bytes 12292
  641.5 431.3 %copy-start.55 = (f32[512]{0:T(512)S(1)}, f32[512]{0:T(512)}, u32[]{:S(2)}) copy-start(f32[512]{0:T(512)} %copy-done.54) | copy-start | bytes 6148
  641.5 446.5 %copy-start.57 = (f32[512]{0:T(512)S(1)}, f32[512]{0:T(512)}, u32[]{:S(2)}) copy-start(f32[512]{0:T(512)} %copy-done.56) | copy-start | bytes 6148
  (46 other events, 150.6 us)
Sparse Core Ops, SparseCore 0:
  11.4 35.8 all-gather.9
  49.4 37.9 all-gather.11
  89.6 36.8 all-gather.13
  131.1 53.1 reduce-scatter.11
  186.8 53.4 all-gather.19
  242.3 31.6 all-gather.15
  276.5 53.3 all-gather.17
  331.5 31.6 all-gather.23
  365.8 53.3 all-gather.21
  453.1 30.3 reduce-scatter.15
  489.4 33.0 all-gather.25
  526.2 75.6 reduce-scatter.29
  606.2 74.5 reduce-scatter.27
  684.3 54.8 reduce-scatter.23
  743.3 74.5 reduce-scatter.31
  821.4 54.8 reduce-scatter.21
  880.1 56.3 reduce-scatter.25
  940.0 56.3 reduce-scatter.19
  999.4 30.8 reduce-scatter.17
  1032.4 55.5 reduce-scatter.13
where the time goes:
time: 1110 us; the launch traced here: 1100 us
  waiting for transfers between devices  729 us (66%)
  matrix products  187 us (17%)
  blocking collectives  83.6 us (8%)
  other arithmetic  69.4 us (6%)
  between operations  15.5 us (1%)
  local copies, waits for them, and re-layouts  13.2 us (1%)
    reduce_scatter x1, waiting for transfers between devices, on_device(): lax.psum_scatter(down_grad.astype(jnp.bfloat16), 'fsdp', scatter_dimensio...  77.4 us
    reduce_scatter x2, waiting for transfers between devices, narrow(): return lax.psum_scatter(terms, 'tp', scatter_dimension=0, tiled=True)  67.9 us
    reduce_scatter x2, waiting for transfers between devices, narrow_grad(): lax.psum_scatter(terms.astype(jnp.bfloat16), 'tp', scatter_dimension=0, t...  62.6 us
    reduce_scatter x1, waiting for transfers between devices, on_device(): lax.psum_scatter(out_weight_grad.astype(jnp.bfloat16), 'fsdp', scatter_di...  58.9 us
    reduce_scatter x1, waiting for transfers between devices, on_device(): lax.psum_scatter(query_weight_grad.astype(jnp.bfloat16), 'fsdp', scatter_...  58.4 us
    reduce_scatter x1, waiting for transfers between devices, on_device(): lax.psum_scatter(value_weight_grad.astype(jnp.bfloat16), 'fsdp', scatter_...  56.5 us
    reduce_scatter x1, waiting for transfers between devices, on_device(): lax.psum_scatter(key_weight_grad.astype(jnp.bfloat16), 'fsdp', scatter_di...  56.5 us
    all_gather x1, waiting for transfers between devices, on_device(): lax.all_gather(down_weight, 'fsdp', axis=1, tiled=True)  56 us
  transfers between devices with their start and end apart: 20, of which 18 were waited for; matrix products, arithmetic and copies ran while one was open for 19% of the time, Pallas kernels for 0%

commit v1 on v0

v1 whole, which is shorter than its diff:
```python
from functools import partial

import jax
import jax.numpy as jnp
from jax import lax
from jax.experimental import pallas as pl
from jax.experimental.pallas import tpu as pltpu
from jax.sharding import PartitionSpec as P

HD = 64

eps = 1e-05
theta_base = 1000000.0
f32 = jnp.float32
bf16 = jnp.bfloat16


def rms_norm(values, gain):
    return values * lax.rsqrt(jnp.mean(values * values, axis=-1, keepdims=True) + eps) * gain


def rotary_tables(length):
    half_size = HD // 2
    frequency = theta_base ** (-jnp.arange(half_size, dtype=f32) * 2.0 / HD)
    angles = jnp.arange(length, dtype=f32)[:, None] * frequency[None, :]
    cosine = jnp.concatenate([jnp.cos(angles), jnp.cos(angles)], axis=-1)
    sine_table = jnp.concatenate([jnp.sin(angles), jnp.sin(angles)], axis=-1)
    return (cosine, sine_table)


def rotate(values, cosine, sine_table):
    half_size = values.shape[-1] // 2
    turned = jnp.concatenate([-values[..., half_size:], values[..., :half_size]], axis=-1)
    return values * cosine[:, None, :] + turned * sine_table[:, None, :]


def prepare(cosine, sine_table, query_raw, key_raw, query_gain, key_gain):
    length = query_raw.shape[0]
    query_rows = rotate(rms_norm(query_raw.reshape(length, -1, HD), query_gain), cosine, sine_table)
    key_rows = rotate(rms_norm(key_raw.reshape(length, -1, HD), key_gain), cosine, sine_table)
    return (query_rows, key_rows)


def dot(former, latter):
    return jnp.dot(former, latter, preferred_element_type=f32)


def dot_transposed(former, latter):
    return lax.dot_general(former, latter, (((1,), (1,)), ((), ())), preferred_element_type=f32)


def dot_leading(former, latter):
    return lax.dot_general(former, latter, (((0,), (0,)), ((), ())), preferred_element_type=f32)


def swap(values, axis_name, bit=1):
    count = lax.axis_size(axis_name)
    return lax.ppermute(values, axis_name, [(i, i ^ bit) for i in range(count)])


def widen(rows):
    if lax.axis_size("tp") == 2:
        return (rows, swap(rows, "tp"))
    return (lax.all_gather(rows, "tp", axis=0, tiled=True),)


def narrow(parts):
    if len(parts) == 2:
        return parts[0].astype(f32) + swap(parts[1].astype(bf16), "tp").astype(f32)
    return lax.psum_scatter(
        parts[0].astype(bf16), "tp", scatter_dimension=0, tiled=True
    ).astype(f32)


def in_order(parts):
    if len(parts) == 1:
        return parts[0]
    first = lax.axis_index("tp") == 0
    return jnp.concatenate(
        [jnp.where(first, parts[0], parts[1]), jnp.where(first, parts[1], parts[0])], axis=0
    )


def in_parts(rows):
    if lax.axis_size("tp") != 2:
        return (rows,)
    half = rows.shape[0] // 2
    index = lax.axis_index("tp")
    return (
        lax.dynamic_slice_in_dim(rows, index * half, half, 0),
        lax.dynamic_slice_in_dim(rows, (1 - index) * half, half, 0),
    )


def sum_everywhere(values):
    for axis_name in ("tp", "fsdp"):
        bit = 1
        while bit < lax.axis_size(axis_name):
            values = values + swap(values, axis_name, bit)
            bit *= 2
    return values


def ffn_body(count, width, *refs):
    rows_in = refs[:count]
    cotangent_in = refs[count : 2 * count]
    weights = refs[2 * count]
    outs = refs[2 * count + 1 : 3 * count + 1]
    grads = refs[3 * count + 1 : 4 * count + 1]
    weight_grads = refs[4 * count + 1]
    rows_turned, cotangent_turned, out_sum, grad_sum, hidden_all, pair_all = refs[4 * count + 2 :]
    step = pl.program_id(0)
    part_rows = rows_in[0].shape[0]

    @pl.when(step == 0)
    def _():
        for part in range(count):
            span = pl.ds(part * part_rows, part_rows)
            rows_turned[:, span] = rows_in[part][...].T
            cotangent_turned[:, span] = cotangent_in[part][...].T
        out_sum[...] = jnp.zeros_like(out_sum)
        grad_sum[...] = jnp.zeros_like(grad_sum)

    pair_weights = weights[:, : 2 * width]
    down = weights[:, 2 * width :]
    chunk = min(256, part_rows)
    for part in range(count):
        for start in range(0, part_rows, chunk):
            here = pl.ds(start, chunk)
            span = pl.ds(part * part_rows + start, chunk)
            both = dot(rows_in[part][here, :], pair_weights)
            gate = both[:, :width]
            up = both[:, width:]
            hidden_grad = dot(cotangent_in[part][here, :], down)
            sigmoid = 1.0 / (1.0 + jnp.exp(-gate))
            silu = gate * sigmoid
            hidden = (silu * up).astype(bf16)
            gate_grad = hidden_grad * up * sigmoid * (1.0 + gate * (1.0 - sigmoid))
            up_grad = hidden_grad * silu
            pair = jnp.concatenate([gate_grad.astype(bf16), up_grad.astype(bf16)], axis=1)
            hidden_all[span, :] = hidden
            pair_all[span, :] = pair
            out_sum[span, :] += dot_transposed(hidden, down)
            grad_sum[span, :] += dot_transposed(pair, pair_weights)
    weight_grads[:, : 2 * width] = dot(rows_turned[...], pair_all[...]).astype(bf16)
    weight_grads[:, 2 * width :] = dot(cotangent_turned[...], hidden_all[...]).astype(bf16)

    @pl.when(step == pl.num_programs(0) - 1)
    def _():
        for part in range(count):
            span = pl.ds(part * part_rows, part_rows)
            outs[part][...] = out_sum[span, :].astype(outs[part].dtype)
            grads[part][...] = grad_sum[span, :].astype(grads[part].dtype)


def hidden_width(units):
    for width in (256, 384, 128):
        if units % width == 0:
            return width
    return units


def feed_forward(rows_parts, cotangent_parts, weights, width):
    count = len(rows_parts)
    part_rows, model = rows_parts[0].shape
    length = count * part_rows
    steps = weights.shape[1] // (3 * width)
    whole = pl.BlockSpec((part_rows, model), lambda i: (0, 0))
    block = pl.BlockSpec((model, 3 * width), lambda i: (0, i))
    kinds = [f32] + [bf16] * (count - 1)
    shapes = [jax.ShapeDtypeStruct((part_rows, model), kind) for kind in kinds]
    results = pl.pallas_call(
        partial(ffn_body, count, width),
        grid=(steps,),
        in_specs=[whole] * (2 * count) + [block],
        out_specs=[whole] * (2 * count) + [block],
        out_shape=shapes + shapes + [jax.ShapeDtypeStruct(weights.shape, bf16)],
        scratch_shapes=[
            pltpu.VMEM((model, length), bf16),
            pltpu.VMEM((model, length), bf16),
            pltpu.VMEM((length, model), f32),
            pltpu.VMEM((length, model), f32),
            pltpu.VMEM((length, width), bf16),
            pltpu.VMEM((length, 2 * width), bf16),
        ],
        compiler_params=pltpu.CompilerParams(vmem_limit_bytes=56 * 1024 * 1024),
        name="feed_forward",
    )(*rows_parts, *cotangent_parts, weights)
    return results[:count], results[count : 2 * count], results[2 * count]


def block_scores(query_block, key_rows, row_start, finish):
    block_rows = query_block.shape[0]
    scores = jnp.einsum(
        "qkgd,skd->kgqs", query_block, key_rows[:finish], preferred_element_type=f32
    ) * HD ** (-0.5)
    causal = (row_start + jnp.arange(block_rows))[:, None] >= jnp.arange(finish)[None, :]
    return jnp.where(causal, scores, -1e30)


def attend(query_rows, key_rows, value_rows):
    length = query_rows.shape[0]
    heads_local = query_rows.shape[1]
    kv_local = key_rows.shape[1]
    grouped = query_rows.reshape(length, kv_local, heads_local // kv_local, HD)
    block_rows = min(512, length)
    outputs = []
    log_totals = []
    for block_index in range(length // block_rows):
        row_start = block_index * block_rows
        finish = row_start + block_rows
        scores = block_scores(grouped[row_start:finish], key_rows, row_start, finish)
        largest = jnp.max(scores, axis=-1, keepdims=True)
        exponent = jnp.exp(scores - largest)
        row_total = jnp.sum(exponent, axis=-1, keepdims=True)
        probability = (exponent / row_total).astype(bf16)
        attended = jnp.einsum(
            "kgqs,skd->qkgd", probability, value_rows[:finish], preferred_element_type=f32
        )
        outputs.append(attended.astype(bf16).reshape(block_rows, heads_local * HD))
        log_totals.append(largest + jnp.log(row_total))
    return (jnp.concatenate(outputs, axis=0), log_totals)


def attend_back(query_rows, key_rows, value_rows, log_totals, attended_grad):
    length = query_rows.shape[0]
    heads_local = query_rows.shape[1]
    kv_local = key_rows.shape[1]
    group_size = heads_local // kv_local
    grouped = query_rows.reshape(length, kv_local, group_size, HD)
    grad_grouped = attended_grad.reshape(length, kv_local, group_size, HD)
    block_rows = min(512, length)
    key_grad = jnp.zeros(key_rows.shape, f32)
    value_grad = jnp.zeros(value_rows.shape, f32)
    query_parts = []
    for block_index in range(length // block_rows):
        row_start = block_index * block_rows
        finish = row_start + block_rows
        query_block = grouped[row_start:finish]
        grad_block = grad_grouped[row_start:finish]
        scores = block_scores(query_block, key_rows, row_start, finish)
        probability = jnp.exp(scores - log_totals[block_index])
        prob_grad = jnp.einsum(
            "qkgd,skd->kgqs", grad_block, value_rows[:finish], preferred_element_type=f32
        )
        inner_sum = jnp.sum(probability * prob_grad, axis=-1, keepdims=True)
        score_grad = (probability * (prob_grad - inner_sum)).astype(bf16)
        query_parts.append(
            jnp.einsum("kgqs,skd->qkgd", score_grad, key_rows[:finish], preferred_element_type=f32)
            * HD ** (-0.5)
        )
        key_grad = key_grad.at[:finish].add(
            jnp.einsum("kgqs,qkgd->skd", score_grad, query_block, preferred_element_type=f32)
            * HD ** (-0.5)
        )
        value_grad = value_grad.at[:finish].add(
            jnp.einsum(
                "kgqs,qkgd->skd", probability.astype(bf16), grad_block, preferred_element_type=f32
            )
        )
    query_grad = jnp.concatenate(query_parts, axis=0).reshape(length, heads_local, HD)
    return (query_grad, key_grad, value_grad)


def on_device(
    tokens,
    out_cotangent,
    attn_gain,
    query_weight,
    key_weight,
    value_weight,
    query_gain,
    key_gain,
    out_weight,
    ffn_gain,
    gate_weight,
    up_weight,
    down_weight,
):
    shard, query_columns = query_weight.shape
    key_columns = key_weight.shape[1]
    qkv_columns = query_columns + 2 * key_columns
    units = gate_weight.shape[1]
    width = hidden_width(units)
    steps = units // width
    attn_shard = jnp.concatenate([query_weight, key_weight, value_weight, out_weight.T], axis=1)
    ffn_shard = jnp.stack(
        [
            gate_weight.reshape(shard, steps, width),
            up_weight.reshape(shard, steps, width),
            down_weight.T.reshape(shard, steps, width),
        ],
        axis=2,
    ).reshape(shard, 3 * units)
    attn_full = lax.all_gather(attn_shard, "fsdp", axis=0, tiled=True)
    qkv_full = attn_full[:, :qkv_columns]
    out_full = attn_full[:, qkv_columns:]
    ffn_full = lax.all_gather(ffn_shard, "fsdp", axis=0, tiled=True)

    residual = tokens.astype(f32)
    normed, attn_norm_pull = jax.vjp(rms_norm, residual, attn_gain)
    normed_rows = in_order(widen(normed.astype(bf16)))
    cotangent_parts = widen(out_cotangent)
    length = normed_rows.shape[0]
    cosine, sine_table = rotary_tables(length)
    qkv_raw = dot(normed_rows, qkv_full)
    query_raw = qkv_raw[:, :query_columns]
    key_raw = qkv_raw[:, query_columns : query_columns + key_columns]
    value_raw = qkv_raw[:, query_columns + key_columns :]
    (query_rows, key_rows), prepare_pull = jax.vjp(
        partial(prepare, cosine, sine_table), query_raw, key_raw, query_gain, key_gain
    )
    query_rows = query_rows.astype(bf16)
    key_rows = key_rows.astype(bf16)
    value_rows = value_raw.astype(bf16).reshape(length, -1, HD)
    attended, log_totals = attend(query_rows, key_rows, value_rows)
    branch = tuple(dot_transposed(part, out_full) for part in in_parts(attended))
    middle = residual + narrow(branch)
    normed_ffn, ffn_norm_pull = jax.vjp(rms_norm, middle, ffn_gain)
    ffn_parts = widen(normed_ffn.astype(bf16))
    out_parts, grad_parts, ffn_grads = feed_forward(ffn_parts, cotangent_parts, ffn_full, width)
    ffn_grads = lax.psum_scatter(ffn_grads, "fsdp", scatter_dimension=0, tiled=True)

    ffn_normed_grad = narrow(grad_parts)
    middle_piece, ffn_gain_local = ffn_norm_pull(ffn_normed_grad)
    middle_grad = out_cotangent.astype(f32) + middle_piece
    branch_rows = in_order(widen(middle_grad.astype(bf16)))
    output = (middle + narrow(out_parts)).astype(bf16)

    out_grad = dot_leading(branch_rows, attended)
    attended_grad = dot(branch_rows, out_full).astype(bf16)
    query_grad, key_grad, value_grad = attend_back(
        query_rows, key_rows, value_rows, log_totals, attended_grad
    )
    query_raw_grad, key_raw_grad, query_gain_local, key_gain_local = prepare_pull(
        (query_grad, key_grad)
    )
    qkv_grad = jnp.concatenate(
        [
            query_raw_grad.astype(bf16),
            key_raw_grad.astype(bf16),
            value_grad.reshape(length, -1).astype(bf16),
        ],
        axis=1,
    )
    normed_grad = narrow(tuple(dot_transposed(part, qkv_full) for part in in_parts(qkv_grad)))
    qkv_weight_grad = dot_leading(normed_rows, qkv_grad)
    attn_grads = jnp.concatenate([qkv_weight_grad.astype(bf16), out_grad.astype(bf16)], axis=1)
    attn_grads = lax.psum_scatter(attn_grads, "fsdp", scatter_dimension=0, tiled=True)
    tokens_piece, attn_gain_local = attn_norm_pull(normed_grad)
    tokens_grad = middle_grad + tokens_piece
    model = attn_gain.shape[0]
    gain_totals = sum_everywhere(
        jnp.concatenate([attn_gain_local, ffn_gain_local, query_gain_local, key_gain_local])
    )
    attn_grads = attn_grads.astype(f32)
    ffn_grads = ffn_grads.reshape(shard, steps, 3, width)
    gate_grad, up_grad, down_grad = (
        ffn_grads[:, :, at].reshape(shard, units).astype(f32) for at in range(3)
    )
    return (
        output,
        tokens_grad,
        gain_totals[:model],
        attn_grads[:, :query_columns],
        attn_grads[:, query_columns : query_columns + key_columns],
        attn_grads[:, query_columns + key_columns : qkv_columns],
        gain_totals[2 * model : 2 * model + HD],
        gain_totals[2 * model + HD :],
        attn_grads[:, qkv_columns:].T,
        gain_totals[model : 2 * model],
        gate_grad,
        up_grad,
        down_grad.T,
    )


def solution(mesh):
    placed = (
        P(("fsdp", "tp"), None),
        P(("fsdp", "tp"), None),
        P(),
        P("fsdp", "tp"),
        P("fsdp", "tp"),
        P("fsdp", "tp"),
        P(),
        P(),
        P("tp", "fsdp"),
        P(),
        P("fsdp", "tp"),
        P("fsdp", "tp"),
        P("tp", "fsdp"),
    )
    return jax.shard_map(
        on_device,
        mesh=mesh,
        in_specs=placed,
        out_specs=(
            P(("fsdp", "tp"), None),
            P(("fsdp", "tp"), None),
            P(),
            P("fsdp", "tp"),
            P("fsdp", "tp"),
            P("fsdp", "tp"),
            P(),
            P(),
            P("tp", "fsdp"),
            P(),
            P("fsdp", "tp"),
            P("fsdp", "tp"),
            P("tp", "fsdp"),
        ),
        check_vma=False,
    )
```

time: 1110 us -> 610 us (0.55)
  waiting for transfers between devices: 729 us -> 356 us
  matrix products: 187 us -> 69.5 us
  blocking collectives: 83.6 us -> 0 us
  Pallas kernels: 0 us -> 57.7 us
  local copies, waits for them, and re-layouts: 13.2 us -> 41.1 us
  other arithmetic: 69.4 us -> 53.7 us
  starting transfers between devices: 1.74 us -> 13.8 us
    reduce_scatter x11 -> x1, waiting for transfers between devices: 476 us -> 144 us  [on_device(): lax.psum_scatter(ffn_grads, 'fsdp', scatter_dimension=0, tiled=True)]
    all_gather x9 -> x2, waiting for transfers between devices: 249 us -> 14.7 us  [the longest x1 14.7 us: on_device(): attn_full = lax.all_gather(attn_shard, 'fsdp', axis=0, tiled=True)]
    ppermute x0 -> x13, waiting for transfers between devices: none -> 181 us  [swap(): return lax.ppermute(values, axis_name, [(i, i ^ bit) for i in range(count)])]
    pallas_call x0 -> x1, Pallas kernels: none -> 57.7 us  [feed_forward(): pl.pallas_call(partial(ffn_body, count, width), grid=(steps,), in_specs=[...]
    all_gather x2 -> x0, blocking collectives: 43.6 us -> none  [the longest x1 24.6 us: on_device(): lax.all_gather(key_weight, 'fsdp', axis=0, tiled=True)]
    dot_general x9 -> x4, matrix products: 55.5 us -> 14 us  [the longest x2 7.1 us: dot(): return jnp.dot(former, latter, preferred_element_type=f32)]
    psum x1 -> x0, blocking collectives: 40 us -> none  [on_device(): lax.psum((attn_gain_local, query_gain_local, key_gain_local, ffn_gain_loc...]
    dot_general x7 -> x4, matrix products: 42.2 us -> 9.19 us  [dot_transposed(): lax.dot_general(former, latter, (((1,), (1,)), ((), ())), preferred_eleme...]
  transfers between devices with their start and end apart: 20 -> 17, of which waited for: 18 -> 16; matrix products, arithmetic and copies ran while one was open for 19% -> 11% of each run, Pallas kernels for 0% -> 0%
where the time goes in v1:
time: 610 us; the launch traced here: 607 us
  waiting for transfers between devices  356 us (58%)
  matrix products  69.5 us (11%)
  Pallas kernels  57.7 us (9%)
  other arithmetic  53.7 us (9%)
  local copies, waits for them, and re-layouts  41.1 us (7%)
  between operations  15.2 us (2%)
  starting transfers between devices  13.8 us (2%)
    ppermute x13, waiting for transfers between devices, swap(): return lax.ppermute(values, axis_name, [(i, i ^ bit) for i in range(count)])  181 us
    reduce_scatter x1, waiting for transfers between devices, on_device(): lax.psum_scatter(ffn_grads, 'fsdp', scatter_dimension=0, tiled=True)  144 us
    pallas_call x1, Pallas kernels, feed_forward(): pl.pallas_call(partial(ffn_body, count, width), grid=(steps,), in_specs=[...  57.7 us
    unnamed x139, local copies, waits for them, and re-layouts  29.4 us
    unnamed x5, waiting for transfers between devices  16.1 us
    all_gather x1, waiting for transfers between devices, on_device(): attn_full = lax.all_gather(attn_shard, 'fsdp', axis=0, tiled=True)  14.7 us
    ppermute x13, starting transfers between devices, swap(): return lax.ppermute(values, axis_name, [(i, i ^ bit) for i in range(count)])  13.2 us
    convert_element_type x2, other arithmetic, attend_back(): score_grad = (probability * (prob_grad - inner_sum)).astype(bf16)  13.1 us
  transfers between devices with their start and end apart: 17, of which 16 were waited for; matrix products, arithmetic and copies ran while one was open for 11% of the time, Pallas kernels for 0%

profile of v1, /device:TPU:0, one launch (start us, length us, event | category | flops | bytes accessed | tf_op | source)
XLA Modules:
  0.0 606.9 jit_solution(4606648621395567065)
XLA Ops:
  12.5 1.8 reshape.313
  15.2 3.0 collective-permute-start
  20.1 21.4 %collective-permute-done = bf16[512,1024]{1,0:T(8,128)(2,1)} collective-permute-done((bf16[512,1024]{1,0:T(8,128)(2,1)S(1)}, bf16[512,1024]{1,0:T(8,128)(2,1)}, u32[]{:S(2)}, u32[]{:S(2)}) %collective-permute-start) | collective-permute-done | bytes 1048608 | tf_op jit(solution)/shard_map/ppermute | solution.py:58
  41.5 2.8 broadcast_select_fusion.3
  44.3 14.7 %all-gather.3.cloned.1.call-done = bf16[1024,1536]{1,0:T(8,128)(2,1)} async-done(((bf16[64,1536]{1,0:T(8,128)(2,1)}), bf16[1024,1536]{1,0:T(8,128)(2,1)}) %all-gather.3.cloned.1.call-update) | async-done | bytes 3145744 | tf_op jit(solution)/shard_map/all_gather | solution.py:295
  59.0 4.4 fusion.109
  69.7 2.1 copy-done.1
  71.8 7.6 %fusion.111 = (f32[4,2,512]{2,1,0:T(2,128)S(1)}, f32[4,2,512,1024]{2,3,1,0:T(8,128)}) fusion(bf16[512,4,2,64]{0,3,2,1:T(8,128)(2,1)S(1)} %bitcast.180, bf16[1024,4,64]{0,2,1:T(8,128)(2,1)S(1)} %fusion.65, pred[512,1024]{0,1:T(8,128)(4,1)S(1)} %copy-done.33), kind=kOutput, calls=%fused_computation.183 | convolution fusion | flops 549449728 | bytes 18366464 | tf_op jit(solution)/shard_map/qkgd,skd->kgqs/dot_general | solution.py:194
  79.4 8.1 %fusion.3 = f32[4,2,512]{2,1,0:T(2,128)S(1)} fusion(f32[4,2,512,1024]{2,3,1,0:T(8,128)} %get-tuple-element.171, f32[4,2,512]{2,1,0:T(2,128)S(1)} %get-tuple-element.170), kind=kLoop, calls=%fused_computation.9 | loop fusion | flops 8384512 | bytes 16809984 | tf_op jit(solution)/shard_map/reduce_sum | solution.py:215
  87.5 5.1 fusion.56
  92.6 3.3 copy-done
  95.9 3.1 fusion.57
  99.0 2.2 convolution_convert_fusion.3
  103.3 24.1 %collective-permute-done.1 = bf16[512,1024]{1,0:T(8,128)(2,1)} collective-permute-done((bf16[512,1024]{1,0:T(8,128)(2,1)S(1)}, bf16[512,1024]{1,0:T(8,128)(2,1)}, u32[]{:S(2)}, u32[]{:S(2)}) %collective-permute-start.1) | collective-permute-done | bytes 1048608 | tf_op jit(solution)/shard_map/ppermute | solution.py:58
  127.4 2.7 multiply_reduce_fusion.4
  133.5 16.4 %collective-permute-done.3.refs_3_ = bf16[512,1024]{1,0:T(8,128)(2,1)} collective-permute-done((bf16[512,1024]{1,0:T(8,128)(2,1)}, bf16[512,1024]{1,0:T(8,128)(2,1)}, u32[]{:S(2)}, u32[]{:S(2)}) %collective-permute-start.3) | collective-permute-done | bytes 1048608 | tf_op jit(solution)/shard_map/ppermute | solution.py:58
  149.8 21.8 %collective-permute-done.2.refs_1_ = bf16[512,1024]{1,0:T(8,128)(2,1)} collective-permute-done((bf16[512,1024]{1,0:T(8,128)(2,1)S(1)}, bf16[512,1024]{1,0:T(8,128)(2,1)}, u32[]{:S(2)}, u32[]{:S(2)}) %collective-permute-start.2) | collective-permute-done | bytes 1048608 | tf_op jit(solution)/shard_map/ppermute | solution.py:58
  171.7 57.7 %feed_forward.1 = (f32[512,1024]{1,0:T(8,128)}, bf16[512,1024]{1,0:T(8,128)(2,1)}, f32[512,1024]{1,0:T(8,128)}, bf16[512,1024]{1,0:T(8,128)(2,1)}, bf16[1024,6912]{1,0:T(8,128)(2,1)}) custom-call(bf16[512,1024]{1,0:T(8,128)(2,1)} %copy-done.17, bf16[512,1024]{1,0:T(8,128)(2,1)} %collective-permute-done.2.refs_1_, bf16[512,1024]{1,0:T(8,128)(2,1)} %refs_2_.1, ...), custom_call_target="tpu_custom_call" | custom-call | tf_op jit(solution)/shard_map/feed_forward/pallas_call | solution.py:172
  231.4 24.2 %collective-permute-done.5 = bf16[512,1024]{1,0:T(8,128)(2,1)S(1)} collective-permute-done((bf16[512,1024]{1,0:T(8,128)(2,1)}, bf16[512,1024]{1,0:T(8,128)(2,1)S(1)}, u32[]{:S(2)}, u32[]{:S(2)}) %collective-permute-start.5) | collective-permute-done | bytes 1048608 | tf_op jit(solution)/shard_map/ppermute | solution.py:58
  255.7 3.1 multiply_reduce_fusion.1
  258.8 18.4 %collective-permute-done.4 = bf16[512,1024]{1,0:T(8,128)(2,1)S(1)} collective-permute-done((bf16[512,1024]{1,0:T(8,128)(2,1)}, bf16[512,1024]{1,0:T(8,128)(2,1)S(1)}, u32[]{:S(2)}, u32[]{:S(2)}) %collective-permute-start.4) | collective-permute-done | bytes 1048608 | tf_op jit(solution)/shard_map/ppermute | solution.py:58
  277.1 4.0 fusion.100
  285.2 20.1 %collective-permute-done.6 = bf16[512,1024]{1,0:T(8,128)(2,1)S(1)} collective-permute-done((bf16[512,1024]{1,0:T(8,128)(2,1)S(1)}, bf16[512,1024]{1,0:T(8,128)(2,1)S(1)}, u32[]{:S(2)}, u32[]{:S(2)}) %collective-permute-start.6) | collective-permute-done | bytes 1048608 | tf_op jit(solution)/shard_map/ppermute | solution.py:58
  305.5 2.3 convolution_convert_fusion.1
  307.8 2.7 convolution_convert_fusion.2
  310.6 2.2 fusion.58
  312.8 5.1 fusion.7
  317.9 4.8 fusion.9
  322.8 2.2 fusion.62
  325.0 1.8 fusion.49
  327.0 7.5 %fusion = (f32[4,2,512]{2,1,0:T(2,128)S(1)}, f32[4,1024,512,2]{2,1,3,0:T(8,128)}) fusion(f32[4,2,512,1024]{2,3,1,0:T(8,128)S(1)} %bitcast.160, f32[4,2,512]{2,1,0:T(2,128)S(1)} %bitcast.189, bf16[1024,4,64,1]{0,2,3,1:T(8,128)(2,1)S(1)} %bitcast.179, bf16[512,4,2,64]{0,3,2,1:T(8,128)(2,1)S(1)} %bitcast.166), kind=kOutput, calls=%fused_computation.2 | convolution fusion | flops 549449728 | bytes 34635776 | tf_op jit(solution)/shard_map/qkgd,skd->kgqs/dot_general | solution.py:243
  334.5 4.7 fusion.53
  339.2 8.3 %fusion.2 = bf16[4,2,512,1024]{2,3,1,0:T(8,128)(2,1)S(1)} fusion(f32[4,1024,512,2]{2,1,3,0:T(8,128)} %get-tuple-element.175, f32[4,2,512,1024]{2,3,1,0:T(8,128)S(1)} %bitcast.160, f32[4,2,512]{2,1,0:T(2,128)S(1)} %get-tuple-element.174, f32[4,2,512]{2,1,0:T(2,128)S(1)} %bitcast.191), kind=kLoop, calls=%fused_computation.4 | loop fusion | flops 16777216 | bytes 41975808 | tf_op jit(solution)/shard_map/convert_element_type | solution.py:247
  347.6 3.3 copy-done.5
  352.4 6.2 %broadcast_multiply_fusion = (f32[1024,4,64]{0,2,1:T(8,128)S(1)}, f32[1024,4,64]{0,2,1:T(8,128)S(1)}) fusion(f32[1024,64]{0,1:T(8,128)S(1)} %get-tuple-element.182, bf16[512,4,2,64]{0,3,2,1:T(8,128)(2,1)S(1)} %bitcast.181, bf16[4,2,512,1024]{2,3,1,0:T(8,128)(2,1)} %copy-done.5, f32[512,4,64]{0,2,1:T(8,128)S(1)} %copy-done.21), kind=kOutput, calls=%fused_computation.138 | convolution fusion | flops 537657344 | bytes 11796480 | tf_op jit(solution)/shard_map/kgqs,qkgd->skd/dot_general | solution.py:253
  366.5 2.3 convolution_convert_fusion
  368.9 2.0 pad_maximum_fusion
  370.8 4.6 copy.83
  380.8 21.8 %collective-permute-done.7 = bf16[512,1024]{1,0:T(8,128)(2,1)S(1)} collective-permute-done((bf16[512,1024]{1,0:T(8,128)(2,1)S(1)}, bf16[512,1024]{1,0:T(8,128)(2,1)S(1)}, u32[]{:S(2)}, u32[]{:S(2)}) %collective-permute-start.7) | collective-permute-done | bytes 1048608 | tf_op jit(solution)/shard_map/ppermute | solution.py:58
  402.7 3.0 fusion.21
  407.1 2.3 collective-permute-done.8
  410.7 3.7 collective-permute-done.10
  414.5 4.4 collective-permute-done.11
  418.8 3.5 fusion.24
  424.6 15.8 %reduce-scatter.7.cloned.1.call-done = bf16[64,1536]{1,0:T(8,128)(2,1)} async-done(((bf16[1024,1536]{1,0:T(8,128)(2,1)}), bf16[64,1536]{1,0:T(8,128)(2,1)}) %reduce-scatter.7.cloned.1.call-update) | async-done | bytes 196624
  444.6 144.3 %reduce-scatter.5.cloned.1.call-done = bf16[64,6912]{1,0:T(8,128)(2,1)} async-done(((bf16[1024,6912]{1,0:T(8,128)(2,1)}), bf16[64,6912]{1,0:T(8,128)(2,1)}) %reduce-scatter.5.cloned.1.call-update) | async-done | bytes 884752 | tf_op jit(solution)/shard_map/reduce_scatter | solution.py:322
  588.9 2.6 reshape.315
  591.5 4.9 fusion.74
  (225 shorter events, 53.5 us)
Async XLA Ops:
  7.2 51.8 %all-gather.3.cloned.1.call-start = ((), (), s32[]{:S(2)}) async-start(), calls=%async_computation.2 | async-start | bytes 3342336 | tf_op jit(solution)/shard_map/all_gather | solution.py:295
  8.9 162.8 %all-gather.5.cloned.1.call-start = ((), (), s32[]{:S(2)}) async-start(), calls=%async_computation.3 | async-start | bytes 15040512 | tf_op jit(solution)/shard_map/all_gather | solution.py:298
  14.3 426.1 %reduce-scatter.7.cloned.1.call-start = ((), (), s32[]{:S(2)}) async-start(), calls=%async_computation.5 | async-start | bytes 3342336
  14.9 29.4 %copy-start.45 = (f32[512]{0:T(512)}, f32[512]{0:T(512)S(1)}, u32[]{:S(2)}) copy-start(f32[512]{0:T(512)S(1)} %fusion.25) | copy-start | bytes 6148
  14.9 29.4 %copy-start.41 = (f32[512]{0:T(512)}, f32[512]{0:T(512)S(1)}, u32[]{:S(2)}) copy-start(f32[512]{0:T(512)S(1)} %fusion.87) | copy-start | bytes 6148
  15.2 26.3 %collective-permute-start = (bf16[512,1024]{1,0:T(8,128)(2,1)S(1)}, bf16[512,1024]{1,0:T(8,128)(2,1)}, u32[]{:S(2)}, u32[]{:S(2)}) collective-permute-start(bf16[512,1024]{1,0:T(8,128)(2,1)S(1)} %fusion.20), channel_id=1, source_target_pairs={{0,1},{1,0},{2,3},{3,2},{4,5},{5,4},{6,7},{7,6},{8,9},{9,8},{10,11... | collective-permute-start | bytes 3145736 | tf_op jit(solution)/shard_map/ppermute | solution.py:58
  18.9 47.5 %copy-start.12 = (f32[1024,64]{0,1:T(8,128)}, f32[1024,64]{0,1:T(8,128)S(1)}, u32[]{:S(2)}) copy-start(f32[1024,64]{0,1:T(8,128)S(1)} %get-tuple-element.181) | copy-start | bytes 786436
  44.3 19.1 %copy-start.29 = (bf16[512,1024]{1,0:T(8,128)(2,1)}, bf16[512,1024]{1,0:T(8,128)(2,1)S(1)}, u32[]{:S(2)}) copy-start(bf16[512,1024]{1,0:T(8,128)(2,1)S(1)} %get-tuple-element.148) | copy-start | bytes 3145732
  63.5 24.0 %copy-start.27 = (bf16[512,256]{0,1:T(8,128)(2,1)}, bf16[512,256]{0,1:T(8,128)(2,1)S(1)}, u32[]{:S(2)}) copy-start(bf16[512,256]{0,1:T(8,128)(2,1)S(1)} %slice.212) | copy-start | bytes 786436
  63.6 29.1 %copy-start.22 = (bf16[1024,256]{0,1:T(8,128)(2,1)}, bf16[1024,256]{0,1:T(8,128)(2,1)S(1)}, u32[]{:S(2)}) copy-start(bf16[1024,256]{0,1:T(8,128)(2,1)S(1)} %slice.221) | copy-start | bytes 1572868
  66.5 5.3 copy-start.24
  66.9 4.9 copy-start.14
  87.4 5.2 copy-start.35
  87.5 8.4 %copy-start = (f32[4,2,512,1024]{2,3,1,0:T(8,128)S(1)}, f32[4,2,512,1024]{2,3,1,0:T(8,128)}, u32[]{:S(2)}) copy-start(f32[4,2,512,1024]{2,3,1,0:T(8,128)} %get-tuple-element.171) | copy-start | bytes 50331652
  92.6 6.4 %copy-start.55 = (bf16[4,64,2,512]{3,1,2,0:T(8,128)(2,1)}, bf16[4,64,2,512]{3,1,2,0:T(8,128)(2,1)S(1)}, u32[]{:S(2)}) copy-start(bf16[4,64,2,512]{3,1,2,0:T(8,128)(2,1)S(1)} %fusion.56) | copy-start | bytes 1572868
  101.2 26.2 %collective-permute-start.1 = (bf16[512,1024]{1,0:T(8,128)(2,1)S(1)}, bf16[512,1024]{1,0:T(8,128)(2,1)}, u32[]{:S(2)}, u32[]{:S(2)}) collective-permute-start(bf16[512,1024]{1,0:T(8,128)(2,1)S(1)} %convolution_convert_fusion.3), channel_id=1, source_target_pairs={{0,1},{1,0},{2,3},{3,2},{4,5},{5,4},{6,7},{7,6},{8,9},{9,8},{10,11... | collective-permute-start | bytes 3145736 | tf_op jit(solution)/shard_map/ppermute | solution.py:58
  102.8 47.0 %collective-permute-start.3 = (bf16[512,1024]{1,0:T(8,128)(2,1)}, bf16[512,1024]{1,0:T(8,128)(2,1)}, u32[]{:S(2)}, u32[]{:S(2)}) collective-permute-start(bf16[512,1024]{1,0:T(8,128)(2,1)} %refs_2_.1), channel_id=1, source_target_pairs={{0,1},{1,0},{2,3},{3,2},{4,5},{5,4},{6,7},{7,6},{8,9},{9,8},{10,11... | collective-permute-start | bytes 3145736 | tf_op jit(solution)/shard_map/ppermute | solution.py:58
  103.3 27.3 %copy-start.39 = (f32[1024]{0:T(1024)S(1)}, f32[1024]{0:T(1024)}, u32[]{:S(2)}) copy-start(f32[1024]{0:T(1024)} %param.34) | copy-start | bytes 12292
  131.8 39.8 %collective-permute-start.2 = (bf16[512,1024]{1,0:T(8,128)(2,1)S(1)}, bf16[512,1024]{1,0:T(8,128)(2,1)}, u32[]{:S(2)}, u32[]{:S(2)}) collective-permute-start(bf16[512,1024]{1,0:T(8,128)(2,1)S(1)} %multiply_convert_fusion.refs_0_), channel_id=1, source_target_pairs={{0,1},{1,0},{2,3},{3,2},{4,5},{5,4},{6,7},{7,6},{8,9},{9,8},{10,11... | collective-permute-start | bytes 3145736 | tf_op jit(solution)/shard_map/ppermute | solution.py:58
  171.6 84.0 %copy-start.40 = (f32[1024]{0:T(1024)S(1)}, f32[1024]{0:T(1024)}, u32[]{:S(2)}) copy-start(f32[1024]{0:T(1024)} %param.34) | copy-start | bytes 12292
  171.7 84.0 %copy-start.44 = (f32[512]{0:T(512)S(1)}, f32[512]{0:T(512)}, u32[]{:S(2)}) copy-start(f32[512]{0:T(512)} %copy-done.43) | copy-start | bytes 6148
  229.4 26.3 %collective-permute-start.5 = (bf16[512,1024]{1,0:T(8,128)(2,1)}, bf16[512,1024]{1,0:T(8,128)(2,1)S(1)}, u32[]{:S(2)}, u32[]{:S(2)}) collective-permute-start(bf16[512,1024]{1,0:T(8,128)(2,1)} %get-tuple-element.85), channel_id=1, source_target_pairs={{0,1},{1,0},{2,3},{3,2},{4,5},{5,4},{6,7},{7,6},{8,9},{9,8},{10,11... | collective-permute-start | bytes 3145736 | tf_op jit(solution)/shard_map/ppermute | solution.py:58
  230.9 46.2 %collective-permute-start.4 = (bf16[512,1024]{1,0:T(8,128)(2,1)}, bf16[512,1024]{1,0:T(8,128)(2,1)S(1)}, u32[]{:S(2)}, u32[]{:S(2)}) collective-permute-start(bf16[512,1024]{1,0:T(8,128)(2,1)} %get-tuple-element.83), channel_id=1, source_target_pairs={{0,1},{1,0},{2,3},{3,2},{4,5},{5,4},{6,7},{7,6},{8,9},{9,8},{10,11... | collective-permute-start | bytes 3145736 | tf_op jit(solution)/shard_map/ppermute | solution.py:58
  255.7 21.5 %copy-start.8 = (f32[512,1024]{1,0:T(8,128)S(1)}, f32[512,1024]{1,0:T(8,128)}, u32[]{:S(2)}) copy-start(f32[512,1024]{1,0:T(8,128)} %get-tuple-element.84) | copy-start | bytes 6291460
  255.7 21.5 %copy-start.26 = (f32[512,1024]{1,0:T(8,128)S(1)}, f32[512,1024]{1,0:T(8,128)}, u32[]{:S(2)}) copy-start(f32[512,1024]{1,0:T(8,128)} %get-tuple-element.82) | copy-start | bytes 6291460
  277.1 5.5 copy-start.3
  281.2 24.2 %collective-permute-start.6 = (bf16[512,1024]{1,0:T(8,128)(2,1)S(1)}, bf16[512,1024]{1,0:T(8,128)(2,1)S(1)}, u32[]{:S(2)}, u32[]{:S(2)}) collective-permute-start(bf16[512,1024]{1,0:T(8,128)(2,1)S(1)} %get-tuple-element.139), channel_id=1, source_target_pairs={{0,1},{1,0},{2,3},{3,2},{4,5},{5,4},{6,7},{7,6},{8,9},{9,8},{10,11... | collective-permute-start | bytes 3145736 | tf_op jit(solution)/shard_map/ppermute | solution.py:58
  285.2 20.3 %copy-start.56 = (bf16[4,64,2,512]{3,1,2,0:T(8,128)(2,1)S(1)}, bf16[4,64,2,512]{3,1,2,0:T(8,128)(2,1)}, u32[]{:S(2)}) copy-start(bf16[4,64,2,512]{3,1,2,0:T(8,128)(2,1)} %copy-done.55) | copy-start | bytes 1572868
  285.2 20.2 %copy-start.58 = (bf16[4,64,2,512]{3,1,2,0:T(8,128)(2,1)S(1)}, bf16[4,64,2,512]{3,1,2,0:T(8,128)(2,1)}, u32[]{:S(2)}) copy-start(bf16[4,64,2,512]{3,1,2,0:T(8,128)(2,1)} %copy-done.57) | copy-start | bytes 1572868
  305.5 5.1 slice-start.4
  317.9 4.8 copy-start.11
  317.9 8.9 %slice-start = ((s8[16777216]{0:T(1024)(128)(4,1)}), s8[4194304]{0:T(1024)(128)(4,1)S(1)}, s32[]{:S(2)}) async-start(s8[16777216]{0:T(1024)(128)(4,1)} %bitcast.159), calls=%async_computation.6 | async-start | bytes 8388608
  317.9 8.9 %slice-start.1 = ((s8[16777216]{0:T(1024)(128)(4,1)}), s8[4194304]{0:T(1024)(128)(4,1)S(1)}, s32[]{:S(2)}) async-start(s8[16777216]{0:T(1024)(128)(4,1)} %bitcast.159), calls=%async_computation.7 | async-start | bytes 8388608
  317.9 8.9 %slice-start.2 = ((s8[16777216]{0:T(1024)(128)(4,1)}), s8[4194304]{0:T(1024)(128)(4,1)S(1)}, s32[]{:S(2)}) async-start(s8[16777216]{0:T(1024)(128)(4,1)} %bitcast.159), calls=%async_computation.8 | async-start | bytes 8388608
  339.2 11.6 %copy-start.16 = (bf16[1024,4,64]{0,2,1:T(8,128)(2,1)S(1)}, bf16[1024,4,64]{0,2,1:T(8,128)(2,1)}, u32[]{:S(2)}) copy-start(bf16[1024,4,64]{0,2,1:T(8,128)(2,1)} %copy-done.14) | copy-start | bytes 1572868
  352.4 6.3 %copy-start.4 = (f32[1024,1024]{0,1:T(8,128)S(1)}, f32[1024,1024]{0,1:T(8,128)}, u32[]{:S(2)}) copy-start(f32[1024,1024]{0,1:T(8,128)} %copy-done.2) | copy-start | bytes 12582916
  375.5 213.4 %reduce-scatter.5.cloned.1.call-start = ((), (), s32[]{:S(2)}) async-start(), calls=%async_computation.4 | async-start | bytes 15040512 | tf_op jit(solution)/shard_map/reduce_scatter | solution.py:322
  378.0 24.7 %copy-start.38 = (f32[1024]{0:T(1024)S(1)}, f32[1024]{0:T(1024)}, u32[]{:S(2)}) copy-start(f32[1024]{0:T(1024)} %param.27) | copy-start | bytes 12292
  378.0 24.7 %copy-start.42 = (f32[512]{0:T(512)S(1)}, f32[512]{0:T(512)}, u32[]{:S(2)}) copy-start(f32[512]{0:T(512)} %copy-done.41) | copy-start | bytes 6148
  379.3 26.4 %copy-start.47 = (f32[1024]{0:T(1024)S(1)}, f32[1024]{0:T(1024)}, u32[]{:S(2)}) copy-start(f32[1024]{0:T(1024)} %get-tuple-element.126) | copy-start | bytes 12292
  379.3 35.1 %copy-start.46 = (f32[512]{0:T(512)S(1)}, f32[512]{0:T(512)}, u32[]{:S(2)}) copy-start(f32[512]{0:T(512)} %copy-done.45) | copy-start | bytes 6148
  379.3 39.5 %copy-start.9 = (f32[512,1024]{1,0:T(8,128)S(1)}, f32[512,1024]{1,0:T(8,128)}, u32[]{:S(2)}) copy-start(f32[512,1024]{1,0:T(8,128)} %get-tuple-element.140) | copy-start | bytes 6291460
  379.3 23.3 %collective-permute-start.7 = (bf16[512,1024]{1,0:T(8,128)(2,1)S(1)}, bf16[512,1024]{1,0:T(8,128)(2,1)S(1)}, u32[]{:S(2)}, u32[]{:S(2)}) collective-permute-start(bf16[512,1024]{1,0:T(8,128)(2,1)S(1)} %fusion.39), channel_id=1, source_target_pairs={{0,1},{1,0},{2,3},{3,2},{4,5},{5,4},{6,7},{7,6},{8,9},{9,8},{10,11... | collective-permute-start | bytes 3145736 | tf_op jit(solution)/shard_map/ppermute | solution.py:58
  405.8 3.7 collective-permute-start.8
  409.5 1.2 collective-permute-start.9
  410.7 3.7 collective-permute-start.10
  414.4 4.5 collective-permute-start.11
  418.8 4.6 collective-permute-start.12
  (34 other events, 70.5 us)
Sparse Core Ops, SparseCore 0:
  10.9 48.1 all-gather.2
  61.9 109.4 all-gather.4
  375.6 64.7 reduce-scatter.6
  444.4 144.4 reduce-scatter.4

commit v2 on v1

--- a/solution.py
+++ b/solution.py
@@ -101,56 +101,209 @@
     return values
 
 
-def ffn_body(count, width, *refs):
-    rows_in = refs[:count]
-    cotangent_in = refs[count : 2 * count]
-    weights = refs[2 * count]
-    outs = refs[2 * count + 1 : 3 * count + 1]
-    grads = refs[3 * count + 1 : 4 * count + 1]
-    weight_grads = refs[4 * count + 1]
-    rows_turned, cotangent_turned, out_sum, grad_sum, hidden_all, pair_all = refs[4 * count + 2 :]
+def ring_size():
+    return lax.axis_size("fsdp") // 2
+
+
+def chip_at(place):
+    chips = ring_size()
+    if isinstance(place, int):
+        return 2 * place if place < chips // 2 else 2 * (chips - 1 - place) + 1
+    return jnp.where(place < chips // 2, 2 * place, 2 * (chips - 1 - place) + 1)
+
+
+def own_place():
+    chip = lax.axis_index("fsdp") // 2
+    return jnp.where(chip % 2 == 0, chip // 2, ring_size() - 1 - chip // 2)
+
+
+def pass_on(values, direction):
+    chips = ring_size()
+    pairs = [
+        (2 * chip_at(place) + core, 2 * chip_at((place + direction) % chips) + core)
+        for place in range(chips)
+        for core in range(2)
+    ]
+    return lax.ppermute(values, "fsdp", pairs)
+
+
+def shard_table(ahead):
+    core = lax.axis_index("fsdp") % 2
+    chips = chip_at((own_place() + jnp.array(ahead, jnp.int32)) % ring_size())
+    return jnp.concatenate([2 * chips + core, 2 * chips + 1 - core]).astype(jnp.int32)
+
+
+def assemble_body(count, table, *refs):
+    whole = refs[count]
+    rows = refs[0].shape[0]
+    for at in range(count):
+        start = pl.multiple_of(table[at] * rows, rows)
+        whole[pl.ds(start, rows), :] = refs[at][...]
+
+
+def gather_ring(shard):
+    chips = ring_size()
+    ahead = [0]
+    blocks = [shard]
+    down = up = shard
+    for step in range(1, chips // 2 + 1):
+        down = pass_on(down, 1)
+        ahead.append(chips - step)
+        blocks.append(down)
+        if step < chips // 2:
+            up = pass_on(up, -1)
+            ahead.append(step)
+            blocks.append(up)
+    blocks = blocks + [swap(block, "fsdp") for block in blocks]
+    rows, columns = shard.shape
+    count = len(blocks)
+    vmem = pl.BlockSpec(memory_space=pltpu.VMEM)
+    return pl.pallas_call(
+        partial(assemble_body, count),
+        in_specs=[pl.BlockSpec(memory_space=pltpu.SMEM)] + [vmem] * count,
+        out_specs=vmem,
+        out_shape=jax.ShapeDtypeStruct((count * rows, columns), shard.dtype),
+        compiler_params=pltpu.CompilerParams(vmem_limit_bytes=48 * 1024 * 1024),
+        name="assemble",
+    )(shard_table(ahead), *blocks)
+
+
+def ring_groups():
+    chips = ring_size()
+    middle = [[chips // 2 - step, chips // 2 + step] for step in range(1, chips // 2)]
+    return [[chips // 2]] + middle + [[0]]
+
+
+def weight_grad_body(parts, groups, rows, *refs):
+    table = refs[0]
+    first_in = refs[1 : 1 + parts]
+    second_in = refs[1 + parts : 1 + 2 * parts]
+    first_grads = refs[1 + 2 * parts : 1 + 3 * parts]
+    second_grads = refs[1 + 3 * parts : 1 + 4 * parts]
+    outs = refs[1 + 4 * parts : -3]
+    first_turned, second_turned, total = refs[-3:]
+    part_rows = first_in[0].shape[0]
+    first_width = first_grads[0].shape[1]
+
+    @pl.when(pl.program_id(0) == 0)
+    def _():
+        for part in range(parts):
+            span = pl.ds(part * part_rows, part_rows)
+            first_turned[:, span] = first_in[part][...].T
+            second_turned[:, span] = second_in[part][...].T
+
+    def joined(pieces):
+        if parts == 1:
+            return pieces[0][...]
+        return jnp.concatenate([piece[...] for piece in pieces], axis=0)
+
+    total[:, :first_width] = dot(first_turned[...], joined(first_grads)).astype(bf16)
+    total[:, first_width:] = dot(second_turned[...], joined(second_grads)).astype(bf16)
+    count = sum(len(group) for group in groups)
+    at = 0
+    for number, group in enumerate(groups):
+        for member in range(len(group)):
+            mine = pl.multiple_of(table[at] * rows, rows)
+            outs[number][member] = total[pl.ds(mine, rows), :]
+            near = pl.multiple_of(table[count + at] * rows, rows)
+            outs[len(groups) + number][member] = total[pl.ds(near, rows), :]
+            at += 1
+
+
+def weight_grads(first, second, first_grads, second_grads, steps):
+    parts = len(first)
+    part_rows, model = first[0].shape
+    length = parts * part_rows
+    first_width = first_grads[0].shape[1] // steps
+    second_width = second_grads[0].shape[1] // steps
+    width = first_width + second_width
+    groups = ring_groups()
+    count = 2 * ring_size()
+    rows = model // count
+    table = shard_table([place for group in groups for place in group])
+    whole = pl.BlockSpec((part_rows, model), lambda i: (0, 0))
+    outs = [jax.ShapeDtypeStruct((len(group), rows, steps * width), bf16) for group in groups] * 2
+    out_specs = [
+        pl.BlockSpec((len(group), rows, width), lambda i: (0, 0, i)) for group in groups
+    ] * 2
+    results = pl.pallas_call(
+        partial(weight_grad_body, parts, groups, rows),
+        grid=(steps,),
+        in_specs=[pl.BlockSpec(memory_space=pltpu.SMEM)]
+        + [whole] * (2 * parts)
+        + [pl.BlockSpec((part_rows, first_width), lambda i: (0, i))] * parts
+        + [pl.BlockSpec((part_rows, second_width), lambda i: (0, i))] * parts,
+        out_specs=out_specs,
+        out_shape=outs,
+        scratch_shapes=[
+            pltpu.VMEM((model, length), bf16),
+            pltpu.VMEM((model, length), bf16),
+            pltpu.VMEM((model, width), bf16),
+        ],
+        compiler_params=pltpu.CompilerParams(vmem_limit_bytes=56 * 1024 * 1024),
+        cost_estimate=pl.CostEstimate(
+            flops=2 * length * model * steps * width,
+            bytes_accessed=4 * model * steps * width,
+            transcendentals=0,
+        ),
+        name="weight_grads",
+    )(table, *first, *second, *first_grads, *second_grads)
+    mine = results[: len(groups)]
+    near = [swap(block, "fsdp") for block in results[len(groups) :]]
+    half = steps * width // 2
+
+    def share(group, member):
+        return mine[group][member].astype(f32) + near[group][member].astype(f32)
+
+    far = share(0, 0).astype(bf16)
+    down = pass_on(far[:, :half], 1)
+    up = pass_on(far[:, half:], -1)
+    for step in range(1, ring_size() // 2):
+        ahead, behind = share(step, 0), share(step, 1)
+        if step == 1:
+            ahead = jnp.concatenate([ahead[:, :half] + down.astype(f32), ahead[:, half:]], axis=1)
+            behind = jnp.concatenate([behind[:, :half], behind[:, half:] + up.astype(f32)], axis=1)
+        else:
+            ahead = ahead + down.astype(f32)
+            behind = behind + up.astype(f32)
+        down = pass_on(ahead.astype(bf16), 1)
+        up = pass_on(behind.astype(bf16), -1)
+    return share(len(groups) - 1, 0) + down.astype(f32) + up.astype(f32)
+
+
+def ffn_body(width, rows_in, cotangent_in, weights, out, grad, pairs, hiddens, out_sum, grad_sum):
     step = pl.program_id(0)
-    part_rows = rows_in[0].shape[0]
+    length = rows_in.shape[0]
 
     @pl.when(step == 0)
     def _():
-        for part in range(count):
-            span = pl.ds(part * part_rows, part_rows)
-            rows_turned[:, span] = rows_in[part][...].T
-            cotangent_turned[:, span] = cotangent_in[part][...].T
         out_sum[...] = jnp.zeros_like(out_sum)
         grad_sum[...] = jnp.zeros_like(grad_sum)
 
     pair_weights = weights[:, : 2 * width]
     down = weights[:, 2 * width :]
-    chunk = min(256, part_rows)
-    for part in range(count):
-        for start in range(0, part_rows, chunk):
-            here = pl.ds(start, chunk)
-            span = pl.ds(part * part_rows + start, chunk)
-            both = dot(rows_in[part][here, :], pair_weights)
-            gate = both[:, :width]
-            up = both[:, width:]
-            hidden_grad = dot(cotangent_in[part][here, :], down)
-            sigmoid = 1.0 / (1.0 + jnp.exp(-gate))
-            silu = gate * sigmoid
-            hidden = (silu * up).astype(bf16)
-            gate_grad = hidden_grad * up * sigmoid * (1.0 + gate * (1.0 - sigmoid))
-            up_grad = hidden_grad * silu
-            pair = jnp.concatenate([gate_grad.astype(bf16), up_grad.astype(bf16)], axis=1)
-            hidden_all[span, :] = hidden
-            pair_all[span, :] = pair
-            out_sum[span, :] += dot_transposed(hidden, down)
-            grad_sum[span, :] += dot_transposed(pair, pair_weights)
-    weight_grads[:, : 2 * width] = dot(rows_turned[...], pair_all[...]).astype(bf16)
-    weight_grads[:, 2 * width :] = dot(cotangent_turned[...], hidden_all[...]).astype(bf16)
+    chunk = min(256, length)
+    for start in range(0, length, chunk):
+        span = pl.ds(start, chunk)
+        both = dot(rows_in[span, :], pair_weights)
+        gate = both[:, :width]
+        up = both[:, width:]
+        hidden_grad = dot(cotangent_in[span, :], down)
+        sigmoid = 1.0 / (1.0 + jnp.exp(-gate))
+        silu = gate * sigmoid
+        hidden = (silu * up).astype(bf16)
+        gate_grad = hidden_grad * up * sigmoid * (1.0 + gate * (1.0 - sigmoid))
+        up_grad = hidden_grad * silu
+        pair = jnp.concatenate([gate_grad.astype(bf16), up_grad.astype(bf16)], axis=1)
+        hiddens[span, :] = hidden
+        pairs[span, :] = pair
+        out_sum[span, :] += dot_transposed(hidden, down)
+        grad_sum[span, :] += dot_transposed(pair, pair_weights)
 
     @pl.when(step == pl.num_programs(0) - 1)
     def _():
-        for part in range(count):
-            span = pl.ds(part * part_rows, part_rows)
-            outs[part][...] = out_sum[span, :].astype(outs[part].dtype)
-            grads[part][...] = grad_sum[span, :].astype(grads[part].dtype)
+        out[...] = out_sum[...].astype(out.dtype)
+        grad[...] = grad_sum[...].astype(grad.dtype)
 
 
 def hidden_width(units):
@@ -160,33 +313,39 @@
     return units
 
 
-def feed_forward(rows_parts, cotangent_parts, weights, width):
-    count = len(rows_parts)
-    part_rows, model = rows_parts[0].shape
-    length = count * part_rows
+def feed_forward(rows, cotangent, weights, width, kind):
+    length, model = rows.shape
     steps = weights.shape[1] // (3 * width)
-    whole = pl.BlockSpec((part_rows, model), lambda i: (0, 0))
-    block = pl.BlockSpec((model, 3 * width), lambda i: (0, i))
-    kinds = [f32] + [bf16] * (count - 1)
-    shapes = [jax.ShapeDtypeStruct((part_rows, model), kind) for kind in kinds]
-    results = pl.pallas_call(
-        partial(ffn_body, count, width),
+    whole = pl.BlockSpec((length, model), lambda i: (0, 0))
+    sums = jax.ShapeDtypeStruct((length, model), kind)
+    return pl.pallas_call(
+        partial(ffn_body, width),
         grid=(steps,),
-        in_specs=[whole] * (2 * count) + [block],
-        out_specs=[whole] * (2 * count) + [block],
-        out_shape=shapes + shapes + [jax.ShapeDtypeStruct(weights.shape, bf16)],
+        in_specs=[whole, whole, pl.BlockSpec((model, 3 * width), lambda i: (0, i))],
+        out_specs=[
+            whole,
+            whole,
+            pl.BlockSpec((length, 2 * width), lambda i: (0, i)),
+            pl.BlockSpec((length, width), lambda i: (0, i)),
+        ],
+        out_shape=[
+            sums,
+            sums,
+            jax.ShapeDtypeStruct((length, steps * 2 * width), bf16),
+            jax.ShapeDtypeStruct((length, steps * width), bf16),
+        ],
         scratch_shapes=[
-            pltpu.VMEM((model, length), bf16),
-            pltpu.VMEM((model, length), bf16),
             pltpu.VMEM((length, model), f32),
             pltpu.VMEM((length, model), f32),
-            pltpu.VMEM((length, width), bf16),
-            pltpu.VMEM((length, 2 * width), bf16),
         ],
         compiler_params=pltpu.CompilerParams(vmem_limit_bytes=56 * 1024 * 1024),
+        cost_estimate=pl.CostEstimate(
+            flops=12 * length * model * steps * width,
+            bytes_accessed=8 * model * steps * width,
+            transcendentals=length * steps * width,
+        ),
         name="feed_forward",
-    )(*rows_parts, *cotangent_parts, weights)
-    return results[:count], results[count : 2 * count], results[2 * count]
+    )(rows, cotangent, weights)
 
 
 def block_scores(query_block, key_rows, row_start, finish):
@@ -292,7 +451,7 @@
         ],
         axis=2,
     ).reshape(shard, 3 * units)
-    attn_full = lax.all_gather(attn_shard, "fsdp", axis=0, tiled=True)
+    attn_full = gather_ring(attn_shard)
     qkv_full = attn_full[:, :qkv_columns]
     out_full = attn_full[:, qkv_columns:]
     ffn_full = lax.all_gather(ffn_shard, "fsdp", axis=0, tiled=True)
@@ -318,16 +477,18 @@
     middle = residual + narrow(branch)
     normed_ffn, ffn_norm_pull = jax.vjp(rms_norm, middle, ffn_gain)
     ffn_parts = widen(normed_ffn.astype(bf16))
-    out_parts, grad_parts, ffn_grads = feed_forward(ffn_parts, cotangent_parts, ffn_full, width)
-    ffn_grads = lax.psum_scatter(ffn_grads, "fsdp", scatter_dimension=0, tiled=True)
-
+    results = [
+        feed_forward(rows, cotangent, ffn_full, width, bf16 if at else f32)
+        for at, (rows, cotangent) in reversed(list(enumerate(zip(ffn_parts, cotangent_parts))))
+    ][::-1]
+    out_parts, grad_parts, pairs, hiddens = zip(*results)
     ffn_normed_grad = narrow(grad_parts)
     middle_piece, ffn_gain_local = ffn_norm_pull(ffn_normed_grad)
     middle_grad = out_cotangent.astype(f32) + middle_piece
     branch_rows = in_order(widen(middle_grad.astype(bf16)))
     output = (middle + narrow(out_parts)).astype(bf16)
-
-    out_grad = dot_leading(branch_rows, attended)
+    ffn_grads = weight_grads(ffn_parts, cotangent_parts, pairs, hiddens, steps)
+
     attended_grad = dot(branch_rows, out_full).astype(bf16)
     query_grad, key_grad, value_grad = attend_back(
         query_rows, key_rows, value_rows, log_totals, attended_grad
@@ -344,19 +505,16 @@
         axis=1,
     )
     normed_grad = narrow(tuple(dot_transposed(part, qkv_full) for part in in_parts(qkv_grad)))
-    qkv_weight_grad = dot_leading(normed_rows, qkv_grad)
-    attn_grads = jnp.concatenate([qkv_weight_grad.astype(bf16), out_grad.astype(bf16)], axis=1)
-    attn_grads = lax.psum_scatter(attn_grads, "fsdp", scatter_dimension=0, tiled=True)
+    attn_grads = weight_grads((normed_rows,), (branch_rows,), (qkv_grad,), (attended,), 1)
     tokens_piece, attn_gain_local = attn_norm_pull(normed_grad)
     tokens_grad = middle_grad + tokens_piece
     model = attn_gain.shape[0]
     gain_totals = sum_everywhere(
         jnp.concatenate([attn_gain_local, ffn_gain_local, query_gain_local, key_gain_local])
     )
-    attn_grads = attn_grads.astype(f32)
     ffn_grads = ffn_grads.reshape(shard, steps, 3, width)
     gate_grad, up_grad, down_grad = (
-        ffn_grads[:, :, at].reshape(shard, units).astype(f32) for at in range(3)
+        ffn_grads[:, :, at].reshape(shard, units) for at in range(3)
     )
     return (
         output,

time: 610 us -> 523 us (0.86)
  waiting for transfers between devices: 356 us -> 179 us
  starting transfers between devices: 13.8 us -> 71.5 us
  Pallas kernels: 57.7 us -> 79.8 us
  other arithmetic: 53.7 us -> 65.2 us
    reduce_scatter x1 -> x0, waiting for transfers between devices: 144 us -> none  [on_device(): lax.psum_scatter(ffn_grads, 'fsdp', scatter_dimension=0, tiled=True)]
    ppermute x0 -> x23, starting transfers between devices: none -> 55.1 us  [pass_on(): return lax.ppermute(values, 'fsdp', pairs)]
    ppermute x13 -> x31, waiting for transfers between devices: 181 us -> 131 us  [swap(): return lax.ppermute(values, axis_name, [(i, i ^ bit) for i in range(count)])]
    ppermute x0 -> x23, waiting for transfers between devices: none -> 44.7 us  [pass_on(): return lax.ppermute(values, 'fsdp', pairs)]
    pallas_call x1 -> x5, Pallas kernels: 57.7 us -> 79.8 us  [the longest x2 45.7 us: feed_forward(): pl.pallas_call(partial(ffn_body, width), grid=(steps,), in_specs=[whole,...]
    unnamed x5 -> x1, waiting for transfers between devices: 16.1 us -> 0.02 us
    unnamed x139 -> x181, local copies, waits for them, and re-layouts: 29.4 us -> 13.4 us
    all_gather x1 -> x0, waiting for transfers between devices: 14.7 us -> none  [on_device(): attn_full = lax.all_gather(attn_shard, 'fsdp', axis=0, tiled=True)]
  transfers between devices with their start and end apart: 17 -> 55, of which waited for: 16 -> 26; matrix products, arithmetic and copies ran while one was open for 11% -> 28% of each run, Pallas kernels for 0% -> 7%
where the time goes in v2:
time: 523 us; the launch traced here: 519 us
  waiting for transfers between devices  179 us (34%)
  Pallas kernels  79.8 us (15%)
  starting transfers between devices  71.5 us (14%)
  matrix products  67.5 us (13%)
  other arithmetic  65.2 us (12%)
  local copies, waits for them, and re-layouts  39.9 us (8%)
  between operations  15.9 us (3%)
    ppermute x31, waiting for transfers between devices, swap(): return lax.ppermute(values, axis_name, [(i, i ^ bit) for i in range(count)])  131 us
    ppermute x23, starting transfers between devices, pass_on(): return lax.ppermute(values, 'fsdp', pairs)  55.1 us
    pallas_call x2, Pallas kernels, feed_forward(): pl.pallas_call(partial(ffn_body, width), grid=(steps,), in_specs=[whole,...  45.7 us
    ppermute x23, waiting for transfers between devices, pass_on(): return lax.ppermute(values, 'fsdp', pairs)  44.7 us
    pallas_call x2, Pallas kernels, weight_grads(): pl.pallas_call(partial(weight_grad_body, parts, groups, rows), grid=(step...  31.8 us
    ppermute x31, starting transfers between devices, swap(): return lax.ppermute(values, axis_name, [(i, i ^ bit) for i in range(count)])  16.4 us
    unnamed x181, local copies, waits for them, and re-layouts  13.4 us
    dot_general x2, matrix products, attend_back(): jnp.einsum('kgqs,qkgd->skd', probability.astype(bf16), grad_block, prefer...  11.6 us
  transfers between devices with their start and end apart: 55, of which 26 were waited for; matrix products, arithmetic and copies ran while one was open for 28% of the time, Pallas kernels for 7%

profile of v2, /device:TPU:0, one launch (start us, length us, event | category | flops | bytes accessed | tf_op | source)
XLA Modules:
  0.0 518.6 jit_solution(1766517679258545584)
XLA Ops:
  13.7 3.1 collective-permute-start.1
  24.2 5.6 %collective-permute-done.3.refs_3_ = bf16[64,1536]{1,0:T(8,128)(2,1)S(1)} collective-permute-done((bf16[64,1536]{1,0:T(8,128)(2,1)S(1)}, bf16[64,1536]{1,0:T(8,128)(2,1)S(1)}, u32[]{:S(2)}, u32[]{:S(2)}) %collective-permute-start.3) | collective-permute-done | bytes 196640 | tf_op jit(solution)/shard_map/ppermute | solution.py:127
  29.7 3.3 collective-permute-start.5
  33.0 3.6 collective-permute-done.4.refs_4_
  36.6 4.4 collective-permute-done.5.refs_5_
  41.0 6.6 %collective-permute-start.7 = (bf16[64,1536]{1,0:T(8,128)(2,1)S(1)}, bf16[64,1536]{1,0:T(8,128)(2,1)S(1)}, u32[]{:S(2)}, u32[]{:S(2)}) collective-permute-start(bf16[64,1536]{1,0:T(8,128)(2,1)S(1)} %collective-permute-done.5.refs_5_), channel_id=1, source_target_pairs={{0,8},{2,10},{8,16},{10,18},{16,24},{18,26},{24,28},{26,30},{28,20... | collective-permute-start | bytes 589832 | tf_op jit(solution)/shard_map/ppermute | solution.py:127
  48.8 4.3 collective-permute-done.6.refs_6_
  67.8 8.6 %fusion.125 = (f32[4,2,512]{2,1,0:T(2,128)S(1)}, f32[4,2,512,1024]{2,3,1,0:T(8,128)}) fusion(bf16[512,4,2,64]{0,3,2,1:T(8,128)(2,1)S(1)} %bitcast.229, bf16[1024,4,64]{0,2,1:T(8,128)(2,1)S(1)} %fusion.70, pred[512,1024]{0,1:T(8,128)(4,1)S(1)} %iota_compare_fusion), kind=kOutput, calls=%fused_computation.236 | convolution fusion | flops 549449728 | bytes 18366464 | tf_op jit(solution)/shard_map/qkgd,skd->kgqs/dot_general | solution.py:353
  76.4 8.1 %fusion.3 = f32[4,2,512]{2,1,0:T(2,128)S(1)} fusion(f32[4,2,512,1024]{2,3,1,0:T(8,128)} %get-tuple-element.200, f32[4,2,512]{2,1,0:T(2,128)S(1)} %get-tuple-element.199), kind=kLoop, calls=%fused_computation.9 | loop fusion | flops 8384512 | bytes 16809984 | tf_op jit(solution)/shard_map/reduce_sum | solution.py:374
  84.6 7.6 %fusion.62 = bf16[4,64,2,512]{3,1,2,0:T(8,128)(2,1)S(1)} fusion(bf16[1024,4,64,1]{0,2,3,1:T(8,128)(2,1)S(1)} %bitcast.227, f32[4,2,512,1024]{2,3,1,0:T(8,128)} %get-tuple-element.200, f32[4,2,512]{2,1,0:T(2,128)S(1)} %fusion.3, f32[4,2,512]{2,1,0:T(2,128)S(1)} %get-tuple-element.199), kind=kOutput, calls=%fused_computation.109 | convolution fusion | flops 549715968 | bytes 17858560 | tf_op jit(solution)/shard_map/kgqs,skd->qkgd/dot_general | solution.py:376
  99.0 2.5 convolution_convert_fusion.1
  104.2 23.5 %collective-permute-done.16 = bf16[512,1024]{1,0:T(8,128)(2,1)} collective-permute-done((bf16[512,1024]{1,0:T(8,128)(2,1)S(1)}, bf16[512,1024]{1,0:T(8,128)(2,1)}, u32[]{:S(2)}, u32[]{:S(2)}) %collective-permute-start.16) | collective-permute-done | bytes 1048608 | tf_op jit(solution)/shard_map/ppermute | solution.py:58
  127.7 2.7 multiply_reduce_fusion.4
  132.0 3.5 all-gather.2.cloned.1.call-done.weights
  135.5 23.2 %feed_forward.2 = (f32[512,1024]{1,0:T(8,128)}, f32[512,1024]{1,0:T(8,128)}, bf16[512,4608]{1,0:T(8,128)(2,1)}, bf16[512,2304]{1,0:T(8,128)(2,1)}) custom-call(bf16[512,1024]{1,0:T(8,128)(2,1)} %multiply_convert_fusion.rows_in.refs_1_, bf16[512,1024]{1,0:T(8,128)(2,1)} %refs_3_.1, bf16[1024,6912]{1,0:T(8,128)(2,1)} %all-gather.2.cloned.1.call-done.weights), custom_call_target="tpu_custom_call" | custom-call | flops 14495514624 | bytes 18874368 | tf_op jit(solution)/shard_map/feed_forward/pallas_call | solution.py:321
  158.7 13.1 %collective-permute-done.17.rows_in.refs_2_ = bf16[512,1024]{1,0:T(8,128)(2,1)} collective-permute-done((bf16[512,1024]{1,0:T(8,128)(2,1)}, bf16[512,1024]{1,0:T(8,128)(2,1)}, u32[]{:S(2)}, u32[]{:S(2)}) %collective-permute-start.17) | collective-permute-done | bytes 1048608 | tf_op jit(solution)/shard_map/ppermute | solution.py:58
  171.8 22.5 %feed_forward.3 = (bf16[512,1024]{1,0:T(8,128)(2,1)}, bf16[512,1024]{1,0:T(8,128)(2,1)}, bf16[512,4608]{1,0:T(8,128)(2,1)}, bf16[512,2304]{1,0:T(8,128)(2,1)}) custom-call(bf16[512,1024]{1,0:T(8,128)(2,1)} %collective-permute-done.17.rows_in.refs_2_, bf16[512,1024]{1,0:T(8,128)(2,1)} %collective-permute-done.18.cotangent_in.refs_4_, ...), custom_call_target="tpu_custom_call" | custom-call | flops 14495514624 | bytes 18874368 | tf_op jit(solution)/shard_map/feed_forward/pallas_call | solution.py:321
  194.3 23.5 %weight_grads.3 = (bf16[1,64,6912]{2,1,0:T(8,128)(2,1)}, bf16[2,64,6912]{2,1,0:T(8,128)(2,1)}, bf16[2,64,6912]{2,1,0:T(8,128)(2,1)}, bf16[2,64,6912]{2,1,0:T(8,1...) custom-call(s32[16]{0:T(128)} %pad_add_fusion.2.refs_0_, ...), custom_call_target="tpu_custom_call" | custom-call | flops 14495514624 | bytes 28311552 | tf_op jit(solution)/shard_map/weight_grads/pallas_call | solution.py:229
  226.7 4.8 collective-permute-start.50
  231.6 18.8 %collective-permute-done.20 = bf16[512,1024]{1,0:T(8,128)(2,1)S(1)} collective-permute-done((bf16[512,1024]{1,0:T(8,128)(2,1)S(1)}, bf16[512,1024]{1,0:T(8,128)(2,1)S(1)}, u32[]{:S(2)}, u32[]{:S(2)}) %collective-permute-start.20) | collective-permute-done | bytes 1048608 | tf_op jit(solution)/shard_map/ppermute | solution.py:58
  250.4 7.2 %collective-permute-start.46 = (bf16[64,3456]{1,0:T(8,128)(2,1)S(1)}, bf16[64,3456]{1,0:T(8,128)(2,1)S(1)}, u32[]{:S(2)}, u32[]{:S(2)}) collective-permute-start(bf16[64,3456]{1,0:T(8,128)(2,1)S(1)} %get-tuple-element.175), channel_id=1, source_target_pairs={{0,8},{2,10},{8,16},{10,18},{16,24},{18,26},{24,28},{26,30},{28,20... | collective-permute-start | bytes 1327112 | tf_op jit(solution)/shard_map/ppermute | solution.py:127
  258.9 13.6 %collective-permute-done.19 = bf16[512,1024]{1,0:T(8,128)(2,1)S(1)} collective-permute-done((bf16[512,1024]{1,0:T(8,128)(2,1)S(1)}, bf16[512,1024]{1,0:T(8,128)(2,1)S(1)}, u32[]{:S(2)}, u32[]{:S(2)}) %collective-permute-start.19) | collective-permute-done | bytes 1048608 | tf_op jit(solution)/shard_map/ppermute | solution.py:58
  272.4 4.0 fusion.111
  278.2 5.1 collective-permute-start.51
  285.0 16.2 %collective-permute-done.21 = bf16[512,1024]{1,0:T(8,128)(2,1)S(1)} collective-permute-done((bf16[512,1024]{1,0:T(8,128)(2,1)S(1)}, bf16[512,1024]{1,0:T(8,128)(2,1)S(1)}, u32[]{:S(2)}, u32[]{:S(2)}) %collective-permute-start.21) | collective-permute-done | bytes 1048608 | tf_op jit(solution)/shard_map/ppermute | solution.py:58
  302.9 2.9 convolution_convert_fusion
  308.0 2.5 fusion.9
  310.5 2.9 fusion.54
  317.9 7.5 %fusion = (f32[4,2,512]{2,1,0:T(2,128)S(1)}, f32[4,1024,512,2]{2,1,3,0:T(8,128)}) fusion(f32[4,2,512,1024]{2,3,1,0:T(8,128)S(1)} %bitcast.211, f32[4,2,512]{2,1,0:T(2,128)S(1)} %bitcast.239, bf16[1024,4,64,1]{0,2,3,1:T(8,128)(2,1)S(1)} %bitcast.228, bf16[512,4,2,64]{0,3,2,1:T(8,128)(2,1)S(1)} %bitcast.217), kind=kOutput, calls=%fused_computation.2 | convolution fusion | flops 549449728 | bytes 34635776 | tf_op jit(solution)/shard_map/qkgd,skd->kgqs/dot_general | solution.py:402
  325.4 8.3 %fusion.2 = bf16[4,2,512,1024]{2,3,1,0:T(8,128)(2,1)S(1)} fusion(f32[4,1024,512,2]{2,1,3,0:T(8,128)} %get-tuple-element.204, f32[4,2,512,1024]{2,3,1,0:T(8,128)S(1)} %bitcast.211, f32[4,2,512]{2,1,0:T(2,128)S(1)} %get-tuple-element.203, f32[4,2,512]{2,1,0:T(2,128)S(1)} %bitcast.240), kind=kLoop, calls=%fused_computation.4 | loop fusion | flops 16777216 | bytes 41975808 | tf_op jit(solution)/shard_map/convert_element_type | solution.py:406
  344.5 2.5 copy.64
  347.1 6.3 %broadcast_multiply_fusion = (f32[1024,4,64]{0,2,1:T(8,128)S(1)}, f32[1024,4,64]{0,2,1:T(8,128)S(1)}) fusion(f32[1024,64]{0,1:T(8,128)S(1)} %copy-done.7, bf16[512,4,2,64]{0,3,2,1:T(8,128)(2,1)} %bitcast.230, bf16[4,2,512,1024]{2,3,1,0:T(8,128)(2,1)} %copy-done.5, f32[512,4,64]{0,2,1:T(8,128)S(1)} %copy-done.27), kind=kOutput, calls=%fused_computation.153 | convolution fusion | flops 537657344 | bytes 11796480 | tf_op jit(solution)/shard_map/kgqs,qkgd->skd/dot_general | solution.py:412
  357.1 9.4 %fusion.58 = bf16[1024,4,64]{0,2,1:T(8,128)(2,1)} fusion(bf16[512,4,2,64]{0,3,2,1:T(8,128)(2,1)S(1)} %bitcast.218, f32[4,2,512,1024]{2,3,1,0:T(8,128)} %get-tuple-element.200, f32[4,2,512]{2,1,0:T(2,128)S(1)} %bitcast.241, f32[512,4,64]{0,2,1:T(8,128)} %fusion.63), kind=kOutput, calls=%fused_computation.107 | convolution fusion | flops 545783808 | bytes 18366464 | tf_op jit(solution)/shard_map/kgqs,qkgd->skd/dot_general | solution.py:416
  367.7 2.7 pad_maximum_fusion.3.refs_3_
  370.4 8.3 %weight_grads.2 = (bf16[1,64,1536]{2,1,0:T(8,128)(2,1)}, bf16[2,64,1536]{2,1,0:T(8,128)(2,1)}, bf16[2,64,1536]{2,1,0:T(8,128)(2,1)}, bf16[2,64,1536]{2,1,0:T(8,1...) custom-call(s32[16]{0:T(128)} %pad_add_fusion.2.refs_0_, ...), custom_call_target="tpu_custom_call" | custom-call | flops 3221225472 | bytes 6291456 | tf_op jit(solution)/shard_map/weight_grads/pallas_call | solution.py:229
  378.9 7.2 %collective-permute-start.47 = (bf16[64,6912]{1,0:T(8,128)(2,1)S(1)}, bf16[64,6912]{1,0:T(8,128)(2,1)S(1)}, u32[]{:S(2)}, u32[]{:S(2)}) collective-permute-start(bf16[64,6912]{1,0:T(8,128)(2,1)S(1)} %pad_maximum_fusion.6), channel_id=1, source_target_pairs={{0,8},{2,10},{8,16},{10,18},{16,24},{18,26},{24,28},{26,30},{28,20... | collective-permute-start | bytes 2654216 | tf_op jit(solution)/shard_map/ppermute | solution.py:127
  388.2 6.8 %collective-permute-done.37 = bf16[64,768]{1,0:T(8,128)(2,1)S(1)} collective-permute-done((bf16[64,768]{1,0:T(8,128)(2,1)S(1)}, bf16[64,768]{1,0:T(8,128)(2,1)S(1)}, u32[]{:S(2)}, u32[]{:S(2)}) %collective-permute-start.37) | collective-permute-done | bytes 98336 | tf_op jit(solution)/shard_map/ppermute | solution.py:127
  396.8 10.9 %collective-permute-done.33 = bf16[64,768]{1,0:T(8,128)(2,1)S(1)} collective-permute-done((bf16[64,768]{1,0:T(8,128)(2,1)S(1)}, bf16[64,768]{1,0:T(8,128)(2,1)S(1)}, u32[]{:S(2)}, u32[]{:S(2)}) %collective-permute-start.33) | collective-permute-done | bytes 98336 | tf_op jit(solution)/shard_map/ppermute | solution.py:127
  408.6 3.1 collective-permute-start.34
  413.0 3.3 collective-permute-done.38
  419.9 3.6 fusion.33
  429.0 13.3 %collective-permute-done.22 = bf16[512,1024]{1,0:T(8,128)(2,1)S(1)} collective-permute-done((bf16[512,1024]{1,0:T(8,128)(2,1)S(1)}, bf16[512,1024]{1,0:T(8,128)(2,1)S(1)}, u32[]{:S(2)}, u32[]{:S(2)}) %collective-permute-start.22) | collective-permute-done | bytes 1048608 | tf_op jit(solution)/shard_map/ppermute | solution.py:58
  456.5 12.1 %collective-permute-done.25 = f32[2176]{0:T(1024)S(1)} collective-permute-done((f32[2176]{0:T(1024)S(1)}, f32[2176]{0:T(1024)S(1)}, u32[]{:S(2)}, u32[]{:S(2)}) %collective-permute-start.25) | collective-permute-done | bytes 8736 | tf_op jit(solution)/shard_map/ppermute | solution.py:58
  473.4 5.3 %collective-permute-start.27 = (f32[2176]{0:T(1024)S(1)}, f32[2176]{0:T(1024)S(1)}, u32[]{:S(2)}, u32[]{:S(2)}) collective-permute-start(f32[2176]{0:T(1024)S(1)} %add.414), channel_id=1, source_target_pairs={{0,16},{2,18},{4,20},{6,22},{8,24},{10,26},{12,28},{14,30},{16,0},... | collective-permute-start | bytes 26120 | tf_op jit(solution)/shard_map/ppermute | solution.py:58
  480.5 15.8 %collective-permute-done.27 = f32[2176]{0:T(1024)S(1)} collective-permute-done((f32[2176]{0:T(1024)S(1)}, f32[2176]{0:T(1024)S(1)}, u32[]{:S(2)}, u32[]{:S(2)}) %collective-permute-start.27) | collective-permute-done | bytes 8736 | tf_op jit(solution)/shard_map/ppermute | solution.py:58
  497.5 2.9 fusion.35
  500.4 2.7 reshape.359
  503.1 4.7 slice_reduce_fusion
  (376 shorter events, 118.3 us)
Async XLA Ops:
  7.2 128.3 %all-gather.2.cloned.1.call-start = ((), (), s32[]{:S(2)}) async-start(), calls=%async_computation | async-start | bytes 15040512 | tf_op jit(solution)/shard_map/all_gather | solution.py:457
  13.7 7.9 %collective-permute-start.1 = (bf16[64,1536]{1,0:T(8,128)(2,1)S(1)}, bf16[64,1536]{1,0:T(8,128)(2,1)S(1)}, u32[]{:S(2)}, u32[]{:S(2)}) collective-permute-start(bf16[64,1536]{1,0:T(8,128)(2,1)S(1)} %pad_maximum_fusion.10.refs_0_), channel_id=1, source_target_pairs={{0,8},{2,10},{8,16},{10,18},{16,24},{18,26},{24,28},{26,30},{28,20... | collective-permute-start | bytes 589832 | tf_op jit(solution)/shard_map/ppermute | solution.py:127
  16.8 7.2 %collective-permute-start.2 = (bf16[64,1536]{1,0:T(8,128)(2,1)S(1)}, bf16[64,1536]{1,0:T(8,128)(2,1)S(1)}, u32[]{:S(2)}, u32[]{:S(2)}) collective-permute-start(bf16[64,1536]{1,0:T(8,128)(2,1)S(1)} %pad_maximum_fusion.10.refs_0_), channel_id=1, source_target_pairs={{0,4},{2,6},{8,0},{10,2},{16,8},{18,10},{24,16},{26,18},{28,24},{3... | collective-permute-start | bytes 589832 | tf_op jit(solution)/shard_map/ppermute | solution.py:127
  16.8 16.2 %collective-permute-start.8 = (bf16[64,1536]{1,0:T(8,128)(2,1)S(1)}, bf16[64,1536]{1,0:T(8,128)(2,1)S(1)}, u32[]{:S(2)}, u32[]{:S(2)}) collective-permute-start(bf16[64,1536]{1,0:T(8,128)(2,1)S(1)} %pad_maximum_fusion.10.refs_0_), channel_id=1, source_target_pairs={{0,2},{2,0},{4,6},{6,4},{8,10},{10,8},{12,14},{14,12},{16,18},{18,... | collective-permute-start | bytes 589832 | tf_op jit(solution)/shard_map/ppermute | solution.py:58
  17.4 41.4 %collective-permute-start = (bf16[512,1024]{1,0:T(8,128)(2,1)S(1)}, bf16[512,1024]{1,0:T(8,128)(2,1)}, u32[]{:S(2)}, u32[]{:S(2)}) collective-permute-start(bf16[512,1024]{1,0:T(8,128)(2,1)S(1)} %fusion.20), channel_id=1, source_target_pairs={{0,1},{1,0},{2,3},{3,2},{4,5},{5,4},{6,7},{7,6},{8,9},{9,8},{10,11... | collective-permute-start | bytes 3145736 | tf_op jit(solution)/shard_map/ppermute | solution.py:58
  21.6 8.1 %collective-permute-start.3 = (bf16[64,1536]{1,0:T(8,128)(2,1)S(1)}, bf16[64,1536]{1,0:T(8,128)(2,1)S(1)}, u32[]{:S(2)}, u32[]{:S(2)}) collective-permute-start(bf16[64,1536]{1,0:T(8,128)(2,1)S(1)} %collective-permute-done.1.refs_1_), channel_id=1, source_target_pairs={{0,8},{2,10},{8,16},{10,18},{16,24},{18,26},{24,28},{26,30},{28,20... | collective-permute-start | bytes 589832 | tf_op jit(solution)/shard_map/ppermute | solution.py:127
  23.9 12.7 %collective-permute-start.4 = (bf16[64,1536]{1,0:T(8,128)(2,1)S(1)}, bf16[64,1536]{1,0:T(8,128)(2,1)S(1)}, u32[]{:S(2)}, u32[]{:S(2)}) collective-permute-start(bf16[64,1536]{1,0:T(8,128)(2,1)S(1)} %collective-permute-done.2.refs_2_), channel_id=1, source_target_pairs={{0,4},{2,6},{8,0},{10,2},{16,8},{18,10},{24,16},{26,18},{28,24},{3... | collective-permute-start | bytes 589832 | tf_op jit(solution)/shard_map/ppermute | solution.py:127
  24.2 12.5 %collective-permute-start.10 = (bf16[64,1536]{1,0:T(8,128)(2,1)S(1)}, bf16[64,1536]{1,0:T(8,128)(2,1)S(1)}, u32[]{:S(2)}, u32[]{:S(2)}) collective-permute-start(bf16[64,1536]{1,0:T(8,128)(2,1)S(1)} %collective-permute-done.2.refs_2_), channel_id=1, source_target_pairs={{0,2},{2,0},{4,6},{6,4},{8,10},{10,8},{12,14},{14,12},{16,18},{18,... | collective-permute-start | bytes 589832 | tf_op jit(solution)/shard_map/ppermute | solution.py:58
  29.7 11.3 %collective-permute-start.5 = (bf16[64,1536]{1,0:T(8,128)(2,1)S(1)}, bf16[64,1536]{1,0:T(8,128)(2,1)S(1)}, u32[]{:S(2)}, u32[]{:S(2)}) collective-permute-start(bf16[64,1536]{1,0:T(8,128)(2,1)S(1)} %collective-permute-done.3.refs_3_), channel_id=1, source_target_pairs={{0,8},{2,10},{8,16},{10,18},{16,24},{18,26},{24,28},{26,30},{28,20... | collective-permute-start | bytes 589832 | tf_op jit(solution)/shard_map/ppermute | solution.py:127
  33.0 15.7 %collective-permute-start.9 = (bf16[64,1536]{1,0:T(8,128)(2,1)S(1)}, bf16[64,1536]{1,0:T(8,128)(2,1)S(1)}, u32[]{:S(2)}, u32[]{:S(2)}) collective-permute-start(bf16[64,1536]{1,0:T(8,128)(2,1)S(1)} %collective-permute-done.1.refs_1_), channel_id=1, source_target_pairs={{0,2},{2,0},{4,6},{6,4},{8,10},{10,8},{12,14},{14,12},{16,18},{18,... | collective-permute-start | bytes 589832 | tf_op jit(solution)/shard_map/ppermute | solution.py:58
  36.6 16.5 %collective-permute-start.11 = (bf16[64,1536]{1,0:T(8,128)(2,1)S(1)}, bf16[64,1536]{1,0:T(8,128)(2,1)S(1)}, u32[]{:S(2)}, u32[]{:S(2)}) collective-permute-start(bf16[64,1536]{1,0:T(8,128)(2,1)S(1)} %collective-permute-done.3.refs_3_), channel_id=1, source_target_pairs={{0,2},{2,0},{4,6},{6,4},{8,10},{10,8},{12,14},{14,12},{16,18},{18,... | collective-permute-start | bytes 589832 | tf_op jit(solution)/shard_map/ppermute | solution.py:58
  36.6 16.5 %collective-permute-start.6 = (bf16[64,1536]{1,0:T(8,128)(2,1)S(1)}, bf16[64,1536]{1,0:T(8,128)(2,1)S(1)}, u32[]{:S(2)}, u32[]{:S(2)}) collective-permute-start(bf16[64,1536]{1,0:T(8,128)(2,1)S(1)} %collective-permute-done.4.refs_4_), channel_id=1, source_target_pairs={{0,4},{2,6},{8,0},{10,2},{16,8},{18,10},{24,16},{26,18},{28,24},{3... | collective-permute-start | bytes 589832 | tf_op jit(solution)/shard_map/ppermute | solution.py:127
  41.0 13.9 %collective-permute-start.7 = (bf16[64,1536]{1,0:T(8,128)(2,1)S(1)}, bf16[64,1536]{1,0:T(8,128)(2,1)S(1)}, u32[]{:S(2)}, u32[]{:S(2)}) collective-permute-start(bf16[64,1536]{1,0:T(8,128)(2,1)S(1)} %collective-permute-done.5.refs_5_), channel_id=1, source_target_pairs={{0,8},{2,10},{8,16},{10,18},{16,24},{18,26},{24,28},{26,30},{28,20... | collective-permute-start | bytes 589832 | tf_op jit(solution)/shard_map/ppermute | solution.py:127
  48.7 6.6 %collective-permute-start.12 = (bf16[64,1536]{1,0:T(8,128)(2,1)S(1)}, bf16[64,1536]{1,0:T(8,128)(2,1)S(1)}, u32[]{:S(2)}, u32[]{:S(2)}) collective-permute-start(bf16[64,1536]{1,0:T(8,128)(2,1)S(1)} %collective-permute-done.4.refs_4_), channel_id=1, source_target_pairs={{0,2},{2,0},{4,6},{6,4},{8,10},{10,8},{12,14},{14,12},{16,18},{18,... | collective-permute-start | bytes 589832 | tf_op jit(solution)/shard_map/ppermute | solution.py:58
  101.5 26.2 %collective-permute-start.16 = (bf16[512,1024]{1,0:T(8,128)(2,1)S(1)}, bf16[512,1024]{1,0:T(8,128)(2,1)}, u32[]{:S(2)}, u32[]{:S(2)}) collective-permute-start(bf16[512,1024]{1,0:T(8,128)(2,1)S(1)} %convolution_convert_fusion.1), channel_id=1, source_target_pairs={{0,1},{1,0},{2,3},{3,2},{4,5},{5,4},{6,7},{7,6},{8,9},{9,8},{10,11... | collective-permute-start | bytes 3145736 | tf_op jit(solution)/shard_map/ppermute | solution.py:58
  101.9 56.8 %collective-permute-start.18 = (bf16[512,1024]{1,0:T(8,128)(2,1)}, bf16[512,1024]{1,0:T(8,128)(2,1)}, u32[]{:S(2)}, u32[]{:S(2)}) collective-permute-start(bf16[512,1024]{1,0:T(8,128)(2,1)} %refs_3_.1), channel_id=1, source_target_pairs={{0,1},{1,0},{2,3},{3,2},{4,5},{5,4},{6,7},{7,6},{8,9},{9,8},{10,11... | collective-permute-start | bytes 3145736 | tf_op jit(solution)/shard_map/ppermute | solution.py:58
  131.7 40.2 %collective-permute-start.17 = (bf16[512,1024]{1,0:T(8,128)(2,1)}, bf16[512,1024]{1,0:T(8,128)(2,1)}, u32[]{:S(2)}, u32[]{:S(2)}) collective-permute-start(bf16[512,1024]{1,0:T(8,128)(2,1)} %multiply_convert_fusion.rows_in.refs_1_), channel_id=1, source_target_pairs={{0,1},{1,0},{2,3},{3,2},{4,5},{5,4},{6,7},{7,6},{8,9},{9,8},{10,11... | collective-permute-start | bytes 3145736 | tf_op jit(solution)/shard_map/ppermute | solution.py:58
  217.8 8.6 %collective-permute-start.45 = (bf16[1,64,6912]{2,1,0:T(8,128)(2,1)}, bf16[1,64,6912]{2,1,0:T(8,128)(2,1)S(1)}, u32[]{:S(2)}, u32[]{:S(2)}) collective-permute-start(bf16[1,64,6912]{2,1,0:T(8,128)(2,1)} %get-tuple-element.132), channel_id=1, source_target_pairs={{0,2},{2,0},{4,6},{6,4},{8,10},{10,8},{12,14},{14,12},{16,18},{18,... | collective-permute-start | bytes 2654216 | tf_op jit(solution)/shard_map/ppermute | solution.py:58
  223.9 52.8 %collective-permute-start.44 = (bf16[2,64,6912]{2,1,0:T(8,128)(2,1)S(1)}, bf16[2,64,6912]{2,1,0:T(8,128)(2,1)S(1)}, u32[]{:S(2)}, u32[]{:S(2)}) collective-permute-start(bf16[2,64,6912]{2,1,0:T(8,128)(2,1)S(1)} %copy-done.79), channel_id=1, source_target_pairs={{0,2},{2,0},{4,6},{6,4},{8,10},{10,8},{12,14},{14,12},{16,18},{18,... | collective-permute-start | bytes 5308424 | tf_op jit(solution)/shard_map/ppermute | solution.py:58
  224.4 192.7 %collective-permute-start.43 = (bf16[2,64,6912]{2,1,0:T(8,128)(2,1)}, bf16[2,64,6912]{2,1,0:T(8,128)(2,1)}, u32[]{:S(2)}, u32[]{:S(2)}) collective-permute-start(bf16[2,64,6912]{2,1,0:T(8,128)(2,1)} %get-tuple-element.128), channel_id=1, source_target_pairs={{0,2},{2,0},{4,6},{6,4},{8,10},{10,8},{12,14},{14,12},{16,18},{18,... | collective-permute-start | bytes 5308424 | tf_op jit(solution)/shard_map/ppermute | solution.py:58
  224.4 26.0 %collective-permute-start.20 = (bf16[512,1024]{1,0:T(8,128)(2,1)S(1)}, bf16[512,1024]{1,0:T(8,128)(2,1)S(1)}, u32[]{:S(2)}, u32[]{:S(2)}) collective-permute-start(bf16[512,1024]{1,0:T(8,128)(2,1)S(1)} %copy-done.81), channel_id=1, source_target_pairs={{0,1},{1,0},{2,3},{3,2},{4,5},{5,4},{6,7},{7,6},{8,9},{9,8},{10,11... | collective-permute-start | bytes 3145736 | tf_op jit(solution)/shard_map/ppermute | solution.py:58
  224.7 47.7 %collective-permute-start.19 = (bf16[512,1024]{1,0:T(8,128)(2,1)S(1)}, bf16[512,1024]{1,0:T(8,128)(2,1)S(1)}, u32[]{:S(2)}, u32[]{:S(2)}) collective-permute-start(bf16[512,1024]{1,0:T(8,128)(2,1)S(1)} %copy-done.80), channel_id=1, source_target_pairs={{0,1},{1,0},{2,3},{3,2},{4,5},{5,4},{6,7},{7,6},{8,9},{9,8},{10,11... | collective-permute-start | bytes 3145736 | tf_op jit(solution)/shard_map/ppermute | solution.py:58
  226.7 50.4 %collective-permute-start.50 = (bf16[64,3456]{1,0:T(8,128)(2,1)S(1)}, bf16[64,3456]{1,0:T(8,128)(2,1)S(1)}, u32[]{:S(2)}, u32[]{:S(2)}) collective-permute-start(bf16[64,3456]{1,0:T(8,128)(2,1)S(1)} %get-tuple-element.176), channel_id=1, source_target_pairs={{0,4},{2,6},{8,0},{10,2},{16,8},{18,10},{24,16},{26,18},{28,24},{3... | collective-permute-start | bytes 1327112 | tf_op jit(solution)/shard_map/ppermute | solution.py:127
  250.4 33.8 %collective-permute-start.46 = (bf16[64,3456]{1,0:T(8,128)(2,1)S(1)}, bf16[64,3456]{1,0:T(8,128)(2,1)S(1)}, u32[]{:S(2)}, u32[]{:S(2)}) collective-permute-start(bf16[64,3456]{1,0:T(8,128)(2,1)S(1)} %get-tuple-element.175), channel_id=1, source_target_pairs={{0,8},{2,10},{8,16},{10,18},{16,24},{18,26},{24,28},{26,30},{28,20... | collective-permute-start | bytes 1327112 | tf_op jit(solution)/shard_map/ppermute | solution.py:127
  276.4 24.7 %collective-permute-start.21 = (bf16[512,1024]{1,0:T(8,128)(2,1)S(1)}, bf16[512,1024]{1,0:T(8,128)(2,1)S(1)}, u32[]{:S(2)}, u32[]{:S(2)}) collective-permute-start(bf16[512,1024]{1,0:T(8,128)(2,1)S(1)} %get-tuple-element.148), channel_id=1, source_target_pairs={{0,1},{1,0},{2,3},{3,2},{4,5},{5,4},{6,7},{7,6},{8,9},{9,8},{10,11... | collective-permute-start | bytes 3145736 | tf_op jit(solution)/shard_map/ppermute | solution.py:58
  278.2 139.2 %collective-permute-start.51 = (bf16[64,6912]{1,0:T(8,128)(2,1)}, bf16[64,6912]{1,0:T(8,128)(2,1)}, u32[]{:S(2)}, u32[]{:S(2)}) collective-permute-start(bf16[64,6912]{1,0:T(8,128)(2,1)} %pad_maximum_fusion.7), channel_id=1, source_target_pairs={{0,4},{2,6},{8,0},{10,2},{16,8},{18,10},{24,16},{26,18},{28,24},{3... | collective-permute-start | bytes 2654216 | tf_op jit(solution)/shard_map/ppermute | solution.py:127
  378.7 7.6 %collective-permute-start.32 = (bf16[1,64,1536]{2,1,0:T(8,128)(2,1)}, bf16[1,64,1536]{2,1,0:T(8,128)(2,1)S(1)}, u32[]{:S(2)}, u32[]{:S(2)}) collective-permute-start(bf16[1,64,1536]{2,1,0:T(8,128)(2,1)} %get-tuple-element.118), channel_id=1, source_target_pairs={{0,2},{2,0},{4,6},{6,4},{8,10},{10,8},{12,14},{14,12},{16,18},{18,... | collective-permute-start | bytes 589832 | tf_op jit(solution)/shard_map/ppermute | solution.py:58
  378.9 41.0 %collective-permute-start.47 = (bf16[64,6912]{1,0:T(8,128)(2,1)S(1)}, bf16[64,6912]{1,0:T(8,128)(2,1)S(1)}, u32[]{:S(2)}, u32[]{:S(2)}) collective-permute-start(bf16[64,6912]{1,0:T(8,128)(2,1)S(1)} %pad_maximum_fusion.6), channel_id=1, source_target_pairs={{0,8},{2,10},{8,16},{10,18},{16,24},{18,26},{24,28},{26,30},{28,20... | collective-permute-start | bytes 2654216 | tf_op jit(solution)/shard_map/ppermute | solution.py:127
  386.3 22.3 %collective-permute-start.30 = (bf16[2,64,1536]{2,1,0:T(8,128)(2,1)}, bf16[2,64,1536]{2,1,0:T(8,128)(2,1)S(1)}, u32[]{:S(2)}, u32[]{:S(2)}) collective-permute-start(bf16[2,64,1536]{2,1,0:T(8,128)(2,1)} %get-tuple-element.114), channel_id=1, source_target_pairs={{0,2},{2,0},{4,6},{6,4},{8,10},{10,8},{12,14},{14,12},{16,18},{18,... | collective-permute-start | bytes 1179656 | tf_op jit(solution)/shard_map/ppermute | solution.py:58
  388.0 7.0 %collective-permute-start.37 = (bf16[64,768]{1,0:T(8,128)(2,1)S(1)}, bf16[64,768]{1,0:T(8,128)(2,1)S(1)}, u32[]{:S(2)}, u32[]{:S(2)}) collective-permute-start(bf16[64,768]{1,0:T(8,128)(2,1)S(1)} %get-tuple-element.188), channel_id=1, source_target_pairs={{0,4},{2,6},{8,0},{10,2},{16,8},{18,10},{24,16},{26,18},{28,24},{3... | collective-permute-start | bytes 294920 | tf_op jit(solution)/shard_map/ppermute | solution.py:127
  395.0 12.7 %collective-permute-start.33 = (bf16[64,768]{1,0:T(8,128)(2,1)S(1)}, bf16[64,768]{1,0:T(8,128)(2,1)S(1)}, u32[]{:S(2)}, u32[]{:S(2)}) collective-permute-start(bf16[64,768]{1,0:T(8,128)(2,1)S(1)} %get-tuple-element.187), channel_id=1, source_target_pairs={{0,8},{2,10},{8,16},{10,18},{16,24},{18,26},{24,28},{26,30},{28,20... | collective-permute-start | bytes 294920 | tf_op jit(solution)/shard_map/ppermute | solution.py:127
  407.8 8.6 %collective-permute-start.38 = (bf16[64,1536]{1,0:T(8,128)(2,1)S(1)}, bf16[64,1536]{1,0:T(8,128)(2,1)S(1)}, u32[]{:S(2)}, u32[]{:S(2)}) collective-permute-start(bf16[64,1536]{1,0:T(8,128)(2,1)S(1)} %pad_maximum_fusion.12), channel_id=1, source_target_pairs={{0,4},{2,6},{8,0},{10,2},{16,8},{18,10},{24,16},{26,18},{28,24},{3... | collective-permute-start | bytes 589832 | tf_op jit(solution)/shard_map/ppermute | solution.py:127
  408.6 7.8 %collective-permute-start.34 = (bf16[64,1536]{1,0:T(8,128)(2,1)S(1)}, bf16[64,1536]{1,0:T(8,128)(2,1)S(1)}, u32[]{:S(2)}, u32[]{:S(2)}) collective-permute-start(bf16[64,1536]{1,0:T(8,128)(2,1)S(1)} %pad_maximum_fusion.11), channel_id=1, source_target_pairs={{0,8},{2,10},{8,16},{10,18},{16,24},{18,26},{24,28},{26,30},{28,20... | collective-permute-start | bytes 589832 | tf_op jit(solution)/shard_map/ppermute | solution.py:127
  416.3 52.4 %collective-permute-start.42 = (bf16[2,64,6912]{2,1,0:T(8,128)(2,1)}, bf16[2,64,6912]{2,1,0:T(8,128)(2,1)}, u32[]{:S(2)}, u32[]{:S(2)}) collective-permute-start(bf16[2,64,6912]{2,1,0:T(8,128)(2,1)} %get-tuple-element.126), channel_id=1, source_target_pairs={{0,2},{2,0},{4,6},{6,4},{8,10},{10,8},{12,14},{14,12},{16,18},{18,... | collective-permute-start | bytes 5308424 | tf_op jit(solution)/shard_map/ppermute | solution.py:58
  416.4 7.2 %collective-permute-start.29 = (bf16[2,64,1536]{2,1,0:T(8,128)(2,1)S(1)}, bf16[2,64,1536]{2,1,0:T(8,128)(2,1)S(1)}, u32[]{:S(2)}, u32[]{:S(2)}) collective-permute-start(bf16[2,64,1536]{2,1,0:T(8,128)(2,1)S(1)} %copy-done.82), channel_id=1, source_target_pairs={{0,2},{2,0},{4,6},{6,4},{8,10},{10,8},{12,14},{14,12},{16,18},{18,... | collective-permute-start | bytes 1179656 | tf_op jit(solution)/shard_map/ppermute | solution.py:58
  417.0 25.2 %collective-permute-start.22 = (bf16[512,1024]{1,0:T(8,128)(2,1)S(1)}, bf16[512,1024]{1,0:T(8,128)(2,1)S(1)}, u32[]{:S(2)}, u32[]{:S(2)}) collective-permute-start(bf16[512,1024]{1,0:T(8,128)(2,1)S(1)} %fusion.44), channel_id=1, source_target_pairs={{0,1},{1,0},{2,3},{3,2},{4,5},{5,4},{6,7},{7,6},{8,9},{9,8},{10,11... | collective-permute-start | bytes 3145736 | tf_op jit(solution)/shard_map/ppermute | solution.py:58
  417.4 6.7 %collective-permute-start.35 = (bf16[64,1536]{1,0:T(8,128)(2,1)S(1)}, bf16[64,1536]{1,0:T(8,128)(2,1)S(1)}, u32[]{:S(2)}, u32[]{:S(2)}) collective-permute-start(bf16[64,1536]{1,0:T(8,128)(2,1)S(1)} %get-tuple-element.179), channel_id=1, source_target_pairs={{0,8},{2,10},{8,16},{10,18},{16,24},{18,26},{24,28},{26,30},{28,20... | collective-permute-start | bytes 589832 | tf_op jit(solution)/shard_map/ppermute | solution.py:127
  419.9 6.5 %collective-permute-start.39 = (bf16[64,1536]{1,0:T(8,128)(2,1)S(1)}, bf16[64,1536]{1,0:T(8,128)(2,1)S(1)}, u32[]{:S(2)}, u32[]{:S(2)}) collective-permute-start(bf16[64,1536]{1,0:T(8,128)(2,1)S(1)} %get-tuple-element.180), channel_id=1, source_target_pairs={{0,4},{2,6},{8,0},{10,2},{16,8},{18,10},{24,16},{26,18},{28,24},{3... | collective-permute-start | bytes 589832 | tf_op jit(solution)/shard_map/ppermute | solution.py:127
  423.5 74.0 %collective-permute-start.41 = (bf16[1,64,6912]{2,1,0:T(8,128)(2,1)}, bf16[1,64,6912]{2,1,0:T(8,128)(2,1)}, u32[]{:S(2)}, u32[]{:S(2)}) collective-permute-start(bf16[1,64,6912]{2,1,0:T(8,128)(2,1)} %get-tuple-element.124), channel_id=1, source_target_pairs={{0,2},{2,0},{4,6},{6,4},{8,10},{10,8},{12,14},{14,12},{16,18},{18,... | collective-permute-start | bytes 2654216 | tf_op jit(solution)/shard_map/ppermute | solution.py:58
  424.1 21.6 %collective-permute-start.28 = (bf16[1,64,1536]{2,1,0:T(8,128)(2,1)}, bf16[1,64,1536]{2,1,0:T(8,128)(2,1)S(1)}, u32[]{:S(2)}, u32[]{:S(2)}) collective-permute-start(bf16[1,64,1536]{2,1,0:T(8,128)(2,1)} %get-tuple-element.110), channel_id=1, source_target_pairs={{0,2},{2,0},{4,6},{6,4},{8,10},{10,8},{12,14},{14,12},{16,18},{18,... | collective-permute-start | bytes 589832 | tf_op jit(solution)/shard_map/ppermute | solution.py:58
  427.2 20.8 %collective-permute-start.36 = (bf16[64,1536]{1,0:T(8,128)(2,1)}, bf16[64,1536]{1,0:T(8,128)(2,1)}, u32[]{:S(2)}, u32[]{:S(2)}) collective-permute-start(bf16[64,1536]{1,0:T(8,128)(2,1)} %get-tuple-element.177), channel_id=1, source_target_pairs={{0,8},{2,10},{8,16},{10,18},{16,24},{18,26},{24,28},{26,30},{28,20... | collective-permute-start | bytes 589832 | tf_op jit(solution)/shard_map/ppermute | solution.py:127
  442.2 7.3 %collective-permute-start.40 = (bf16[64,1536]{1,0:T(8,128)(2,1)}, bf16[64,1536]{1,0:T(8,128)(2,1)}, u32[]{:S(2)}, u32[]{:S(2)}) collective-permute-start(bf16[64,1536]{1,0:T(8,128)(2,1)} %get-tuple-element.178), channel_id=1, source_target_pairs={{0,4},{2,6},{8,0},{10,2},{16,8},{18,10},{24,16},{26,18},{28,24},{3... | collective-permute-start | bytes 589832 | tf_op jit(solution)/shard_map/ppermute | solution.py:127
  445.7 23.0 %collective-permute-start.48 = (bf16[64,6912]{1,0:T(8,128)(2,1)}, bf16[64,6912]{1,0:T(8,128)(2,1)S(1)}, u32[]{:S(2)}, u32[]{:S(2)}) collective-permute-start(bf16[64,6912]{1,0:T(8,128)(2,1)} %get-tuple-element.154), channel_id=1, source_target_pairs={{0,8},{2,10},{8,16},{10,18},{16,24},{18,26},{24,28},{26,30},{28,20... | collective-permute-start | bytes 2654216 | tf_op jit(solution)/shard_map/ppermute | solution.py:127
  448.1 20.9 %collective-permute-start.52 = (bf16[64,6912]{1,0:T(8,128)(2,1)}, bf16[64,6912]{1,0:T(8,128)(2,1)S(1)}, u32[]{:S(2)}, u32[]{:S(2)}) collective-permute-start(bf16[64,6912]{1,0:T(8,128)(2,1)} %get-tuple-element.155), channel_id=1, source_target_pairs={{0,4},{2,6},{8,0},{10,2},{16,8},{18,10},{24,16},{26,18},{28,24},{3... | collective-permute-start | bytes 2654216 | tf_op jit(solution)/shard_map/ppermute | solution.py:127
  454.4 14.2 %collective-permute-start.25 = (f32[2176]{0:T(1024)S(1)}, f32[2176]{0:T(1024)S(1)}, u32[]{:S(2)}, u32[]{:S(2)}) collective-permute-start(f32[2176]{0:T(1024)S(1)} %add.412), channel_id=1, source_target_pairs={{0,4},{2,6},{4,0},{6,2},{8,12},{10,14},{12,8},{14,10},{16,20},{18,... | collective-permute-start | bytes 26120 | tf_op jit(solution)/shard_map/ppermute | solution.py:58
  471.1 26.4 %collective-permute-start.49 = (bf16[64,6912]{1,0:T(8,128)(2,1)S(1)}, bf16[64,6912]{1,0:T(8,128)(2,1)S(1)}, u32[]{:S(2)}, u32[]{:S(2)}) collective-permute-start(bf16[64,6912]{1,0:T(8,128)(2,1)S(1)} %get-tuple-element.152), channel_id=1, source_target_pairs={{0,8},{2,10},{8,16},{10,18},{16,24},{18,26},{24,28},{26,30},{28,20... | collective-permute-start | bytes 2654216 | tf_op jit(solution)/shard_map/ppermute | solution.py:127
  473.4 24.2 %collective-permute-start.53 = (bf16[64,6912]{1,0:T(8,128)(2,1)S(1)}, bf16[64,6912]{1,0:T(8,128)(2,1)S(1)}, u32[]{:S(2)}, u32[]{:S(2)}) collective-permute-start(bf16[64,6912]{1,0:T(8,128)(2,1)S(1)} %get-tuple-element.153), channel_id=1, source_target_pairs={{0,4},{2,6},{8,0},{10,2},{16,8},{18,10},{24,16},{26,18},{28,24},{3... | collective-permute-start | bytes 2654216 | tf_op jit(solution)/shard_map/ppermute | solution.py:127
  473.4 22.9 %collective-permute-start.27 = (f32[2176]{0:T(1024)S(1)}, f32[2176]{0:T(1024)S(1)}, u32[]{:S(2)}, u32[]{:S(2)}) collective-permute-start(f32[2176]{0:T(1024)S(1)} %add.414), channel_id=1, source_target_pairs={{0,16},{2,18},{4,20},{6,22},{8,24},{10,26},{12,28},{14,30},{16,0},... | collective-permute-start | bytes 26120 | tf_op jit(solution)/shard_map/ppermute | solution.py:58
  (96 other events, 721.4 us)
Sparse Core Ops, SparseCore 0:
  13.7 121.7 all-gather.1

commit v3 on v2

v3 whole, which is shorter than its diff:
```python
from functools import partial

import jax
import jax.numpy as jnp
from jax import lax
from jax.experimental import pallas as pl
from jax.experimental.pallas import tpu as pltpu
from jax.sharding import PartitionSpec as P

HD = 64

eps = 1e-05
theta_base = 1000000.0
f32 = jnp.float32
bf16 = jnp.bfloat16


def rms_norm(values, gain):
    return values * lax.rsqrt(jnp.mean(values * values, axis=-1, keepdims=True) + eps) * gain


def rotary_tables(length):
    half_size = HD // 2
    frequency = theta_base ** (-jnp.arange(half_size, dtype=f32) * 2.0 / HD)
    angles = frequency[:, None] * jnp.arange(length, dtype=f32)[None, :]
    return (jnp.cos(angles), jnp.sin(angles))


def dot(former, latter):
    return jnp.dot(former, latter, preferred_element_type=f32)


def dot_transposed(former, latter):
    return lax.dot_general(former, latter, (((1,), (1,)), ((), ())), preferred_element_type=f32)


def dot_leading(former, latter):
    return lax.dot_general(former, latter, (((0,), (0,)), ((), ())), preferred_element_type=f32)


def swap(values, axis_name, bit=1):
    count = lax.axis_size(axis_name)
    return lax.ppermute(values, axis_name, [(i, i ^ bit) for i in range(count)])


def widen(rows):
    if lax.axis_size("tp") == 2:
        return (rows, swap(rows, "tp"))
    return (lax.all_gather(rows, "tp", axis=0, tiled=True),)


def narrow(parts):
    if len(parts) == 2:
        return parts[0].astype(f32) + swap(parts[1].astype(bf16), "tp").astype(f32)
    return lax.psum_scatter(
        parts[0].astype(bf16), "tp", scatter_dimension=0, tiled=True
    ).astype(f32)


def sum_everywhere(values):
    count, chips = lax.axis_size("tp"), ring_size()
    terms = [values]
    for step in range(1, count):
        terms.append(lax.ppermute(values, "tp", [(i, (i + step) % count) for i in range(count)]))
    values = sum(terms[1:], terms[0])
    values = values + swap(values, "fsdp")
    return sum([pass_on(values, step) for step in range(1, chips)], values)


def ring_size():
    return lax.axis_size("fsdp") // 2


def chip_at(place):
    chips = ring_size()
    if isinstance(place, int):
        return 2 * place if place < chips // 2 else 2 * (chips - 1 - place) + 1
    return jnp.where(place < chips // 2, 2 * place, 2 * (chips - 1 - place) + 1)


def own_place():
    chip = lax.axis_index("fsdp") // 2
    return jnp.where(chip % 2 == 0, chip // 2, ring_size() - 1 - chip // 2)


def pass_on(values, direction):
    chips = ring_size()
    pairs = [
        (2 * chip_at(place) + core, 2 * chip_at((place + direction) % chips) + core)
        for place in range(chips)
        for core in range(2)
    ]
    return lax.ppermute(values, "fsdp", pairs)


def shard_table(ahead):
    core = lax.axis_index("fsdp") % 2
    chips = chip_at((own_place() + jnp.array(ahead, jnp.int32)) % ring_size())
    return jnp.concatenate([2 * chips + core, 2 * chips + 1 - core]).astype(jnp.int32)


def assemble_body(count, table, *refs):
    whole = refs[count]
    rows = refs[0].shape[0]
    for at in range(count):
        start = pl.multiple_of(table[at] * rows, rows)
        whole[pl.ds(start, rows), :] = refs[at][...]


def gather_ring(shard):
    chips = ring_size()
    ahead = [0]
    blocks = [shard]
    down = up = shard
    for step in range(1, chips // 2 + 1):
        down = pass_on(down, 1)
        ahead.append(chips - step)
        blocks.append(down)
        if step < chips // 2:
            up = pass_on(up, -1)
            ahead.append(step)
            blocks.append(up)
    blocks = blocks + [swap(block, "fsdp") for block in blocks]
    rows, columns = shard.shape
    count = len(blocks)
    vmem = pl.BlockSpec(memory_space=pltpu.VMEM)
    return pl.pallas_call(
        partial(assemble_body, count),
        in_specs=[pl.BlockSpec(memory_space=pltpu.SMEM)] + [vmem] * count,
        out_specs=vmem,
        out_shape=jax.ShapeDtypeStruct((count * rows, columns), shard.dtype),
        compiler_params=pltpu.CompilerParams(vmem_limit_bytes=48 * 1024 * 1024),
        name="assemble",
    )(shard_table(ahead), *blocks)


def ring_groups():
    chips = ring_size()
    middle = [[chips // 2 - step, chips // 2 + step] for step in range(1, chips // 2)]
    return [[chips // 2]] + middle + [[0]]


def anywhere():
    return pl.BlockSpec(memory_space=pl.ANY)


def held(values, after):
    return pl.pallas_call(
        lambda *refs: None,
        in_specs=[anywhere()] * (1 + len(after)),
        out_specs=anywhere(),
        out_shape=jax.ShapeDtypeStruct(values.shape, values.dtype),
        input_output_aliases={0: 0},
        name="held",
    )(values, *after)


def weight_grad_body(parts, groups, rows, extra, *refs):
    table = refs[0]
    first_in = refs[1 : 1 + parts]
    second_in = refs[1 + parts : 1 + 2 * parts]
    first_grads = refs[1 + 2 * parts : 1 + 3 * parts]
    second_grads = refs[1 + 3 * parts : 1 + 4 * parts]
    outs = refs[1 + 4 * parts + extra : -3]
    first_turned, second_turned, total = refs[-3:]
    part_rows = first_in[0].shape[0]
    first_width = first_grads[0].shape[1]

    @pl.when(pl.program_id(0) == 0)
    def _():
        for part in range(parts):
            span = pl.ds(part * part_rows, part_rows)
            first_turned[:, span] = first_in[part][...].T
            second_turned[:, span] = second_in[part][...].T

    def joined(pieces):
        if parts == 1:
            return pieces[0][...]
        return jnp.concatenate([piece[...] for piece in pieces], axis=0)

    total[:, :first_width] = dot(first_turned[...], joined(first_grads)).astype(bf16)
    total[:, first_width:] = dot(second_turned[...], joined(second_grads)).astype(bf16)
    count = sum(len(group) for group in groups)
    at = 0
    for number, group in enumerate(groups):
        for member in range(len(group)):
            mine = pl.multiple_of(table[at] * rows, rows)
            outs[number][member] = total[pl.ds(mine, rows), :]
            near = pl.multiple_of(table[count + at] * rows, rows)
            outs[len(groups) + number][member] = total[pl.ds(near, rows), :]
            at += 1


def weight_grads(first, second, first_grads, second_grads, steps, after, before=()):
    parts = len(first)
    part_rows, model = first[0].shape
    length = parts * part_rows
    first_width = first_grads[0].shape[1] // steps
    second_width = second_grads[0].shape[1] // steps
    width = first_width + second_width
    groups = ring_groups()
    count = 2 * ring_size()
    rows = model // count
    table = shard_table([place for group in groups for place in group])
    whole = pl.BlockSpec((part_rows, model), lambda i: (0, 0))
    outs = [jax.ShapeDtypeStruct((len(group), rows, steps * width), bf16) for group in groups] * 2
    out_specs = [
        pl.BlockSpec((len(group), rows, width), lambda i: (0, 0, i)) for group in groups
    ] * 2
    results = pl.pallas_call(
        partial(weight_grad_body, parts, groups, rows, len(after)),
        grid=(steps,),
        in_specs=[pl.BlockSpec(memory_space=pltpu.SMEM)]
        + [whole] * (2 * parts)
        + [pl.BlockSpec((part_rows, first_width), lambda i: (0, i))] * parts
        + [pl.BlockSpec((part_rows, second_width), lambda i: (0, i))] * parts
        + [anywhere()] * len(after),
        out_specs=out_specs,
        out_shape=outs,
        scratch_shapes=[
            pltpu.VMEM((model, length), bf16),
            pltpu.VMEM((model, length), bf16),
            pltpu.VMEM((model, width), bf16),
        ],
        compiler_params=pltpu.CompilerParams(vmem_limit_bytes=56 * 1024 * 1024),
        cost_estimate=pl.CostEstimate(
            flops=2 * length * model * steps * width,
            bytes_accessed=4 * model * steps * width,
            transcendentals=0,
        ),
        name="weight_grads",
    )(table, *first, *second, *first_grads, *second_grads, *after)
    mine = results[: len(groups)]
    near = list(results[len(groups) :])
    if before:
        near[0] = held(near[0], before)
    near = [swap(block, "fsdp") for block in near]
    return mine, near


def ring_call(body, operands, outs, after, name):
    vmem = pl.BlockSpec(memory_space=pltpu.VMEM)
    return pl.pallas_call(
        body,
        in_specs=[vmem] * len(operands) + [anywhere()] * len(after),
        out_specs=[vmem] * len(outs),
        out_shape=outs,
        compiler_params=pltpu.CompilerParams(vmem_limit_bytes=48 * 1024 * 1024),
        name=name,
    )(*operands, *after)


def both_cores(mine, near, member):
    return mine[member].astype(f32) + near[member].astype(f32)


def open_body(cut, mine, near, *refs):
    low, high = refs[-2:]
    total = both_cores(mine, near, 0).astype(bf16)
    low[...] = total[:, :cut]
    high[...] = total[:, cut:]


def step_body(cut, mine, near, down, up, *refs):
    ahead, behind = refs[-2:]
    columns = ahead.shape[1]
    ahead_sum = both_cores(mine, near, 0)
    behind_sum = both_cores(mine, near, 1)
    if down.shape[1] == columns:
        ahead[...] = (ahead_sum + down[...].astype(f32)).astype(bf16)
        behind[...] = (behind_sum + up[...].astype(f32)).astype(bf16)
    else:
        ahead[:, :cut] = (ahead_sum[:, :cut] + down[...].astype(f32)).astype(bf16)
        ahead[:, cut:] = ahead_sum[:, cut:].astype(bf16)
        behind[:, :cut] = behind_sum[:, :cut].astype(bf16)
        behind[:, cut:] = (behind_sum[:, cut:] + up[...].astype(f32)).astype(bf16)


def close_body(pieces, mine, near, down, up, *outs):
    total = both_cores(mine, near, 0) + down[...].astype(f32) + up[...].astype(f32)
    for start, width, number, place, turn in pieces:
        values = total[:, start : start + width]
        if turn:
            outs[number][place : place + width, :] = values.T
        else:
            outs[number][:, place : place + width] = values


def ring_cut(columns):
    return columns // 2 // 128 * 128


def ring_pass(sums):
    return pass_on(sums[0], 1), pass_on(sums[1], -1)


def ring_open(blocks, after=()):
    mine, near = blocks
    rows, columns = mine[0].shape[1:]
    cut = ring_cut(columns)
    outs = [jax.ShapeDtypeStruct((rows, width), bf16) for width in (cut, columns - cut)]
    sums = ring_call(partial(open_body, cut), (mine[0], near[0]), outs, after, "ring_open")
    return ring_pass(sums), tuple(sums)


def ring_step(blocks, number, state, after=()):
    mine, near = blocks[0][number], blocks[1][number]
    rows, columns = mine.shape[1:]
    outs = [jax.ShapeDtypeStruct((rows, columns), bf16)] * 2
    body = partial(step_body, ring_cut(columns))
    sums = ring_call(body, (mine, near, *state), outs, after, "ring_step")
    return ring_pass(sums), tuple(sums)


def ring_close(blocks, state, pieces):
    mine, near = blocks[0][-1], blocks[1][-1]
    rows = mine.shape[1]
    in_kernel = all(width % 128 == 0 for _, width, _, _, turn in pieces if turn)
    sizes, turns = {}, {}
    for _, width, number, place, turn in pieces:
        sizes[number] = max(sizes.get(number, 0), place + width)
        turns[number] = turn
    if not in_kernel:
        pieces = [piece[:4] + (False,) for piece in pieces]
    outs = [
        jax.ShapeDtypeStruct(
            (sizes[number], rows) if turns[number] and in_kernel else (rows, sizes[number]), f32
        )
        for number in range(len(sizes))
    ]
    results = ring_call(
        partial(close_body, pieces), (mine, near, *state), outs, (), "ring_close"
    )
    return [
        result.T if turns[number] and not in_kernel else result
        for number, result in enumerate(results)
    ]


def ffn_body(width, extra, *refs):
    rows_in, cotangent_in, weights = refs[:3]
    out, grad, pairs, hiddens, out_sum, grad_sum = refs[3 + extra :]
    step = pl.program_id(0)
    length = rows_in.shape[0]

    @pl.when(step == 0)
    def _():
        out_sum[...] = jnp.zeros_like(out_sum)
        grad_sum[...] = jnp.zeros_like(grad_sum)

    pair_weights = weights[:, : 2 * width]
    down = weights[:, 2 * width :]
    chunk = min(256, length)
    for start in range(0, length, chunk):
        span = pl.ds(start, chunk)
        both = dot(rows_in[span, :], pair_weights)
        gate = both[:, :width]
        up = both[:, width:]
        hidden_grad = dot(cotangent_in[span, :], down)
        sigmoid = 1.0 / (1.0 + jnp.exp(-gate))
        silu = gate * sigmoid
        hidden = (silu * up).astype(bf16)
        gate_grad = hidden_grad * up * sigmoid * (1.0 + gate * (1.0 - sigmoid))
        up_grad = hidden_grad * silu
        pair = jnp.concatenate([gate_grad.astype(bf16), up_grad.astype(bf16)], axis=1)
        hiddens[span, :] = hidden
        pairs[span, :] = pair
        out_sum[span, :] += dot_transposed(hidden, down)
        grad_sum[span, :] += dot_transposed(pair, pair_weights)

    @pl.when(step == pl.num_programs(0) - 1)
    def _():
        out[...] = out_sum[...].astype(out.dtype)
        grad[...] = grad_sum[...].astype(grad.dtype)


def hidden_width(units):
    for width in (256, 384, 128):
        if units % width == 0:
            return width
    return units


def feed_forward(rows, cotangent, weights, width, kind, after):
    length, model = rows.shape
    steps = weights.shape[1] // (3 * width)
    whole = pl.BlockSpec((length, model), lambda i: (0, 0))
    sums = jax.ShapeDtypeStruct((length, model), kind)
    return pl.pallas_call(
        partial(ffn_body, width, len(after)),
        grid=(steps,),
        in_specs=[whole, whole, pl.BlockSpec((model, 3 * width), lambda i: (0, i))]
        + [anywhere()] * len(after),
        out_specs=[
            whole,
            whole,
            pl.BlockSpec((length, 2 * width), lambda i: (0, i)),
            pl.BlockSpec((length, width), lambda i: (0, i)),
        ],
        out_shape=[
            sums,
            sums,
            jax.ShapeDtypeStruct((length, steps * 2 * width), bf16),
            jax.ShapeDtypeStruct((length, steps * width), bf16),
        ],
        scratch_shapes=[
            pltpu.VMEM((length, model), f32),
            pltpu.VMEM((length, model), f32),
        ],
        compiler_params=pltpu.CompilerParams(vmem_limit_bytes=56 * 1024 * 1024),
        cost_estimate=pl.CostEstimate(
            flops=12 * length * model * steps * width,
            bytes_accessed=8 * model * steps * width,
            transcendentals=length * steps * width,
        ),
        name="feed_forward",
    )(rows, cotangent, weights, *after)


def lines(start, size):
    if isinstance(start, int):
        return pl.ds(start, size)
    return pl.ds(pl.multiple_of(start, size), size)


def part_starts(place, count, part_rows):
    if count == 1:
        return [0]
    return [place[0] * part_rows, (1 - place[0]) * part_rows]


def causal_block(size):
    keys = lax.broadcasted_iota(jnp.int32, (size, size), 0)
    queries = lax.broadcasted_iota(jnp.int32, (size, size), 1)
    return keys <= queries


def attend_body(count, *refs):
    place, weights, query_gain, key_gain, cosine, sine = refs[:6]
    rows_in = refs[6 : 6 + count]
    branches = refs[6 + count : 6 + 2 * count]
    attended_out = refs[6 + 2 * count : 6 + 3 * count]
    raw, query_rows, key_rows, value_rows, attended, log_totals = refs[6 + 3 * count : 12 + 3 * count]
    rows, turned = refs[12 + 3 * count :]
    part_rows = rows_in[0].shape[0]
    length = rows.shape[0]
    heads = query_rows.shape[0] // HD
    kv_heads = key_rows.shape[0] // HD
    group_size = heads // kv_heads
    columns = (heads + 2 * kv_heads) * HD
    half = HD // 2
    starts = part_starts(place, count, part_rows)
    for part in range(count):
        rows[lines(starts[part], part_rows), :] = rows_in[part][...]

    chunk = min(256, columns)
    for first in range(0, columns, chunk):
        product = dot_transposed(weights[:, first : first + chunk].T, rows[...])
        for at in range(0, chunk, HD):
            head = (first + at) // HD
            values = product[at : at + HD]
            if head >= heads + kv_heads:
                start = (head - heads - kv_heads) * HD
                value_rows[start : start + HD, :] = values.astype(bf16)
                continue
            raw[first + at : first + at + HD, :] = values
            gain = query_gain if head < heads else key_gain
            scale = lax.rsqrt(jnp.mean(values * values, axis=0, keepdims=True) + eps)
            normed = values * scale * gain[...]
            top, bottom = normed[:half], normed[half:]
            top, bottom = (
                top * cosine[...] - bottom * sine[...],
                bottom * cosine[...] + top * sine[...],
            )
            if head < heads:
                target, start = query_rows, head * HD
                top = top.astype(bf16).astype(f32) * HD**-0.5
                bottom = bottom.astype(bf16).astype(f32) * HD**-0.5
            else:
                target, start = key_rows, (head - heads) * HD
            target[start : start + half, :] = top.astype(bf16)
            target[start + half : start + HD, :] = bottom.astype(bf16)

    block = min(256, length)
    causal = causal_block(block)

    def one_group(kv_head, carry):
        span = lines(kv_head * HD, HD)
        keys = key_rows[span, :].T
        values = value_rows[span, :]
        for member in range(group_size):
            head = kv_head * group_size + member
            for start in range(0, length, block):
                here = slice(start, start + block)
                query = query_rows[lines(head * HD, HD), here]
                weight = jnp.where(causal, jnp.exp(dot(keys[here], query)), 0.0)
                total = jnp.sum(weight, axis=0, keepdims=True)
                result = dot(values[:, here], weight.astype(bf16))
                if start:
                    weight = jnp.exp(dot(keys[:start], query))
                    total = total + jnp.sum(weight, axis=0, keepdims=True)
                    result = result + dot(values[:, :start], weight.astype(bf16))
                attended[lines(head * HD, HD), here] = (result * (1.0 / total)).astype(bf16)
                log_totals[head, :, here] = jnp.log(total)
        return carry

    lax.fori_loop(0, kv_heads, one_group, 0)
    turned[...] = attended[...].T
    for part in range(count):
        mine = turned[lines(starts[part], part_rows), :]
        attended_out[part][...] = mine
        branches[part][...] = dot_transposed(mine, weights[:, columns:]).astype(branches[part].dtype)


def attend(place, weights, query_gain, key_gain, cosine, sine, parts, query_columns, key_columns):
    count = len(parts)
    part_rows, model = parts[0].shape
    length = count * part_rows
    heads = query_columns // HD
    shape = jax.ShapeDtypeStruct
    kinds = [f32] + [bf16] * (count - 1)
    vmem = pl.BlockSpec(memory_space=pltpu.VMEM)
    outs = (
        [shape((part_rows, model), kind) for kind in kinds]
        + [shape((part_rows, query_columns), bf16)] * count
        + [
            shape((query_columns + key_columns, length), f32),
            shape((query_columns, length), bf16),
            shape((key_columns, length), bf16),
            shape((key_columns, length), bf16),
            shape((query_columns, length), bf16),
            shape((heads, 1, length), f32),
        ]
    )
    results = pl.pallas_call(
        partial(attend_body, count),
        in_specs=[pl.BlockSpec(memory_space=pltpu.SMEM)] + [vmem] * (5 + count),
        out_specs=[vmem] * len(outs),
        out_shape=outs,
        scratch_shapes=[
            pltpu.VMEM((length, model), bf16),
            pltpu.VMEM((length, query_columns), bf16),
        ],
        compiler_params=pltpu.CompilerParams(vmem_limit_bytes=56 * 1024 * 1024),
        cost_estimate=pl.CostEstimate(
            flops=2 * length * model * (2 * query_columns + 2 * key_columns)
            + 8 * length * length * query_columns,
            bytes_accessed=16 * length * model,
            transcendentals=heads * length * length,
        ),
        name="attend",
    )(place, weights, query_gain, key_gain, cosine, sine, *parts)
    return results[:count], results[count : 2 * count], results[2 * count :]


def attend_back_body(count, stage, stages, extra, *refs):
    place, weights, query_gain, key_gain, cosine, sine = refs[:6]
    raw, query_rows, key_rows, value_rows, attended, log_totals = refs[6:12]
    branch_in = refs[12 : 12 + count]
    refs = refs[12 + count :]
    if stage:
        earlier = refs[:3]
        refs = refs[3:]
    refs = refs[extra:]
    last = stage == stages - 1
    if last:
        grads, raw_grads, refs = refs[:count], refs[count : 2 * count], refs[2 * count :]
        query_gain_grad, key_gain_grad, turned_grads = refs[:3]
        rows, attended_grad, key_sum, value_sum, straight = refs[3:]
    else:
        turned_grads, query_gain_grad, key_gain_grad = refs[:3]
        rows, attended_grad, key_sum, value_sum = refs[3:]
    part_rows = branch_in[0].shape[0]
    length = rows.shape[0]
    heads = query_rows.shape[0] // HD
    kv_heads = key_rows.shape[0] // HD
    group_size = heads // kv_heads
    columns = (heads + 2 * kv_heads) * HD
    half = HD // 2
    starts = part_starts(place, count, part_rows)
    for part in range(count):
        rows[lines(starts[part], part_rows), :] = branch_in[part][...]
    groups_here = kv_heads // stages
    stage_rows = groups_here * group_size * HD
    chunk = min(256, stage_rows)
    for first in range(stage * stage_rows, (stage + 1) * stage_rows, chunk):
        piece = weights[:, columns + first : columns + first + chunk].T
        attended_grad[first : first + chunk, :] = dot_transposed(piece, rows[...]).astype(bf16)
    if stage:
        turned_grads[...] = earlier[0][...]
        query_gain_grad[...] = earlier[1][...]
        key_gain_grad[...] = earlier[2][...]
    else:
        turned_grads[...] = jnp.zeros_like(turned_grads)
        query_gain_grad[...] = jnp.zeros_like(query_gain_grad)
        key_gain_grad[...] = jnp.zeros_like(key_gain_grad)
    block = min(256, length)
    causal = causal_block(block)

    def unprepare(grad, values, gain, gain_grad):
        top, bottom = grad[:half], grad[half:]
        grad = jnp.concatenate(
            [
                top * cosine[...] + bottom * sine[...],
                bottom * cosine[...] - top * sine[...],
            ],
            axis=0,
        )
        scale = lax.rsqrt(jnp.mean(values * values, axis=0, keepdims=True) + eps)
        normed = values * scale
        gain_grad[...] += jnp.sum(grad * normed, axis=1, keepdims=True)
        grad = grad * gain[...]
        inner = jnp.mean(grad * normed, axis=0, keepdims=True)
        return (scale * (grad - normed * inner)).astype(bf16)

    def one_group(kv_head, carry):
        span = lines(kv_head * HD, HD)
        keys_turned = key_rows[span, :]
        keys = keys_turned.T
        values = value_rows[span, :].T
        key_sum[...] = jnp.zeros_like(key_sum)
        value_sum[...] = jnp.zeros_like(value_sum)
        for member in range(group_size):
            head = kv_head * group_size + member
            head_span = lines(head * HD, HD)
            query_parts = []
            for start in range(0, length, block):
                here = slice(start, start + block)
                query = query_rows[head_span, here]
                grad = attended_grad[head_span, here]
                inner = jnp.sum(
                    grad.astype(f32) * attended[head_span, here].astype(f32), axis=0, keepdims=True
                )
                log_total = log_totals[head, :, here]
                query_grad = None
                for low, high in [(start, start + block)] + ([(0, start)] if start else []):
                    prob = jnp.exp(dot(keys[low:high], query) - log_total)
                    if low == start:
                        prob = jnp.where(causal, prob, 0.0)
                    prob_grad = dot(values[low:high], grad)
                    score_grad = (prob * (prob_grad - inner)).astype(bf16)
                    piece = dot(keys_turned[:, low:high], score_grad)
                    query_grad = piece if query_grad is None else query_grad + piece
                    key_sum[:, low:high] += dot_transposed(query, score_grad)
                    value_sum[:, low:high] += dot_transposed(grad, prob.astype(bf16))
                query_parts.append(query_grad * HD**-0.5)
            turned_grads[head_span, :] = unprepare(
                jnp.concatenate(query_parts, axis=1), raw[head_span, :], query_gain, query_gain_grad
            )
        key_span = lines((heads + kv_head) * HD, HD)
        turned_grads[key_span, :] = unprepare(
            key_sum[...], raw[key_span, :], key_gain, key_gain_grad
        )
        turned_grads[lines((heads + kv_heads + kv_head) * HD, HD), :] = value_sum[...].astype(bf16)
        return carry

    lax.fori_loop(stage * groups_here, (stage + 1) * groups_here, one_group, 0)
    if last:
        straight[...] = turned_grads[...].T
        for part in range(count):
            mine = straight[lines(starts[part], part_rows), :]
            raw_grads[part][...] = mine
            grads[part][...] = dot_transposed(mine, weights[:, :columns]).astype(grads[part].dtype)


def back_stages(kept):
    return 2 if kept[2].shape[0] // HD % 2 == 0 else 1


def attend_back(fixed, kept, parts, stage, earlier, after):
    count = len(parts)
    stages = back_stages(kept)
    part_rows, model = parts[0].shape
    length = count * part_rows
    query_columns = kept[1].shape[0]
    columns = query_columns + 2 * kept[2].shape[0]
    shape = jax.ShapeDtypeStruct
    vmem = pl.BlockSpec(memory_space=pltpu.VMEM)
    last = stage == stages - 1
    gains = [shape((HD, 1), f32)] * 2
    turned = shape((columns, length), bf16)
    scratch = [
        pltpu.VMEM((length, model), bf16),
        pltpu.VMEM((query_columns, length), bf16),
        pltpu.VMEM((HD, length), f32),
        pltpu.VMEM((HD, length), f32),
    ]
    if last:
        outs = (
            [shape((part_rows, model), kind) for kind in [f32] + [bf16] * (count - 1)]
            + [shape((part_rows, columns), bf16)] * count
            + gains
        )
        scratch = [pltpu.VMEM(turned.shape, bf16)] + scratch + [pltpu.VMEM((length, columns), bf16)]
    else:
        outs = [turned] + gains
    results = pl.pallas_call(
        partial(attend_back_body, count, stage, stages, len(after)),
        in_specs=[pl.BlockSpec(memory_space=pltpu.SMEM)]
        + [vmem] * (11 + count + len(earlier))
        + [anywhere()] * len(after),
        out_specs=[vmem] * len(outs),
        out_shape=outs,
        scratch_shapes=scratch,
        compiler_params=pltpu.CompilerParams(vmem_limit_bytes=56 * 1024 * 1024),
        cost_estimate=pl.CostEstimate(
            flops=(
                2 * length * model * (query_columns + columns)
                + 20 * length * length * query_columns
            )
            // stages,
            bytes_accessed=16 * length * model,
            transcendentals=query_columns // HD * length * length // stages,
        ),
        name="attend_back",
    )(*fixed, *kept, *parts, *earlier, *after)
    if not last:
        return results
    return results[:count], results[count : 2 * count], results[2 * count], results[2 * count + 1]


def on_device(
    tokens,
    out_cotangent,
    attn_gain,
    query_weight,
    key_weight,
    value_weight,
    query_gain,
    key_gain,
    out_weight,
    ffn_gain,
    gate_weight,
    up_weight,
    down_weight,
):
    shard, query_columns = query_weight.shape
    key_columns = key_weight.shape[1]
    qkv_columns = query_columns + 2 * key_columns
    units = gate_weight.shape[1]
    width = hidden_width(units)
    steps = units // width
    attn_shard = jnp.concatenate([query_weight, key_weight, value_weight, out_weight.T], axis=1)
    ffn_shard = jnp.stack(
        [
            gate_weight.reshape(shard, steps, width),
            up_weight.reshape(shard, steps, width),
            down_weight.T.reshape(shard, steps, width),
        ],
        axis=2,
    ).reshape(shard, 3 * units)
    attn_full = gather_ring(attn_shard)
    ffn_full = lax.all_gather(ffn_shard, "fsdp", axis=0, tiled=True)

    residual = tokens.astype(f32)
    normed, attn_norm_pull = jax.vjp(rms_norm, residual, attn_gain)
    normed_parts = widen(normed.astype(bf16))
    cotangent_parts = widen(out_cotangent)
    length = len(normed_parts) * normed_parts[0].shape[0]
    cosine, sine = rotary_tables(length)
    place = lax.axis_index("tp").astype(jnp.int32).reshape(1)
    fixed = (place, attn_full, query_gain[:, None], key_gain[:, None], cosine, sine)
    branch, attended, kept = attend(*fixed, normed_parts, query_columns, key_columns)
    middle = residual + narrow(branch)
    normed_ffn, ffn_norm_pull = jax.vjp(rms_norm, middle, ffn_gain)
    ffn_parts = widen(normed_ffn.astype(bf16))
    results = []
    for at in reversed(range(len(ffn_parts))):
        after = [results[-1][1]] if results else []
        results.append(
            feed_forward(
                ffn_parts[at], cotangent_parts[at], ffn_full, width, bf16 if at else f32, after
            )
        )
    out_parts, grad_parts, pairs, hiddens = (list(item) for item in zip(*results[::-1]))
    ffn_normed_grad = narrow(grad_parts)
    middle_piece, ffn_gain_local = ffn_norm_pull(ffn_normed_grad)
    middle_grad = out_cotangent.astype(f32) + middle_piece
    branch_parts = widen(middle_grad.astype(bf16))

    ffn_blocks = weight_grads(
        ffn_parts,
        cotangent_parts,
        pairs,
        hiddens,
        steps,
        (branch_parts[0],),
        branch_parts[1:],
    )
    ffn_state, sent = ring_open(ffn_blocks)
    ffn_next, attn_next, last = 1, 1, ring_size() // 2
    stages = back_stages(kept)
    back = ()
    for stage in range(stages):
        back = attend_back(fixed, kept, branch_parts, stage, back, sent)
        done = back[1] if stage < stages - 1 else back[2]
        if stage == 0:
            out_parts[-1] = held(out_parts[-1], (done,))
        if ffn_next < last:
            ffn_state, sent = ring_step(ffn_blocks, ffn_next, ffn_state, (done,))
            ffn_next += 1
    output = (middle + narrow(out_parts)).astype(bf16)
    normed_grad, qkv_grad, query_gain_local, key_gain_local = back
    normed_grad = narrow([*normed_grad[:-1], held(normed_grad[-1], sent)])
    attn_blocks = weight_grads(normed_parts, branch_parts, qkv_grad, attended, 1, sent)
    attn_state, sent = ring_open(attn_blocks)
    while ffn_next < last or attn_next < last:
        if attn_next < last:
            attn_state, sent = ring_step(attn_blocks, attn_next, attn_state, sent)
            attn_next += 1
        if ffn_next < last:
            ffn_state, sent = ring_step(ffn_blocks, ffn_next, ffn_state, sent)
            ffn_next += 1
    ffn_pieces = [
        (step * 3 * width + number * width, width, number, step * width, number == 2)
        for step in range(steps)
        for number in range(3)
    ]
    gate_grad, up_grad, down_grad = ring_close(ffn_blocks, ffn_state, ffn_pieces)
    attn_pieces = [
        (0, query_columns, 0, 0, False),
        (query_columns, key_columns, 1, 0, False),
        (query_columns + key_columns, key_columns, 2, 0, False),
        (qkv_columns, query_columns, 3, 0, True),
    ]
    query_grad, key_grad, value_grad, out_grad = ring_close(attn_blocks, attn_state, attn_pieces)
    tokens_piece, attn_gain_local = attn_norm_pull(normed_grad)
    tokens_grad = middle_grad + tokens_piece
    model = attn_gain.shape[0]
    gain_totals = sum_everywhere(
        jnp.concatenate([attn_gain_local, ffn_gain_local, query_gain_local[:, 0], key_gain_local[:, 0]])
    )
    return (
        output,
        tokens_grad,
        gain_totals[:model],
        query_grad,
        key_grad,
        value_grad,
        gain_totals[2 * model : 2 * model + HD],
        gain_totals[2 * model + HD :],
        out_grad,
        gain_totals[model : 2 * model],
        gate_grad,
        up_grad,
        down_grad,
    )


def solution(mesh):
    placed = (
        P(("fsdp", "tp"), None),
        P(("fsdp", "tp"), None),
        P(),
        P("fsdp", "tp"),
        P("fsdp", "tp"),
        P("fsdp", "tp"),
        P(),
        P(),
        P("tp", "fsdp"),
        P(),
        P("fsdp", "tp"),
        P("fsdp", "tp"),
        P("tp", "fsdp"),
    )
    return jax.shard_map(
        on_device,
        mesh=mesh,
        in_specs=placed,
        out_specs=(
            P(("fsdp", "tp"), None),
            P(("fsdp", "tp"), None),
            P(),
            P("fsdp", "tp"),
            P("fsdp", "tp"),
            P("fsdp", "tp"),
            P(),
            P(),
            P("tp", "fsdp"),
            P(),
            P("fsdp", "tp"),
            P("fsdp", "tp"),
            P("tp", "fsdp"),
        ),
        check_vma=False,
    )
```

time: 523 us -> 440 us (0.84)
  matrix products: 67.5 us -> 0 us
  Pallas kernels: 79.8 us -> 145 us
  other arithmetic: 65.2 us -> 22.6 us
  local copies, waits for them, and re-layouts: 39.9 us -> 24.8 us
  waiting for transfers between devices: 179 us -> 166 us
  starting transfers between devices: 71.5 us -> 59.8 us
    dot_general x18 -> x0, matrix products: 67.5 us -> none  [the longest x2 11.6 us: attend_back(): jnp.einsum('kgqs,qkgd->skd', probability.astype(bf16), grad_block, prefer...]
    pallas_call x4 -> x20, Pallas kernels: 77.5 us -> 143 us  [the longest x2 45.7 us: feed_forward(): pl.pallas_call(partial(ffn_body, width, len(after)), grid=(steps,), in_sp...]
    ppermute x31 -> x27, waiting for transfers between devices: 131 us -> 73.1 us  [swap(): return lax.ppermute(values, axis_name, [(i, i ^ bit) for i in range(count)])]
    ppermute x23 -> x30, waiting for transfers between devices: 44.7 us -> 90.2 us  [pass_on(): return lax.ppermute(values, 'fsdp', pairs)]
    convert_element_type x14 -> x3, other arithmetic: 26.1 us -> 6.52 us  [the longest x1 4.19 us: on_device(): output = (middle + narrow(out_parts)).astype(bf16)]
    slice x14 -> x0, local copies, waits for them, and re-layouts: 9.92 us -> none  [the longest x1 4.72 us: on_device(): ffn_grads[:, :, at].reshape(shard, units)]
    reduce_sum x2 -> x0, other arithmetic: 9.36 us -> none  [attend(): row_total = jnp.sum(exponent, axis=-1, keepdims=True)]
    concatenate x10 -> x0, other arithmetic: 9 us -> none  [the longest x2 2.95 us: in_order(): jnp.concatenate([jnp.where(first, parts[0], parts[1]), jnp.where(first, p...]
  transfers between devices with their start and end apart: 55 -> 59, of which waited for: 26 -> 22; matrix products, arithmetic and copies ran while one was open for 28% -> 5% of each run, Pallas kernels for 7% -> 27%
where the time goes in v3:
time: 440 us; the launch traced here: 433 us
  waiting for transfers between devices  166 us (38%)
  Pallas kernels  145 us (33%)
  starting transfers between devices  59.8 us (14%)
  local copies, waits for them, and re-layouts  24.8 us (6%)
  other arithmetic  22.6 us (5%)
  between operations  15 us (3%)
    ppermute x30, waiting for transfers between devices, pass_on(): return lax.ppermute(values, 'fsdp', pairs)  90.2 us
    ppermute x27, waiting for transfers between devices, swap(): return lax.ppermute(values, axis_name, [(i, i ^ bit) for i in range(count)])  73.1 us
    ppermute x30, starting transfers between devices, pass_on(): return lax.ppermute(values, 'fsdp', pairs)  47.4 us
    pallas_call x2, Pallas kernels, feed_forward(): pl.pallas_call(partial(ffn_body, width, len(after)), grid=(steps,), in_sp...  45.7 us
    pallas_call x2, Pallas kernels, attend_back(): pl.pallas_call(partial(attend_back_body, count, stage, stages, len(after)...  36.4 us
    pallas_call x2, Pallas kernels, weight_grads(): pl.pallas_call(partial(weight_grad_body, parts, groups, rows, len(after))...  31.4 us
    pallas_call x1, Pallas kernels, attend(): pl.pallas_call(partial(attend_body, count), in_specs=[pl.BlockSpec(memory...  18.2 us
    unnamed x120, local copies, waits for them, and re-layouts  15.3 us
  transfers between devices with their start and end apart: 59, of which 22 were waited for; matrix products, arithmetic and copies ran while one was open for 5% of the time, Pallas kernels for 27%

profile of v3, /device:TPU:0, one launch (start us, length us, event | category | flops | bytes accessed | tf_op | source)
XLA Modules:
  0.0 433.1 jit_solution(15136153376796339112)
XLA Ops:
  11.8 1.8 reshape.79
  13.7 3.1 collective-permute-start
  21.6 1.8 collective-permute-start.2
  23.4 2.9 collective-permute-done.1.refs_2_
  26.8 2.9 collective-permute-done.2.refs_3_
  29.7 3.4 collective-permute-start.4
  33.1 8.9 %collective-permute-done.3.refs_4_ = bf16[64,1536]{1,0:T(8,128)(2,1)S(1)} collective-permute-done((bf16[64,1536]{1,0:T(8,128)(2,1)S(1)}, bf16[64,1536]{1,0:T(8,128)(2,1)S(1)}, u32[]{:S(2)}, u32[]{:S(2)}) %collective-permute-start.3) | collective-permute-done | bytes 196640 | tf_op jit(solution)/shard_map/ppermute | solution.py:93
  42.2 6.0 %collective-permute-start.6 = (bf16[64,1536]{1,0:T(8,128)(2,1)S(1)}, bf16[64,1536]{1,0:T(8,128)(2,1)S(1)}, u32[]{:S(2)}, u32[]{:S(2)}) collective-permute-start(bf16[64,1536]{1,0:T(8,128)(2,1)S(1)} %collective-permute-done.4.refs_5_), channel_id=1, source_target_pairs={{0,8},{2,10},{8,16},{10,18},{16,24},{18,26},{24,28},{26,30},{28,20... | collective-permute-start | bytes 589832 | tf_op jit(solution)/shard_map/ppermute | solution.py:93
  48.9 9.5 %collective-permute-done.5.refs_6_ = bf16[64,1536]{1,0:T(8,128)(2,1)S(1)} collective-permute-done((bf16[64,1536]{1,0:T(8,128)(2,1)S(1)}, bf16[64,1536]{1,0:T(8,128)(2,1)S(1)}, u32[]{:S(2)}, u32[]{:S(2)}) %collective-permute-start.5) | collective-permute-done | bytes 196640 | tf_op jit(solution)/shard_map/ppermute | solution.py:93
  60.1 2.5 assemble.1.refs_1_
  62.6 18.2 %attend.1 = (f32[512,1024]{1,0:T(8,128)}, bf16[512,1024]{1,0:T(8,128)(2,1)}, bf16[512,512]{1,0:T(8,128)(2,1)}, bf16[512,512]{1,0:T(8,128)(2,1)}, f32[768,1024]{1...) custom-call(s32[1]{0:T(128)} %bitcast.refs_0_, ...), custom_call_target="tpu_custom_call" | custom-call | flops 7516192768 | bytes 16777216 | tf_op jit(solution)/shard_map/attend/pallas_call | solution.py:535
  82.9 24.2 %collective-permute-done.16 = bf16[512,1024]{1,0:T(8,128)(2,1)S(1)} collective-permute-done((bf16[512,1024]{1,0:T(8,128)(2,1)}, bf16[512,1024]{1,0:T(8,128)(2,1)S(1)}, u32[]{:S(2)}, u32[]{:S(2)}) %collective-permute-start.16) | collective-permute-done | bytes 1048608 | tf_op jit(solution)/shard_map/ppermute | solution.py:43
  107.1 2.1 multiply_reduce_fusion.2
  111.0 18.6 %collective-permute-done.18.refs_1_.refs_4_ = bf16[512,1024]{1,0:T(8,128)(2,1)S(1)} collective-permute-done((bf16[512,1024]{1,0:T(8,128)(2,1)S(1)}, bf16[512,1024]{1,0:T(8,128)(2,1)S(1)}, u32[]{:S(2)}, u32[]{:S(2)}) %collective-permute-start.18) | collective-permute-done | bytes 1048608 | tf_op jit(solution)/shard_map/ppermute | solution.py:43
  130.5 20.8 %collective-permute-done.17.refs_0_.refs_2_ = bf16[512,1024]{1,0:T(8,128)(2,1)} collective-permute-done((bf16[512,1024]{1,0:T(8,128)(2,1)S(1)}, bf16[512,1024]{1,0:T(8,128)(2,1)}, u32[]{:S(2)}, u32[]{:S(2)}) %collective-permute-start.17) | collective-permute-done | bytes 1048608 | tf_op jit(solution)/shard_map/ppermute | solution.py:43
  151.4 22.5 %feed_forward.2 = (bf16[512,1024]{1,0:T(8,128)(2,1)}, bf16[512,1024]{1,0:T(8,128)(2,1)}, bf16[512,4608]{1,0:T(8,128)(2,1)}, bf16[512,2304]{1,0:T(8,128)(2,1)}) custom-call(bf16[512,1024]{1,0:T(8,128)(2,1)} %collective-permute-done.17.refs_0_.refs_2_, bf16[512,1024]{1,0:T(8,128)(2,1)} %copy-done.56, bf16[1024,6912]{1,0:T(8,128)(2,1)} %all-gather.2.cloned.1.call-done.refs_2_), custom_call_target="tpu_custom_call" | custom-call | flops 14495514624 | bytes 18874368 | tf_op jit(solution)/shard_map/feed_forward/pallas_call | solution.py:389
  174.7 23.2 %feed_forward.3 = (f32[512,1024]{1,0:T(8,128)}, f32[512,1024]{1,0:T(8,128)}, bf16[512,4608]{1,0:T(8,128)(2,1)}, bf16[512,2304]{1,0:T(8,128)(2,1)}) custom-call(bf16[512,1024]{1,0:T(8,128)(2,1)} %copy-done.36, bf16[512,1024]{1,0:T(8,128)(2,1)} %refs_3_.1, bf16[1024,6912]{1,0:T(8,128)(2,1)} %all-gather.2.cloned.1.call-done.refs_2_, ...), custom_call_target="tpu_custom_call" | custom-call | flops 14495514624 | bytes 18874368 | tf_op jit(solution)/shard_map/feed_forward/pallas_call | solution.py:389
  198.5 3.0 multiply_reduce_fusion
  201.5 2.0 fusion.17
  204.5 23.1 %weight_grads.2 = (bf16[1,64,6912]{2,1,0:T(8,128)(2,1)}, bf16[2,64,6912]{2,1,0:T(8,128)(2,1)}, bf16[2,64,6912]{2,1,0:T(8,128)(2,1)}, bf16[2,64,6912]{2,1,0:T(8,1...) custom-call(s32[16]{0:T(128)} %pad_add_fusion.1.refs_0_, ...), custom_call_target="tpu_custom_call" | custom-call | flops 14495514624 | bytes 28311552 | tf_op jit(solution)/shard_map/weight_grads/pallas_call | solution.py:210
  228.3 5.8 %collective-permute-done.21.near = bf16[1,64,6912]{2,1,0:T(8,128)(2,1)S(1)} collective-permute-done((bf16[1,64,6912]{2,1,0:T(8,128)(2,1)}, bf16[1,64,6912]{2,1,0:T(8,128)(2,1)S(1)}, u32[]{:S(2)}, u32[]{:S(2)}) %collective-permute-start.21) | collective-permute-done | bytes 884768 | tf_op jit(solution)/shard_map/ppermute | solution.py:43
  234.4 5.1 %collective-permute-start.24 = (bf16[64,3456]{1,0:T(8,128)(2,1)S(1)}, bf16[64,3456]{1,0:T(8,128)(2,1)S(1)}, u32[]{:S(2)}, u32[]{:S(2)}) collective-permute-start(bf16[64,3456]{1,0:T(8,128)(2,1)S(1)} %get-tuple-element.101.refs_14_), channel_id=1, source_target_pairs={{0,8},{2,10},{8,16},{10,18},{16,24},{18,26},{24,28},{26,30},{28,20... | collective-permute-start | bytes 1327112 | tf_op jit(solution)/shard_map/ppermute | solution.py:93
  239.5 16.1 %attend_back.2 = (bf16[1024,1024]{1,0:T(8,128)(2,1)}, f32[64,1]{1,0:T(8,128)}, f32[64,1]{1,0:T(8,128)}) custom-call(s32[1]{0:T(128)} %bitcast.refs_0_, bf16[1024,1536]{1,0:T(8,128)(2,1)} %assemble.1.refs_1_, f32[64,1]{1,0:T(8,128)} %copy.43.refs_2_, f32[64,1]{1,0:T(8,128)} %copy.44.refs_3_, f32[32,1024]{1,0:T(8,128)} %get-tuple-element.196.refs_4_, ...), custom_call_target="tpu_custom_call" | custom-call | flops 6979321856 | bytes 16777216 | tf_op jit(solution)/shard_map/attend_back/pallas_call | solution.py:697
  257.0 4.3 collective-permute-start.27
  261.3 20.4 %attend_back.3 = (f32[512,1024]{1,0:T(8,128)}, bf16[512,1024]{1,0:T(8,128)(2,1)}, bf16[512,1024]{1,0:T(8,128)(2,1)}, bf16[512,1024]{1,0:T(8,128)(2,1)}, f32[64,1]{1,0:T(8,128)}, /*index=5*/f32[64,1]{1,0:T(8,128)}) custom-call(s32[1]{0:T(128)} %bitcast.refs_0_, bf16[1024,1536]{1,0:T(8,128)(2,1)} %assemble.1.refs_1_, f32[64,1]{1,0:T(8,128)} %copy.43.refs_2_, ...), custom_call_target="tpu_custom_call" | custom-call | flops 6979321856 | bytes 16777216 | tf_op jit(solution)/shard_map/attend_back/pallas_call | solution.py:697
  283.1 2.1 ring_step.7
  289.2 8.3 %weight_grads.3 = (bf16[1,64,1536]{2,1,0:T(8,128)(2,1)}, bf16[2,64,1536]{2,1,0:T(8,128)(2,1)}, bf16[2,64,1536]{2,1,0:T(8,128)(2,1)}, bf16[2,64,1536]{2,1,0:T(8,1...) custom-call(s32[16]{0:T(128)} %pad_add_fusion.1.refs_0_, ...), custom_call_target="tpu_custom_call" | custom-call | flops 3221225472 | bytes 6291456 | tf_op jit(solution)/shard_map/weight_grads/pallas_call | solution.py:210
  297.8 1.7 collective-permute-start.49
  304.6 17.1 %collective-permute-done.44.down = bf16[64,768]{1,0:T(8,128)(2,1)S(1)} collective-permute-done((bf16[64,768]{1,0:T(8,128)(2,1)S(1)}, bf16[64,768]{1,0:T(8,128)(2,1)S(1)}, u32[]{:S(2)}, u32[]{:S(2)}) %collective-permute-start.44) | collective-permute-done | bytes 98336 | tf_op jit(solution)/shard_map/ppermute | solution.py:93
  322.7 3.7 fusion.3
  327.1 18.6 %collective-permute-done.45.up = bf16[64,768]{1,0:T(8,128)(2,1)} collective-permute-done((bf16[64,768]{1,0:T(8,128)(2,1)}, bf16[64,768]{1,0:T(8,128)(2,1)}, u32[]{:S(2)}, u32[]{:S(2)}) %collective-permute-start.45) | collective-permute-done | bytes 98336 | tf_op jit(solution)/shard_map/ppermute | solution.py:93
  346.8 2.6 collective-permute-done.30
  349.4 1.9 collective-permute-done.42.near
  357.4 1.8 collective-permute-start.46
  359.9 4.2 add_convert_fusion
  364.1 3.2 ring_step.9
  368.7 4.2 collective-permute-start.36
  372.9 3.7 collective-permute-start.34
  377.3 2.0 collective-permute-done.35
  379.3 2.0 collective-permute-start.57
  382.9 3.3 fusion.5
  386.1 14.6 %collective-permute-done.32 = f32[2176]{0:T(1024)S(1)} collective-permute-done((f32[2176]{0:T(1024)S(1)}, f32[2176]{0:T(1024)S(1)}, u32[]{:S(2)}, u32[]{:S(2)}) %collective-permute-start.32) | collective-permute-done | bytes 8736 | tf_op jit(solution)/shard_map/ppermute | solution.py:93
  401.1 5.8 %collective-permute-done.51.down = bf16[64,1536]{1,0:T(8,128)(2,1)S(1)} collective-permute-done((bf16[64,1536]{1,0:T(8,128)(2,1)S(1)}, bf16[64,1536]{1,0:T(8,128)(2,1)S(1)}, u32[]{:S(2)}, u32[]{:S(2)}) %collective-permute-start.51) | collective-permute-done | bytes 196640 | tf_op jit(solution)/shard_map/ppermute | solution.py:93
  406.9 1.7 collective-permute-start.52
  409.2 3.3 collective-permute-done.52.up
  412.8 2.0 collective-permute-start.54
  415.3 3.1 collective-permute-done.53.down
  422.2 2.7 ring_close.3
  (249 shorter events, 52.4 us)
Async XLA Ops:
  7.2 144.2 %all-gather.2.cloned.1.call-start = ((), (), s32[]{:S(2)}) async-start(), calls=%async_computation | async-start | bytes 15040512 | tf_op jit(solution)/shard_map/all_gather | solution.py:753
  13.7 7.9 %collective-permute-start = (bf16[64,1536]{1,0:T(8,128)(2,1)S(1)}, bf16[64,1536]{1,0:T(8,128)(2,1)S(1)}, u32[]{:S(2)}, u32[]{:S(2)}) collective-permute-start(bf16[64,1536]{1,0:T(8,128)(2,1)S(1)} %pad_maximum_fusion.1.refs_0_), channel_id=1, source_target_pairs={{0,8},{2,10},{8,16},{10,18},{16,24},{18,26},{24,28},{26,30},{28,20... | collective-permute-start | bytes 589832 | tf_op jit(solution)/shard_map/ppermute | solution.py:93
  17.4 45.2 %collective-permute-start.15 = (bf16[512,1024]{1,0:T(8,128)(2,1)S(1)}, bf16[512,1024]{1,0:T(8,128)(2,1)}, u32[]{:S(2)}, u32[]{:S(2)}) collective-permute-start(bf16[512,1024]{1,0:T(8,128)(2,1)S(1)} %fusion.2.refs_6_.refs_1_), channel_id=1, source_target_pairs={{0,1},{1,0},{2,3},{3,2},{4,5},{5,4},{6,7},{7,6},{8,9},{9,8},{10,11... | collective-permute-start | bytes 3145736 | tf_op jit(solution)/shard_map/ppermute | solution.py:43
  19.0 14.1 %collective-permute-start.7 = (bf16[64,1536]{1,0:T(8,128)(2,1)S(1)}, bf16[64,1536]{1,0:T(8,128)(2,1)S(1)}, u32[]{:S(2)}, u32[]{:S(2)}) collective-permute-start(bf16[64,1536]{1,0:T(8,128)(2,1)S(1)} %pad_maximum_fusion.1.refs_0_), channel_id=1, source_target_pairs={{0,2},{2,0},{4,6},{6,4},{8,10},{10,8},{12,14},{14,12},{16,18},{18,... | collective-permute-start | bytes 589832 | tf_op jit(solution)/shard_map/ppermute | solution.py:43
  19.0 7.3 %collective-permute-start.1 = (bf16[64,1536]{1,0:T(8,128)(2,1)S(1)}, bf16[64,1536]{1,0:T(8,128)(2,1)S(1)}, u32[]{:S(2)}, u32[]{:S(2)}) collective-permute-start(bf16[64,1536]{1,0:T(8,128)(2,1)S(1)} %pad_maximum_fusion.1.refs_0_), channel_id=1, source_target_pairs={{0,4},{2,6},{8,0},{10,2},{16,8},{18,10},{24,16},{26,18},{28,24},{3... | collective-permute-start | bytes 589832 | tf_op jit(solution)/shard_map/ppermute | solution.py:93
  21.6 8.1 %collective-permute-start.2 = (bf16[64,1536]{1,0:T(8,128)(2,1)S(1)}, bf16[64,1536]{1,0:T(8,128)(2,1)S(1)}, u32[]{:S(2)}, u32[]{:S(2)}) collective-permute-start(bf16[64,1536]{1,0:T(8,128)(2,1)S(1)} %collective-permute-done.refs_1_), channel_id=1, source_target_pairs={{0,8},{2,10},{8,16},{10,18},{16,24},{18,26},{24,28},{26,30},{28,20... | collective-permute-start | bytes 589832 | tf_op jit(solution)/shard_map/ppermute | solution.py:93
  26.3 15.9 %collective-permute-start.9 = (bf16[64,1536]{1,0:T(8,128)(2,1)S(1)}, bf16[64,1536]{1,0:T(8,128)(2,1)S(1)}, u32[]{:S(2)}, u32[]{:S(2)}) collective-permute-start(bf16[64,1536]{1,0:T(8,128)(2,1)S(1)} %collective-permute-done.1.refs_2_), channel_id=1, source_target_pairs={{0,2},{2,0},{4,6},{6,4},{8,10},{10,8},{12,14},{14,12},{16,18},{18,... | collective-permute-start | bytes 589832 | tf_op jit(solution)/shard_map/ppermute | solution.py:43
  26.3 15.7 %collective-permute-start.3 = (bf16[64,1536]{1,0:T(8,128)(2,1)S(1)}, bf16[64,1536]{1,0:T(8,128)(2,1)S(1)}, u32[]{:S(2)}, u32[]{:S(2)}) collective-permute-start(bf16[64,1536]{1,0:T(8,128)(2,1)S(1)} %collective-permute-done.1.refs_2_), channel_id=1, source_target_pairs={{0,4},{2,6},{8,0},{10,2},{16,8},{18,10},{24,16},{26,18},{28,24},{3... | collective-permute-start | bytes 589832 | tf_op jit(solution)/shard_map/ppermute | solution.py:93
  29.7 12.5 %collective-permute-start.4 = (bf16[64,1536]{1,0:T(8,128)(2,1)S(1)}, bf16[64,1536]{1,0:T(8,128)(2,1)S(1)}, u32[]{:S(2)}, u32[]{:S(2)}) collective-permute-start(bf16[64,1536]{1,0:T(8,128)(2,1)S(1)} %collective-permute-done.2.refs_3_), channel_id=1, source_target_pairs={{0,8},{2,10},{8,16},{10,18},{16,24},{18,26},{24,28},{26,30},{28,20... | collective-permute-start | bytes 589832 | tf_op jit(solution)/shard_map/ppermute | solution.py:93
  33.1 15.3 %collective-permute-start.8 = (bf16[64,1536]{1,0:T(8,128)(2,1)S(1)}, bf16[64,1536]{1,0:T(8,128)(2,1)S(1)}, u32[]{:S(2)}, u32[]{:S(2)}) collective-permute-start(bf16[64,1536]{1,0:T(8,128)(2,1)S(1)} %collective-permute-done.refs_1_), channel_id=1, source_target_pairs={{0,2},{2,0},{4,6},{6,4},{8,10},{10,8},{12,14},{14,12},{16,18},{18,... | collective-permute-start | bytes 589832 | tf_op jit(solution)/shard_map/ppermute | solution.py:43
  42.0 6.4 %collective-permute-start.11 = (bf16[64,1536]{1,0:T(8,128)(2,1)S(1)}, bf16[64,1536]{1,0:T(8,128)(2,1)S(1)}, u32[]{:S(2)}, u32[]{:S(2)}) collective-permute-start(bf16[64,1536]{1,0:T(8,128)(2,1)S(1)} %collective-permute-done.3.refs_4_), channel_id=1, source_target_pairs={{0,2},{2,0},{4,6},{6,4},{8,10},{10,8},{12,14},{14,12},{16,18},{18,... | collective-permute-start | bytes 589832 | tf_op jit(solution)/shard_map/ppermute | solution.py:43
  42.2 16.1 %collective-permute-start.5 = (bf16[64,1536]{1,0:T(8,128)(2,1)S(1)}, bf16[64,1536]{1,0:T(8,128)(2,1)S(1)}, u32[]{:S(2)}, u32[]{:S(2)}) collective-permute-start(bf16[64,1536]{1,0:T(8,128)(2,1)S(1)} %collective-permute-done.3.refs_4_), channel_id=1, source_target_pairs={{0,4},{2,6},{8,0},{10,2},{16,8},{18,10},{24,16},{26,18},{28,24},{3... | collective-permute-start | bytes 589832 | tf_op jit(solution)/shard_map/ppermute | solution.py:93
  42.2 16.3 %collective-permute-start.6 = (bf16[64,1536]{1,0:T(8,128)(2,1)S(1)}, bf16[64,1536]{1,0:T(8,128)(2,1)S(1)}, u32[]{:S(2)}, u32[]{:S(2)}) collective-permute-start(bf16[64,1536]{1,0:T(8,128)(2,1)S(1)} %collective-permute-done.4.refs_5_), channel_id=1, source_target_pairs={{0,8},{2,10},{8,16},{10,18},{16,24},{18,26},{24,28},{26,30},{28,20... | collective-permute-start | bytes 589832 | tf_op jit(solution)/shard_map/ppermute | solution.py:93
  48.3 11.8 %collective-permute-start.10 = (bf16[64,1536]{1,0:T(8,128)(2,1)S(1)}, bf16[64,1536]{1,0:T(8,128)(2,1)S(1)}, u32[]{:S(2)}, u32[]{:S(2)}) collective-permute-start(bf16[64,1536]{1,0:T(8,128)(2,1)S(1)} %collective-permute-done.2.refs_3_), channel_id=1, source_target_pairs={{0,2},{2,0},{4,6},{6,4},{8,10},{10,8},{12,14},{14,12},{16,18},{18,... | collective-permute-start | bytes 589832 | tf_op jit(solution)/shard_map/ppermute | solution.py:43
  48.4 11.7 %collective-permute-start.12 = (bf16[64,1536]{1,0:T(8,128)(2,1)S(1)}, bf16[64,1536]{1,0:T(8,128)(2,1)S(1)}, u32[]{:S(2)}, u32[]{:S(2)}) collective-permute-start(bf16[64,1536]{1,0:T(8,128)(2,1)S(1)} %collective-permute-done.4.refs_5_), channel_id=1, source_target_pairs={{0,2},{2,0},{4,6},{6,4},{8,10},{10,8},{12,14},{14,12},{16,18},{18,... | collective-permute-start | bytes 589832 | tf_op jit(solution)/shard_map/ppermute | solution.py:43
  80.8 26.3 %collective-permute-start.16 = (bf16[512,1024]{1,0:T(8,128)(2,1)}, bf16[512,1024]{1,0:T(8,128)(2,1)S(1)}, u32[]{:S(2)}, u32[]{:S(2)}) collective-permute-start(bf16[512,1024]{1,0:T(8,128)(2,1)} %get-tuple-element.84), channel_id=1, source_target_pairs={{0,1},{1,0},{2,3},{3,2},{4,5},{5,4},{6,7},{7,6},{8,9},{9,8},{10,11... | collective-permute-start | bytes 3145736 | tf_op jit(solution)/shard_map/ppermute | solution.py:43
  81.7 47.9 %collective-permute-start.18 = (bf16[512,1024]{1,0:T(8,128)(2,1)S(1)}, bf16[512,1024]{1,0:T(8,128)(2,1)S(1)}, u32[]{:S(2)}, u32[]{:S(2)}) collective-permute-start(bf16[512,1024]{1,0:T(8,128)(2,1)S(1)} %copy-done.37), channel_id=1, source_target_pairs={{0,1},{1,0},{2,3},{3,2},{4,5},{5,4},{6,7},{7,6},{8,9},{9,8},{10,11... | collective-permute-start | bytes 3145736 | tf_op jit(solution)/shard_map/ppermute | solution.py:43
  109.5 41.9 %collective-permute-start.17 = (bf16[512,1024]{1,0:T(8,128)(2,1)S(1)}, bf16[512,1024]{1,0:T(8,128)(2,1)}, u32[]{:S(2)}, u32[]{:S(2)}) collective-permute-start(bf16[512,1024]{1,0:T(8,128)(2,1)S(1)} %multiply_convert_fusion.refs_0_.refs_1_), channel_id=1, source_target_pairs={{0,1},{1,0},{2,3},{3,2},{4,5},{5,4},{6,7},{7,6},{8,9},{9,8},{10,11... | collective-permute-start | bytes 3145736 | tf_op jit(solution)/shard_map/ppermute | solution.py:43
  173.8 24.7 %collective-permute-start.19 = (bf16[512,1024]{1,0:T(8,128)(2,1)}, bf16[512,1024]{1,0:T(8,128)(2,1)S(1)}, u32[]{:S(2)}, u32[]{:S(2)}) collective-permute-start(bf16[512,1024]{1,0:T(8,128)(2,1)} %get-tuple-element.85.refs_3_), channel_id=1, source_target_pairs={{0,1},{1,0},{2,3},{3,2},{4,5},{5,4},{6,7},{7,6},{8,9},{9,8},{10,11... | collective-permute-start | bytes 3145736 | tf_op jit(solution)/shard_map/ppermute | solution.py:43
  203.6 24.2 %collective-permute-start.20 = (bf16[512,1024]{1,0:T(8,128)(2,1)S(1)}, bf16[512,1024]{1,0:T(8,128)(2,1)}, u32[]{:S(2)}, u32[]{:S(2)}) collective-permute-start(bf16[512,1024]{1,0:T(8,128)(2,1)S(1)} %get-tuple-element.185.refs_9_.refs_12_.refs_3_), channel_id=1, source_target_pairs={{0,1},{1,0},{2,3},{3,2},{4,5},{5,4},{6,7},{7,6},{8,9},{9,8},{10,11... | collective-permute-start | bytes 3145736 | tf_op jit(solution)/shard_map/ppermute | solution.py:43
  227.7 28.0 %collective-permute-start.23 = (bf16[2,64,6912]{2,1,0:T(8,128)(2,1)}, bf16[2,64,6912]{2,1,0:T(8,128)(2,1)S(1)}, u32[]{:S(2)}, u32[]{:S(2)}) collective-permute-start(bf16[2,64,6912]{2,1,0:T(8,128)(2,1)} %get-tuple-element.107), channel_id=1, source_target_pairs={{0,2},{2,0},{4,6},{6,4},{8,10},{10,8},{12,14},{14,12},{16,18},{18,... | collective-permute-start | bytes 5308424 | tf_op jit(solution)/shard_map/ppermute | solution.py:43
  227.8 6.4 %collective-permute-start.21 = (bf16[1,64,6912]{2,1,0:T(8,128)(2,1)}, bf16[1,64,6912]{2,1,0:T(8,128)(2,1)S(1)}, u32[]{:S(2)}, u32[]{:S(2)}) collective-permute-start(bf16[1,64,6912]{2,1,0:T(8,128)(2,1)} %held.3), channel_id=1, source_target_pairs={{0,2},{2,0},{4,6},{6,4},{8,10},{10,8},{12,14},{14,12},{16,18},{18,... | collective-permute-start | bytes 2654216 | tf_op jit(solution)/shard_map/ppermute | solution.py:43
  228.3 53.4 %collective-permute-start.26 = (bf16[2,64,6912]{2,1,0:T(8,128)(2,1)}, bf16[2,64,6912]{2,1,0:T(8,128)(2,1)}, u32[]{:S(2)}, u32[]{:S(2)}) collective-permute-start(bf16[2,64,6912]{2,1,0:T(8,128)(2,1)} %get-tuple-element.113), channel_id=1, source_target_pairs={{0,2},{2,0},{4,6},{6,4},{8,10},{10,8},{12,14},{14,12},{16,18},{18,... | collective-permute-start | bytes 5308424 | tf_op jit(solution)/shard_map/ppermute | solution.py:43
  234.4 21.2 %collective-permute-start.24 = (bf16[64,3456]{1,0:T(8,128)(2,1)S(1)}, bf16[64,3456]{1,0:T(8,128)(2,1)S(1)}, u32[]{:S(2)}, u32[]{:S(2)}) collective-permute-start(bf16[64,3456]{1,0:T(8,128)(2,1)S(1)} %get-tuple-element.101.refs_14_), channel_id=1, source_target_pairs={{0,8},{2,10},{8,16},{10,18},{16,24},{18,26},{24,28},{26,30},{28,20... | collective-permute-start | bytes 1327112 | tf_op jit(solution)/shard_map/ppermute | solution.py:93
  239.5 16.1 %collective-permute-start.25 = (bf16[64,3456]{1,0:T(8,128)(2,1)S(1)}, bf16[64,3456]{1,0:T(8,128)(2,1)S(1)}, u32[]{:S(2)}, u32[]{:S(2)}) collective-permute-start(bf16[64,3456]{1,0:T(8,128)(2,1)S(1)} %get-tuple-element.102.refs_15_), channel_id=1, source_target_pairs={{0,4},{2,6},{8,0},{10,2},{16,8},{18,10},{24,16},{26,18},{28,24},{3... | collective-permute-start | bytes 1327112 | tf_op jit(solution)/shard_map/ppermute | solution.py:93
  257.0 24.7 %collective-permute-start.27 = (bf16[64,6912]{1,0:T(8,128)(2,1)S(1)}, bf16[64,6912]{1,0:T(8,128)(2,1)S(1)}, u32[]{:S(2)}, u32[]{:S(2)}) collective-permute-start(bf16[64,6912]{1,0:T(8,128)(2,1)S(1)} %get-tuple-element.108.refs_17_), channel_id=1, source_target_pairs={{0,8},{2,10},{8,16},{10,18},{16,24},{18,26},{24,28},{26,30},{28,20... | collective-permute-start | bytes 2654216 | tf_op jit(solution)/shard_map/ppermute | solution.py:93
  261.2 21.1 %collective-permute-start.28 = (bf16[64,6912]{1,0:T(8,128)(2,1)S(1)}, bf16[64,6912]{1,0:T(8,128)(2,1)S(1)}, u32[]{:S(2)}, u32[]{:S(2)}) collective-permute-start(bf16[64,6912]{1,0:T(8,128)(2,1)S(1)} %get-tuple-element.109.refs_18_), channel_id=1, source_target_pairs={{0,4},{2,6},{8,0},{10,2},{16,8},{18,10},{24,16},{26,18},{28,24},{3... | collective-permute-start | bytes 2654216 | tf_op jit(solution)/shard_map/ppermute | solution.py:93
  287.2 35.5 %collective-permute-start.29 = (bf16[512,1024]{1,0:T(8,128)(2,1)}, bf16[512,1024]{1,0:T(8,128)(2,1)}, u32[]{:S(2)}, u32[]{:S(2)}) collective-permute-start(bf16[512,1024]{1,0:T(8,128)(2,1)} %held.5), channel_id=1, source_target_pairs={{0,1},{1,0},{2,3},{3,2},{4,5},{5,4},{6,7},{7,6},{8,9},{9,8},{10,11... | collective-permute-start | bytes 3145736 | tf_op jit(solution)/shard_map/ppermute | solution.py:43
  288.2 69.2 %collective-permute-start.48 = (bf16[2,64,6912]{2,1,0:T(8,128)(2,1)}, bf16[2,64,6912]{2,1,0:T(8,128)(2,1)}, u32[]{:S(2)}, u32[]{:S(2)}) collective-permute-start(bf16[2,64,6912]{2,1,0:T(8,128)(2,1)} %get-tuple-element.137), channel_id=1, source_target_pairs={{0,2},{2,0},{4,6},{6,4},{8,10},{10,8},{12,14},{14,12},{16,18},{18,... | collective-permute-start | bytes 5308424 | tf_op jit(solution)/shard_map/ppermute | solution.py:43
  288.2 70.9 %collective-permute-start.22 = (bf16[512,1024]{1,0:T(8,128)(2,1)}, bf16[512,1024]{1,0:T(8,128)(2,1)}, u32[]{:S(2)}, u32[]{:S(2)}) collective-permute-start(bf16[512,1024]{1,0:T(8,128)(2,1)} %held.4), channel_id=1, source_target_pairs={{0,1},{1,0},{2,3},{3,2},{4,5},{5,4},{6,7},{7,6},{8,9},{9,8},{10,11... | collective-permute-start | bytes 3145736 | tf_op jit(solution)/shard_map/ppermute | solution.py:43
  297.8 61.7 %collective-permute-start.49 = (bf16[64,6912]{1,0:T(8,128)(2,1)S(1)}, bf16[64,6912]{1,0:T(8,128)(2,1)S(1)}, u32[]{:S(2)}, u32[]{:S(2)}) collective-permute-start(bf16[64,6912]{1,0:T(8,128)(2,1)S(1)} %copy-done.10), channel_id=1, source_target_pairs={{0,8},{2,10},{8,16},{10,18},{16,24},{18,26},{24,28},{26,30},{28,20... | collective-permute-start | bytes 2654216 | tf_op jit(solution)/shard_map/ppermute | solution.py:93
  301.1 20.6 %collective-permute-start.44 = (bf16[64,768]{1,0:T(8,128)(2,1)S(1)}, bf16[64,768]{1,0:T(8,128)(2,1)S(1)}, u32[]{:S(2)}, u32[]{:S(2)}) collective-permute-start(bf16[64,768]{1,0:T(8,128)(2,1)S(1)} %get-tuple-element.132.refs_0_), channel_id=1, source_target_pairs={{0,8},{2,10},{8,16},{10,18},{16,24},{18,26},{24,28},{26,30},{28,20... | collective-permute-start | bytes 294920 | tf_op jit(solution)/shard_map/ppermute | solution.py:93
  322.4 41.7 %collective-permute-start.50 = (bf16[64,6912]{1,0:T(8,128)(2,1)S(1)}, bf16[64,6912]{1,0:T(8,128)(2,1)S(1)}, u32[]{:S(2)}, u32[]{:S(2)}) collective-permute-start(bf16[64,6912]{1,0:T(8,128)(2,1)S(1)} %copy-done.8), channel_id=1, source_target_pairs={{0,4},{2,6},{8,0},{10,2},{16,8},{18,10},{24,16},{26,18},{28,24},{3... | collective-permute-start | bytes 2654216 | tf_op jit(solution)/shard_map/ppermute | solution.py:93
  322.6 23.1 %collective-permute-start.45 = (bf16[64,768]{1,0:T(8,128)(2,1)}, bf16[64,768]{1,0:T(8,128)(2,1)}, u32[]{:S(2)}, u32[]{:S(2)}) collective-permute-start(bf16[64,768]{1,0:T(8,128)(2,1)} %copy-done.21), channel_id=1, source_target_pairs={{0,4},{2,6},{8,0},{10,2},{16,8},{18,10},{24,16},{26,18},{28,24},{3... | collective-permute-start | bytes 294920 | tf_op jit(solution)/shard_map/ppermute | solution.py:93
  352.5 14.8 %collective-permute-start.41 = (bf16[2,64,1536]{2,1,0:T(8,128)(2,1)}, bf16[2,64,1536]{2,1,0:T(8,128)(2,1)S(1)}, u32[]{:S(2)}, u32[]{:S(2)}) collective-permute-start(bf16[2,64,1536]{2,1,0:T(8,128)(2,1)} %get-tuple-element.127), channel_id=1, source_target_pairs={{0,2},{2,0},{4,6},{6,4},{8,10},{10,8},{12,14},{14,12},{16,18},{18,... | collective-permute-start | bytes 1179656 | tf_op jit(solution)/shard_map/ppermute | solution.py:43
  357.4 10.0 %collective-permute-start.46 = (bf16[64,1536]{1,0:T(8,128)(2,1)S(1)}, bf16[64,1536]{1,0:T(8,128)(2,1)S(1)}, u32[]{:S(2)}, u32[]{:S(2)}) collective-permute-start(bf16[64,1536]{1,0:T(8,128)(2,1)S(1)} %get-tuple-element.134.refs_0_), channel_id=1, source_target_pairs={{0,8},{2,10},{8,16},{10,18},{16,24},{18,26},{24,28},{26,30},{28,20... | collective-permute-start | bytes 589832 | tf_op jit(solution)/shard_map/ppermute | solution.py:93
  359.2 8.2 %collective-permute-start.47 = (bf16[64,1536]{1,0:T(8,128)(2,1)S(1)}, bf16[64,1536]{1,0:T(8,128)(2,1)S(1)}, u32[]{:S(2)}, u32[]{:S(2)}) collective-permute-start(bf16[64,1536]{1,0:T(8,128)(2,1)S(1)} %get-tuple-element.135.refs_1_), channel_id=1, source_target_pairs={{0,4},{2,6},{8,0},{10,2},{16,8},{18,10},{24,16},{26,18},{28,24},{3... | collective-permute-start | bytes 589832 | tf_op jit(solution)/shard_map/ppermute | solution.py:93
  359.5 17.2 %collective-permute-start.38 = (f32[2176]{0:T(1024)S(1)}, f32[2176]{0:T(1024)S(1)}, u32[]{:S(2)}, u32[]{:S(2)}) collective-permute-start(f32[2176]{0:T(1024)S(1)} %add.169), channel_id=1, source_target_pairs={{0,4},{2,6},{8,0},{10,2},{16,8},{18,10},{24,16},{26,18},{28,24},{3... | collective-permute-start | bytes 26120 | tf_op jit(solution)/shard_map/ppermute | solution.py:93
  367.5 9.2 %collective-permute-start.37 = (f32[2176]{0:T(1024)S(1)}, f32[2176]{0:T(1024)S(1)}, u32[]{:S(2)}, u32[]{:S(2)}) collective-permute-start(f32[2176]{0:T(1024)S(1)} %add.169), channel_id=1, source_target_pairs={{0,12},{2,14},{8,4},{10,6},{16,0},{18,2},{24,8},{26,10},{28,16},{3... | collective-permute-start | bytes 26120 | tf_op jit(solution)/shard_map/ppermute | solution.py:93
  368.7 8.1 %collective-permute-start.36 = (f32[2176]{0:T(1024)S(1)}, f32[2176]{0:T(1024)S(1)}, u32[]{:S(2)}, u32[]{:S(2)}) collective-permute-start(f32[2176]{0:T(1024)S(1)} %add.169), channel_id=1, source_target_pairs={{0,20},{2,22},{8,12},{10,14},{16,4},{18,6},{24,0},{26,2},{28,8},{3... | collective-permute-start | bytes 26120 | tf_op jit(solution)/shard_map/ppermute | solution.py:93
  372.9 6.4 %collective-permute-start.35 = (f32[2176]{0:T(1024)S(1)}, f32[2176]{0:T(1024)S(1)}, u32[]{:S(2)}, u32[]{:S(2)}) collective-permute-start(f32[2176]{0:T(1024)S(1)} %add.169), channel_id=1, source_target_pairs={{0,28},{2,30},{8,20},{10,22},{16,12},{18,14},{24,4},{26,6},{28,0},... | collective-permute-start | bytes 26120 | tf_op jit(solution)/shard_map/ppermute | solution.py:93
  372.9 6.4 %collective-permute-start.34 = (f32[2176]{0:T(1024)S(1)}, f32[2176]{0:T(1024)S(1)}, u32[]{:S(2)}, u32[]{:S(2)}) collective-permute-start(f32[2176]{0:T(1024)S(1)} %add.169), channel_id=1, source_target_pairs={{0,24},{2,26},{8,28},{10,30},{16,20},{18,22},{24,12},{26,14},{28,4... | collective-permute-start | bytes 26120 | tf_op jit(solution)/shard_map/ppermute | solution.py:93
  376.7 43.3 %collective-permute-start.55 = (bf16[1,64,6912]{2,1,0:T(8,128)(2,1)}, bf16[1,64,6912]{2,1,0:T(8,128)(2,1)S(1)}, u32[]{:S(2)}, u32[]{:S(2)}) collective-permute-start(bf16[1,64,6912]{2,1,0:T(8,128)(2,1)} %get-tuple-element.149), channel_id=1, source_target_pairs={{0,2},{2,0},{4,6},{6,4},{8,10},{10,8},{12,14},{14,12},{16,18},{18,... | collective-permute-start | bytes 2654216 | tf_op jit(solution)/shard_map/ppermute | solution.py:43
  376.8 24.2 %collective-permute-start.40 = (bf16[2,64,1536]{2,1,0:T(8,128)(2,1)S(1)}, bf16[2,64,1536]{2,1,0:T(8,128)(2,1)S(1)}, u32[]{:S(2)}, u32[]{:S(2)}) collective-permute-start(bf16[2,64,1536]{2,1,0:T(8,128)(2,1)S(1)} %copy-done.57), channel_id=1, source_target_pairs={{0,2},{2,0},{4,6},{6,4},{8,10},{10,8},{12,14},{14,12},{16,18},{18,... | collective-permute-start | bytes 1179656 | tf_op jit(solution)/shard_map/ppermute | solution.py:43
  379.3 40.7 %collective-permute-start.56 = (bf16[64,6912]{1,0:T(8,128)(2,1)}, bf16[64,6912]{1,0:T(8,128)(2,1)S(1)}, u32[]{:S(2)}, u32[]{:S(2)}) collective-permute-start(bf16[64,6912]{1,0:T(8,128)(2,1)} %get-tuple-element.138.refs_0_), channel_id=1, source_target_pairs={{0,8},{2,10},{8,16},{10,18},{16,24},{18,26},{24,28},{26,30},{28,20... | collective-permute-start | bytes 2654216 | tf_op jit(solution)/shard_map/ppermute | solution.py:93
  379.3 41.7 %collective-permute-start.57 = (bf16[64,6912]{1,0:T(8,128)(2,1)}, bf16[64,6912]{1,0:T(8,128)(2,1)}, u32[]{:S(2)}, u32[]{:S(2)}) collective-permute-start(bf16[64,6912]{1,0:T(8,128)(2,1)} %get-tuple-element.139.refs_1_), channel_id=1, source_target_pairs={{0,4},{2,6},{8,0},{10,2},{16,8},{18,10},{24,16},{26,18},{28,24},{3... | collective-permute-start | bytes 2654216 | tf_op jit(solution)/shard_map/ppermute | solution.py:93
  381.4 19.3 %collective-permute-start.32 = (f32[2176]{0:T(1024)S(1)}, f32[2176]{0:T(1024)S(1)}, u32[]{:S(2)}, u32[]{:S(2)}) collective-permute-start(f32[2176]{0:T(1024)S(1)} %add.169), channel_id=1, source_target_pairs={{0,8},{2,10},{8,16},{10,18},{16,24},{18,26},{24,28},{26,30},{28,20... | collective-permute-start | bytes 26120 | tf_op jit(solution)/shard_map/ppermute | solution.py:93
  401.0 11.7 %collective-permute-start.39 = (bf16[1,64,1536]{2,1,0:T(8,128)(2,1)S(1)}, bf16[1,64,1536]{2,1,0:T(8,128)(2,1)S(1)}, u32[]{:S(2)}, u32[]{:S(2)}) collective-permute-start(bf16[1,64,1536]{2,1,0:T(8,128)(2,1)S(1)} %copy-done.58), channel_id=1, source_target_pairs={{0,2},{2,0},{4,6},{6,4},{8,10},{10,8},{12,14},{14,12},{16,18},{18,... | collective-permute-start | bytes 589832 | tf_op jit(solution)/shard_map/ppermute | solution.py:43
  (70 other events, 1040.3 us)
Sparse Core Ops, SparseCore 0:
  13.8 121.7 all-gather.1

commit v4 on v3

--- a/solution.py
+++ b/solution.py
@@ -49,9 +49,13 @@
     return (lax.all_gather(rows, "tp", axis=0, tiled=True),)
 
 
+def narrow_send(part):
+    return swap(part.astype(bf16), "tp")
+
+
 def narrow(parts):
     if len(parts) == 2:
-        return parts[0].astype(f32) + swap(parts[1].astype(bf16), "tp").astype(f32)
+        return parts[0].astype(f32) + narrow_send(parts[1]).astype(f32)
     return lax.psum_scatter(
         parts[0].astype(bf16), "tp", scatter_dimension=0, tiled=True
     ).astype(f32)
@@ -375,7 +379,7 @@
 
 
 def hidden_width(units):
-    for width in (256, 384, 128):
+    for width in (768, 256, 384, 128):
         if units % width == 0:
             return width
     return units
@@ -553,16 +557,16 @@
     return results[:count], results[count : 2 * count], results[2 * count :]
 
 
-def attend_back_body(count, stage, stages, extra, *refs):
+def attend_back_body(count, first_group, last_group, extra, *refs):
     place, weights, query_gain, key_gain, cosine, sine = refs[:6]
     raw, query_rows, key_rows, value_rows, attended, log_totals = refs[6:12]
     branch_in = refs[12 : 12 + count]
     refs = refs[12 + count :]
-    if stage:
+    if first_group:
         earlier = refs[:3]
         refs = refs[3:]
     refs = refs[extra:]
-    last = stage == stages - 1
+    last = last_group * HD == key_rows.shape[0]
     if last:
         grads, raw_grads, refs = refs[:count], refs[count : 2 * count], refs[2 * count :]
         query_gain_grad, key_gain_grad, turned_grads = refs[:3]
@@ -580,13 +584,13 @@
     starts = part_starts(place, count, part_rows)
     for part in range(count):
         rows[lines(starts[part], part_rows), :] = branch_in[part][...]
-    groups_here = kv_heads // stages
-    stage_rows = groups_here * group_size * HD
+    stage_rows = (last_group - first_group) * group_size * HD
     chunk = min(256, stage_rows)
-    for first in range(stage * stage_rows, (stage + 1) * stage_rows, chunk):
+    begin = first_group * group_size * HD
+    for first in range(begin, begin + stage_rows, chunk):
         piece = weights[:, columns + first : columns + first + chunk].T
         attended_grad[first : first + chunk, :] = dot_transposed(piece, rows[...]).astype(bf16)
-    if stage:
+    if first_group:
         turned_grads[...] = earlier[0][...]
         query_gain_grad[...] = earlier[1][...]
         key_gain_grad[...] = earlier[2][...]
@@ -654,7 +658,7 @@
         turned_grads[lines((heads + kv_heads + kv_head) * HD, HD), :] = value_sum[...].astype(bf16)
         return carry
 
-    lax.fori_loop(stage * groups_here, (stage + 1) * groups_here, one_group, 0)
+    lax.fori_loop(first_group, last_group, one_group, 0)
     if last:
         straight[...] = turned_grads[...].T
         for part in range(count):
@@ -664,19 +668,25 @@
 
 
 def back_stages(kept):
-    return 2 if kept[2].shape[0] // HD % 2 == 0 else 1
+    kv_heads = kept[2].shape[0] // HD
+    if kv_heads % 4:
+        return [(0, kv_heads)]
+    quarter = kv_heads // 4
+    return [(0, quarter), (quarter, 3 * quarter), (3 * quarter, kv_heads)]
 
 
 def attend_back(fixed, kept, parts, stage, earlier, after):
     count = len(parts)
-    stages = back_stages(kept)
+    first_group, last_group = stage
+    kv_heads = kept[2].shape[0] // HD
     part_rows, model = parts[0].shape
     length = count * part_rows
     query_columns = kept[1].shape[0]
     columns = query_columns + 2 * kept[2].shape[0]
     shape = jax.ShapeDtypeStruct
     vmem = pl.BlockSpec(memory_space=pltpu.VMEM)
-    last = stage == stages - 1
+    last = last_group == kv_heads
+    share = kv_heads // (last_group - first_group)
     gains = [shape((HD, 1), f32)] * 2
     turned = shape((columns, length), bf16)
     scratch = [
@@ -695,7 +705,7 @@
     else:
         outs = [turned] + gains
     results = pl.pallas_call(
-        partial(attend_back_body, count, stage, stages, len(after)),
+        partial(attend_back_body, count, first_group, last_group, len(after)),
         in_specs=[pl.BlockSpec(memory_space=pltpu.SMEM)]
         + [vmem] * (11 + count + len(earlier))
         + [anywhere()] * len(after),
@@ -708,9 +718,9 @@
                 2 * length * model * (query_columns + columns)
                 + 20 * length * length * query_columns
             )
-            // stages,
+            // share,
             bytes_accessed=16 * length * model,
-            transcendentals=query_columns // HD * length * length // stages,
+            transcendentals=query_columns // HD * length * length // share,
         ),
         name="attend_back",
     )(*fixed, *kept, *parts, *earlier, *after)
@@ -755,13 +765,16 @@
     residual = tokens.astype(f32)
     normed, attn_norm_pull = jax.vjp(rms_norm, residual, attn_gain)
     normed_parts = widen(normed.astype(bf16))
-    cotangent_parts = widen(out_cotangent)
+    if len(normed_parts) == 2:
+        cotangent_parts = widen(held(out_cotangent, normed_parts[1:]))
+    else:
+        cotangent_parts = widen(out_cotangent)
     length = len(normed_parts) * normed_parts[0].shape[0]
     cosine, sine = rotary_tables(length)
     place = lax.axis_index("tp").astype(jnp.int32).reshape(1)
     fixed = (place, attn_full, query_gain[:, None], key_gain[:, None], cosine, sine)
     branch, attended, kept = attend(*fixed, normed_parts, query_columns, key_columns)
-    middle = residual + narrow(branch)
+    middle = residual + narrow([*branch[:-1], held(branch[-1], cotangent_parts[1:])])
     normed_ffn, ffn_norm_pull = jax.vjp(rms_norm, middle, ffn_gain)
     ffn_parts = widen(normed_ffn.astype(bf16))
     results = []
@@ -789,28 +802,31 @@
     )
     ffn_state, sent = ring_open(ffn_blocks)
     ffn_next, attn_next, last = 1, 1, ring_size() // 2
-    stages = back_stages(kept)
+    out_other = [narrow_send(held(out_parts[-1], branch_parts[1:]))] if len(out_parts) == 2 else []
     back = ()
-    for stage in range(stages):
+    for stage in back_stages(kept):
         back = attend_back(fixed, kept, branch_parts, stage, back, sent)
-        done = back[1] if stage < stages - 1 else back[2]
-        if stage == 0:
-            out_parts[-1] = held(out_parts[-1], (done,))
+        done = back[1] if len(back) == 3 else back[2]
         if ffn_next < last:
-            ffn_state, sent = ring_step(ffn_blocks, ffn_next, ffn_state, (done,))
+            after = (done, *out_other) if ffn_next == 2 else (done,)
+            ffn_state, sent = ring_step(ffn_blocks, ffn_next, ffn_state, after)
             ffn_next += 1
-    output = (middle + narrow(out_parts)).astype(bf16)
+    if out_other:
+        output = middle + out_parts[0] + out_other[0].astype(f32)
+    else:
+        output = middle + narrow(out_parts)
+    output = output.astype(bf16)
     normed_grad, qkv_grad, query_gain_local, key_gain_local = back
     normed_grad = narrow([*normed_grad[:-1], held(normed_grad[-1], sent)])
     attn_blocks = weight_grads(normed_parts, branch_parts, qkv_grad, attended, 1, sent)
     attn_state, sent = ring_open(attn_blocks)
     while ffn_next < last or attn_next < last:
+        if ffn_next < last:
+            ffn_state, sent = ring_step(ffn_blocks, ffn_next, ffn_state)
+            ffn_next += 1
         if attn_next < last:
             attn_state, sent = ring_step(attn_blocks, attn_next, attn_state, sent)
             attn_next += 1
-        if ffn_next < last:
-            ffn_state, sent = ring_step(ffn_blocks, ffn_next, ffn_state, sent)
-            ffn_next += 1
     ffn_pieces = [
         (step * 3 * width + number * width, width, number, step * width, number == 2)
         for step in range(steps)

time: 440 us -> 396 us (0.900)
  waiting for transfers between devices: 166 us -> 116 us
  Pallas kernels: 145 us -> 155 us
  starting transfers between devices: 59.8 us -> 55 us
    ppermute x30, waiting for transfers between devices: 90.2 us -> 57.1 us  [pass_on(): return lax.ppermute(values, 'fsdp', pairs)]
    ppermute x27, waiting for transfers between devices: 73.1 us -> 58.5 us  [swap(): return lax.ppermute(values, axis_name, [(i, i ^ bit) for i in range(count)])]
    pallas_call x2 -> x3, Pallas kernels: 36.4 us -> 42.5 us  [attend_back(): pl.pallas_call(partial(attend_back_body, count, first_group, last_group,...]
    pallas_call x10, Pallas kernels: 10.9 us -> 15.7 us  [ring_call(): pl.pallas_call(body, in_specs=[vmem] * len(operands) + [anywhere()] * len...]
    unnamed x120 -> x105, local copies, waits for them, and re-layouts: 15.3 us -> 14.7 us
  transfers between devices with their start and end apart: 59 -> 59, of which waited for: 22 -> 23; matrix products, arithmetic and copies ran while one was open for 5% -> 6% of each run, Pallas kernels for 27% -> 33%
where the time goes in v4:
time: 396 us; the launch traced here: 388 us
  Pallas kernels  155 us (39%)
  waiting for transfers between devices  116 us (29%)
  starting transfers between devices  55 us (14%)
  other arithmetic  24.9 us (6%)
  local copies, waits for them, and re-layouts  23.4 us (6%)
  between operations  15.1 us (4%)
    ppermute x27, waiting for transfers between devices, swap(): return lax.ppermute(values, axis_name, [(i, i ^ bit) for i in range(count)])  58.5 us
    ppermute x30, waiting for transfers between devices, pass_on(): return lax.ppermute(values, 'fsdp', pairs)  57.1 us
    pallas_call x2, Pallas kernels, feed_forward(): pl.pallas_call(partial(ffn_body, width, len(after)), grid=(steps,), in_sp...  44.1 us
    ppermute x30, starting transfers between devices, pass_on(): return lax.ppermute(values, 'fsdp', pairs)  43.7 us
    pallas_call x3, Pallas kernels, attend_back(): pl.pallas_call(partial(attend_back_body, count, first_group, last_group,...  42.5 us
    pallas_call x2, Pallas kernels, weight_grads(): pl.pallas_call(partial(weight_grad_body, parts, groups, rows, len(after))...  31.7 us
    pallas_call x1, Pallas kernels, attend(): pl.pallas_call(partial(attend_body, count), in_specs=[pl.BlockSpec(memory...  18.1 us
    pallas_call x10, Pallas kernels, ring_call(): pl.pallas_call(body, in_specs=[vmem] * len(operands) + [anywhere()] * len...  15.7 us
  transfers between devices with their start and end apart: 59, of which 23 were waited for; matrix products, arithmetic and copies ran while one was open for 6% of the time, Pallas kernels for 33%

profile of v4, /device:TPU:0, one launch (start us, length us, event | category | flops | bytes accessed | tf_op | source)
XLA Modules:
  0.0 388.5 jit_solution(6607763319291190212)
XLA Ops:
  12.4 1.8 reshape.79
  15.9 2.9 collective-permute-start.15
  22.0 3.3 collective-permute-done.refs_1_
  28.3 7.1 %collective-permute-done.2.refs_3_ = bf16[64,1536]{1,0:T(8,128)(2,1)S(1)} collective-permute-done((bf16[64,1536]{1,0:T(8,128)(2,1)S(1)}, bf16[64,1536]{1,0:T(8,128)(2,1)S(1)}, u32[]{:S(2)}, u32[]{:S(2)}) %collective-permute-start.2) | collective-permute-done | bytes 196640 | tf_op jit(solution)/shard_map/ppermute | solution.py:97
  35.4 3.7 collective-permute-start.4
  39.1 5.2 %collective-permute-done.3.refs_4_ = bf16[64,1536]{1,0:T(8,128)(2,1)S(1)} collective-permute-done((bf16[64,1536]{1,0:T(8,128)(2,1)S(1)}, bf16[64,1536]{1,0:T(8,128)(2,1)S(1)}, u32[]{:S(2)}, u32[]{:S(2)}) %collective-permute-start.3) | collective-permute-done | bytes 196640 | tf_op jit(solution)/shard_map/ppermute | solution.py:97
  44.8 2.5 collective-permute-done.4.refs_5_
  47.3 8.6 %collective-permute-start.6 = (bf16[64,1536]{1,0:T(8,128)(2,1)S(1)}, bf16[64,1536]{1,0:T(8,128)(2,1)S(1)}, u32[]{:S(2)}, u32[]{:S(2)}) collective-permute-start(bf16[64,1536]{1,0:T(8,128)(2,1)S(1)} %collective-permute-done.4.refs_5_), channel_id=1, source_target_pairs={{0,8},{2,10},{8,16},{10,18},{16,24},{18,26},{24,28},{26,30},{28,20... | collective-permute-start | bytes 589832 | tf_op jit(solution)/shard_map/ppermute | solution.py:97
  57.9 3.0 collective-permute-done.5.refs_6_
  61.0 2.3 collective-permute-done.6.refs_7_
  64.7 2.5 assemble.1.refs_1_
  67.2 18.1 %attend.1 = (f32[512,1024]{1,0:T(8,128)}, bf16[512,1024]{1,0:T(8,128)(2,1)}, bf16[512,512]{1,0:T(8,128)(2,1)}, bf16[512,512]{1,0:T(8,128)(2,1)}, f32[768,1024]{1...) custom-call(s32[1]{0:T(128)} %bitcast.refs_0_, ...), custom_call_target="tpu_custom_call" | custom-call | flops 7516192768 | bytes 16777216 | tf_op jit(solution)/shard_map/attend/pallas_call | solution.py:539
  85.4 25.6 %collective-permute-done.17 = bf16[512,1024]{1,0:T(8,128)(2,1)S(1)} collective-permute-done((bf16[512,1024]{1,0:T(8,128)(2,1)}, bf16[512,1024]{1,0:T(8,128)(2,1)S(1)}, u32[]{:S(2)}, u32[]{:S(2)}) %collective-permute-start.17) | collective-permute-done | bytes 1048608 | tf_op jit(solution)/shard_map/ppermute | solution.py:43
  111.0 2.1 multiply_reduce_fusion.2
  114.7 23.6 %collective-permute-done.18.refs_0_.refs_2_ = bf16[512,1024]{1,0:T(8,128)(2,1)} collective-permute-done((bf16[512,1024]{1,0:T(8,128)(2,1)S(1)}, bf16[512,1024]{1,0:T(8,128)(2,1)}, u32[]{:S(2)}, u32[]{:S(2)}) %collective-permute-start.18) | collective-permute-done | bytes 1048608 | tf_op jit(solution)/shard_map/ppermute | solution.py:43
  138.3 21.5 %feed_forward.2 = (bf16[512,1024]{1,0:T(8,128)(2,1)}, bf16[512,1024]{1,0:T(8,128)(2,1)}, bf16[512,4608]{1,0:T(8,128)(2,1)}, bf16[512,2304]{1,0:T(8,128)(2,1)}) custom-call(bf16[512,1024]{1,0:T(8,128)(2,1)} %collective-permute-done.18.refs_0_.refs_2_, bf16[512,1024]{1,0:T(8,128)(2,1)} %collective-permute-done.16.refs_1_.refs_4_, ...), custom_call_target="tpu_custom_call" | custom-call | flops 14495514624 | bytes 18874368 | tf_op jit(solution)/shard_map/feed_forward/pallas_call | solution.py:393
  160.7 22.6 %feed_forward.3 = (f32[512,1024]{1,0:T(8,128)}, f32[512,1024]{1,0:T(8,128)}, bf16[512,4608]{1,0:T(8,128)(2,1)}, bf16[512,2304]{1,0:T(8,128)(2,1)}) custom-call(bf16[512,1024]{1,0:T(8,128)(2,1)} %copy-done.33, bf16[512,1024]{1,0:T(8,128)(2,1)} %held.5.refs_1_.refs_3_, bf16[1024,6912]{1,0:T(8,128)(2,1)} %all-gather.2.cloned.1.call-done.refs_2_, ...), custom_call_target="tpu_custom_call" | custom-call | flops 14495514624 | bytes 18874368 | tf_op jit(solution)/shard_map/feed_forward/pallas_call | solution.py:393
  184.9 3.0 multiply_reduce_fusion
  188.0 2.0 fusion.17
  191.3 23.5 %weight_grads.2 = (bf16[1,64,6912]{2,1,0:T(8,128)(2,1)}, bf16[2,64,6912]{2,1,0:T(8,128)(2,1)}, bf16[2,64,6912]{2,1,0:T(8,128)(2,1)}, bf16[2,64,6912]{2,1,0:T(8,1...) custom-call(s32[16]{0:T(128)} %pad_add_fusion.1.refs_0_, ...), custom_call_target="tpu_custom_call" | custom-call | flops 14495514624 | bytes 28311552 | tf_op jit(solution)/shard_map/weight_grads/pallas_call | solution.py:214
  215.5 5.8 %collective-permute-done.22.near = bf16[1,64,6912]{2,1,0:T(8,128)(2,1)S(1)} collective-permute-done((bf16[1,64,6912]{2,1,0:T(8,128)(2,1)}, bf16[1,64,6912]{2,1,0:T(8,128)(2,1)S(1)}, u32[]{:S(2)}, u32[]{:S(2)}) %collective-permute-start.22) | collective-permute-done | bytes 884768 | tf_op jit(solution)/shard_map/ppermute | solution.py:43
  222.3 4.1 %collective-permute-start.24 = (bf16[64,3456]{1,0:T(8,128)(2,1)}, bf16[64,3456]{1,0:T(8,128)(2,1)S(1)}, u32[]{:S(2)}, u32[]{:S(2)}) collective-permute-start(bf16[64,3456]{1,0:T(8,128)(2,1)} %get-tuple-element.104.refs_14_), channel_id=1, source_target_pairs={{0,8},{2,10},{8,16},{10,18},{16,24},{18,26},{24,28},{26,30},{28,20... | collective-permute-start | bytes 1327112 | tf_op jit(solution)/shard_map/ppermute | solution.py:97
  226.5 2.0 collective-permute-start.25
  229.5 11.3 %attend_back.3 = (bf16[1024,1024]{1,0:T(8,128)(2,1)}, f32[64,1]{1,0:T(8,128)}, f32[64,1]{1,0:T(8,128)}) custom-call(s32[1]{0:T(128)} %bitcast.refs_0_, bf16[1024,1536]{1,0:T(8,128)(2,1)} %assemble.1.refs_1_, f32[64,1]{1,0:T(8,128)} %copy.47.refs_2_, f32[64,1]{1,0:T(8,128)} %copy.48.refs_3_, f32[32,1024]{1,0:T(8,128)} %get-tuple-element.202.refs_4_, ...), custom_call_target="tpu_custom_call" | custom-call | flops 3489660928 | bytes 16777216 | tf_op jit(solution)/shard_map/attend_back/pallas_call | solution.py:707
  243.1 1.9 collective-permute-start.27
  245.2 16.5 %attend_back.4 = (bf16[1024,1024]{1,0:T(8,128)(2,1)}, f32[64,1]{1,0:T(8,128)}, f32[64,1]{1,0:T(8,128)}) custom-call(s32[1]{0:T(128)} %bitcast.refs_0_, bf16[1024,1536]{1,0:T(8,128)(2,1)} %assemble.1.refs_1_, f32[64,1]{1,0:T(8,128)} %copy.47.refs_2_, f32[64,1]{1,0:T(8,128)} %copy.48.refs_3_, f32[32,1024]{1,0:T(8,128)} %get-tuple-element.202.refs_4_, ...), custom_call_target="tpu_custom_call" | custom-call | flops 6979321856 | bytes 16777216 | tf_op jit(solution)/shard_map/attend_back/pallas_call | solution.py:707
  261.8 2.5 collective-permute-done.27.down
  266.6 2.6 ring_step.7
  269.3 1.8 collective-permute-start.30
  271.5 14.7 %attend_back.5 = (f32[512,1024]{1,0:T(8,128)}, bf16[512,1024]{1,0:T(8,128)(2,1)}, bf16[512,1024]{1,0:T(8,128)(2,1)}, bf16[512,1024]{1,0:T(8,128)(2,1)}, f32[64,1]{1,0:T(8,128)}, /*index=5*/f32[64,1]{1,0:T(8,128)}) custom-call(s32[1]{0:T(128)} %bitcast.refs_0_, bf16[1024,1536]{1,0:T(8,128)(2,1)} %assemble.1.refs_1_, f32[64,1]{1,0:T(8,128)} %copy.47.refs_2_, ...), custom_call_target="tpu_custom_call" | custom-call | flops 3489660928 | bytes 16777216 | tf_op jit(solution)/shard_map/attend_back/pallas_call | solution.py:707
  286.2 3.0 collective-permute-done.30.down
  291.4 3.1 ring_step.8
  295.5 8.2 %weight_grads.3 = (bf16[1,64,1536]{2,1,0:T(8,128)(2,1)}, bf16[2,64,1536]{2,1,0:T(8,128)(2,1)}, bf16[2,64,1536]{2,1,0:T(8,128)(2,1)}, bf16[2,64,1536]{2,1,0:T(8,1...) custom-call(s32[16]{0:T(128)} %pad_add_fusion.1.refs_0_, ...), custom_call_target="tpu_custom_call" | custom-call | flops 3221225472 | bytes 6291456 | tf_op jit(solution)/shard_map/weight_grads/pallas_call | solution.py:214
  306.9 1.7 collective-permute-start.47
  309.0 2.8 collective-permute-done.47.down
  316.6 5.0 %collective-permute-done.49.down = bf16[64,1536]{1,0:T(8,128)(2,1)S(1)} collective-permute-done((bf16[64,1536]{1,0:T(8,128)(2,1)S(1)}, bf16[64,1536]{1,0:T(8,128)(2,1)S(1)}, u32[]{:S(2)}, u32[]{:S(2)}) %collective-permute-start.49) | collective-permute-done | bytes 196640 | tf_op jit(solution)/shard_map/ppermute | solution.py:97
  323.0 5.4 %collective-permute-done.50.up = bf16[64,1536]{1,0:T(8,128)(2,1)S(1)} collective-permute-done((bf16[64,1536]{1,0:T(8,128)(2,1)S(1)}, bf16[64,1536]{1,0:T(8,128)(2,1)S(1)}, u32[]{:S(2)}, u32[]{:S(2)}) %collective-permute-start.50) | collective-permute-done | bytes 196640 | tf_op jit(solution)/shard_map/ppermute | solution.py:97
  334.7 2.0 collective-permute-start.51
  337.1 3.4 fusion.3
  340.5 3.1 collective-permute-done.51.down
  344.6 6.6 %collective-permute-done.52.up = bf16[64,1536]{1,0:T(8,128)(2,1)} collective-permute-done((bf16[64,1536]{1,0:T(8,128)(2,1)}, bf16[64,1536]{1,0:T(8,128)(2,1)}, u32[]{:S(2)}, u32[]{:S(2)}) %collective-permute-start.52) | collective-permute-done | bytes 196640 | tf_op jit(solution)/shard_map/ppermute | solution.py:97
  351.2 2.0 ring_step.11
  355.3 3.9 add_convert_fusion
  359.2 2.8 ring_close.3
  363.1 1.7 ring_close.2
  366.9 3.3 collective-permute-start.39
  371.8 2.9 collective-permute-start.37
  375.5 4.4 %fusion.5 = f32[512,1024]{1,0:T(8,128)} fusion(f32[512,1024]{1,0:T(8,128)} %get-tuple-element.192, bf16[512,1024]{1,0:T(8,128)(2,1)S(1)} %copy-done.28, f32[512]{0:T(512)S(1)} %multiply_multiply_fusion, f32[1024]{0:T(1024)S(1)} %copy-done.36, f32[512]{0:T(512)S(1)} %copy-done.39, f32[512,1024]{1,0:T(8,128)} %get-tuple-element.120, ...), kind=kLoop, calls=%fused_computation.12 | loop fusion | flops 4718592 | bytes 8396800 | tf_op jit(solution)/shard_map/add | solution.py:844
  (237 shorter events, 59.9 us)
Async XLA Ops:
  7.2 131.1 %all-gather.2.cloned.1.call-start = ((), (), s32[]{:S(2)}) async-start(), calls=%async_computation | async-start | bytes 15040512 | tf_op jit(solution)/shard_map/all_gather | solution.py:763
  15.9 28.4 %collective-permute-start.15 = (bf16[512,1024]{1,0:T(8,128)(2,1)}, bf16[512,1024]{1,0:T(8,128)(2,1)}, u32[]{:S(2)}, u32[]{:S(2)}) collective-permute-start(bf16[512,1024]{1,0:T(8,128)(2,1)} %fusion.2.refs_6_.refs_1_), channel_id=1, source_target_pairs={{0,1},{1,0},{2,3},{3,2},{4,5},{5,4},{6,7},{7,6},{8,9},{9,8},{10,11... | collective-permute-start | bytes 3145736 | tf_op jit(solution)/shard_map/ppermute | solution.py:43
  20.5 24.3 %collective-permute-start.7 = (bf16[64,1536]{1,0:T(8,128)(2,1)S(1)}, bf16[64,1536]{1,0:T(8,128)(2,1)S(1)}, u32[]{:S(2)}, u32[]{:S(2)}) collective-permute-start(bf16[64,1536]{1,0:T(8,128)(2,1)S(1)} %pad_maximum_fusion.1.refs_0_), channel_id=1, source_target_pairs={{0,2},{2,0},{4,6},{6,4},{8,10},{10,8},{12,14},{14,12},{16,18},{18,... | collective-permute-start | bytes 589832 | tf_op jit(solution)/shard_map/ppermute | solution.py:43
  20.5 7.3 %collective-permute-start.1 = (bf16[64,1536]{1,0:T(8,128)(2,1)S(1)}, bf16[64,1536]{1,0:T(8,128)(2,1)S(1)}, u32[]{:S(2)}, u32[]{:S(2)}) collective-permute-start(bf16[64,1536]{1,0:T(8,128)(2,1)S(1)} %pad_maximum_fusion.1.refs_0_), channel_id=1, source_target_pairs={{0,4},{2,6},{8,0},{10,2},{16,8},{18,10},{24,16},{26,18},{28,24},{3... | collective-permute-start | bytes 589832 | tf_op jit(solution)/shard_map/ppermute | solution.py:97
  25.3 10.1 %collective-permute-start.2 = (bf16[64,1536]{1,0:T(8,128)(2,1)S(1)}, bf16[64,1536]{1,0:T(8,128)(2,1)S(1)}, u32[]{:S(2)}, u32[]{:S(2)}) collective-permute-start(bf16[64,1536]{1,0:T(8,128)(2,1)S(1)} %collective-permute-done.refs_1_), channel_id=1, source_target_pairs={{0,8},{2,10},{8,16},{10,18},{16,24},{18,26},{24,28},{26,30},{28,20... | collective-permute-start | bytes 589832 | tf_op jit(solution)/shard_map/ppermute | solution.py:97
  27.8 28.1 %collective-permute-start.9 = (bf16[64,1536]{1,0:T(8,128)(2,1)S(1)}, bf16[64,1536]{1,0:T(8,128)(2,1)S(1)}, u32[]{:S(2)}, u32[]{:S(2)}) collective-permute-start(bf16[64,1536]{1,0:T(8,128)(2,1)S(1)} %collective-permute-done.1.refs_2_), channel_id=1, source_target_pairs={{0,2},{2,0},{4,6},{6,4},{8,10},{10,8},{12,14},{14,12},{16,18},{18,... | collective-permute-start | bytes 589832 | tf_op jit(solution)/shard_map/ppermute | solution.py:43
  27.8 16.5 %collective-permute-start.3 = (bf16[64,1536]{1,0:T(8,128)(2,1)S(1)}, bf16[64,1536]{1,0:T(8,128)(2,1)S(1)}, u32[]{:S(2)}, u32[]{:S(2)}) collective-permute-start(bf16[64,1536]{1,0:T(8,128)(2,1)S(1)} %collective-permute-done.1.refs_2_), channel_id=1, source_target_pairs={{0,4},{2,6},{8,0},{10,2},{16,8},{18,10},{24,16},{26,18},{28,24},{3... | collective-permute-start | bytes 589832 | tf_op jit(solution)/shard_map/ppermute | solution.py:97
  35.4 11.9 %collective-permute-start.4 = (bf16[64,1536]{1,0:T(8,128)(2,1)S(1)}, bf16[64,1536]{1,0:T(8,128)(2,1)S(1)}, u32[]{:S(2)}, u32[]{:S(2)}) collective-permute-start(bf16[64,1536]{1,0:T(8,128)(2,1)S(1)} %collective-permute-done.2.refs_3_), channel_id=1, source_target_pairs={{0,8},{2,10},{8,16},{10,18},{16,24},{18,26},{24,28},{26,30},{28,20... | collective-permute-start | bytes 589832 | tf_op jit(solution)/shard_map/ppermute | solution.py:97
  44.3 13.1 %collective-permute-start.8 = (bf16[64,1536]{1,0:T(8,128)(2,1)S(1)}, bf16[64,1536]{1,0:T(8,128)(2,1)S(1)}, u32[]{:S(2)}, u32[]{:S(2)}) collective-permute-start(bf16[64,1536]{1,0:T(8,128)(2,1)S(1)} %collective-permute-done.refs_1_), channel_id=1, source_target_pairs={{0,2},{2,0},{4,6},{6,4},{8,10},{10,8},{12,14},{14,12},{16,18},{18,... | collective-permute-start | bytes 589832 | tf_op jit(solution)/shard_map/ppermute | solution.py:43
  44.3 13.1 %collective-permute-start.11 = (bf16[64,1536]{1,0:T(8,128)(2,1)S(1)}, bf16[64,1536]{1,0:T(8,128)(2,1)S(1)}, u32[]{:S(2)}, u32[]{:S(2)}) collective-permute-start(bf16[64,1536]{1,0:T(8,128)(2,1)S(1)} %collective-permute-done.3.refs_4_), channel_id=1, source_target_pairs={{0,2},{2,0},{4,6},{6,4},{8,10},{10,8},{12,14},{14,12},{16,18},{18,... | collective-permute-start | bytes 589832 | tf_op jit(solution)/shard_map/ppermute | solution.py:43
  44.8 16.1 %collective-permute-start.5 = (bf16[64,1536]{1,0:T(8,128)(2,1)S(1)}, bf16[64,1536]{1,0:T(8,128)(2,1)S(1)}, u32[]{:S(2)}, u32[]{:S(2)}) collective-permute-start(bf16[64,1536]{1,0:T(8,128)(2,1)S(1)} %collective-permute-done.3.refs_4_), channel_id=1, source_target_pairs={{0,4},{2,6},{8,0},{10,2},{16,8},{18,10},{24,16},{26,18},{28,24},{3... | collective-permute-start | bytes 589832 | tf_op jit(solution)/shard_map/ppermute | solution.py:97
  47.3 16.0 %collective-permute-start.6 = (bf16[64,1536]{1,0:T(8,128)(2,1)S(1)}, bf16[64,1536]{1,0:T(8,128)(2,1)S(1)}, u32[]{:S(2)}, u32[]{:S(2)}) collective-permute-start(bf16[64,1536]{1,0:T(8,128)(2,1)S(1)} %collective-permute-done.4.refs_5_), channel_id=1, source_target_pairs={{0,8},{2,10},{8,16},{10,18},{16,24},{18,26},{24,28},{26,30},{28,20... | collective-permute-start | bytes 589832 | tf_op jit(solution)/shard_map/ppermute | solution.py:97
  55.9 29.4 %collective-permute-start.16 = (bf16[512,1024]{1,0:T(8,128)(2,1)}, bf16[512,1024]{1,0:T(8,128)(2,1)}, u32[]{:S(2)}, u32[]{:S(2)}) collective-permute-start(bf16[512,1024]{1,0:T(8,128)(2,1)} %held.5.refs_1_.refs_3_), channel_id=1, source_target_pairs={{0,1},{1,0},{2,3},{3,2},{4,5},{5,4},{6,7},{7,6},{8,9},{9,8},{10,11... | collective-permute-start | bytes 3145736 | tf_op jit(solution)/shard_map/ppermute | solution.py:43
  57.4 7.1 %collective-permute-start.10 = (bf16[64,1536]{1,0:T(8,128)(2,1)S(1)}, bf16[64,1536]{1,0:T(8,128)(2,1)S(1)}, u32[]{:S(2)}, u32[]{:S(2)}) collective-permute-start(bf16[64,1536]{1,0:T(8,128)(2,1)S(1)} %collective-permute-done.2.refs_3_), channel_id=1, source_target_pairs={{0,2},{2,0},{4,6},{6,4},{8,10},{10,8},{12,14},{14,12},{16,18},{18,... | collective-permute-start | bytes 589832 | tf_op jit(solution)/shard_map/ppermute | solution.py:43
  85.3 25.7 %collective-permute-start.17 = (bf16[512,1024]{1,0:T(8,128)(2,1)}, bf16[512,1024]{1,0:T(8,128)(2,1)S(1)}, u32[]{:S(2)}, u32[]{:S(2)}) collective-permute-start(bf16[512,1024]{1,0:T(8,128)(2,1)} %held.6), channel_id=1, source_target_pairs={{0,1},{1,0},{2,3},{3,2},{4,5},{5,4},{6,7},{7,6},{8,9},{9,8},{10,11... | collective-permute-start | bytes 3145736 | tf_op jit(solution)/shard_map/ppermute | solution.py:43
  113.4 24.9 %collective-permute-start.18 = (bf16[512,1024]{1,0:T(8,128)(2,1)S(1)}, bf16[512,1024]{1,0:T(8,128)(2,1)}, u32[]{:S(2)}, u32[]{:S(2)}) collective-permute-start(bf16[512,1024]{1,0:T(8,128)(2,1)S(1)} %multiply_convert_fusion.refs_0_.refs_1_), channel_id=1, source_target_pairs={{0,1},{1,0},{2,3},{3,2},{4,5},{5,4},{6,7},{7,6},{8,9},{9,8},{10,11... | collective-permute-start | bytes 3145736 | tf_op jit(solution)/shard_map/ppermute | solution.py:43
  159.7 25.2 %collective-permute-start.19 = (bf16[512,1024]{1,0:T(8,128)(2,1)}, bf16[512,1024]{1,0:T(8,128)(2,1)S(1)}, u32[]{:S(2)}, u32[]{:S(2)}) collective-permute-start(bf16[512,1024]{1,0:T(8,128)(2,1)} %get-tuple-element.88.refs_3_), channel_id=1, source_target_pairs={{0,1},{1,0},{2,3},{3,2},{4,5},{5,4},{6,7},{7,6},{8,9},{9,8},{10,11... | collective-permute-start | bytes 3145736 | tf_op jit(solution)/shard_map/ppermute | solution.py:43
  190.0 24.9 %collective-permute-start.20 = (bf16[512,1024]{1,0:T(8,128)(2,1)S(1)}, bf16[512,1024]{1,0:T(8,128)(2,1)}, u32[]{:S(2)}, u32[]{:S(2)}) collective-permute-start(bf16[512,1024]{1,0:T(8,128)(2,1)S(1)} %get-tuple-element.191.refs_9_.refs_12_.refs_3_), channel_id=1, source_target_pairs={{0,1},{1,0},{2,3},{3,2},{4,5},{5,4},{6,7},{7,6},{8,9},{9,8},{10,11... | collective-permute-start | bytes 3145736 | tf_op jit(solution)/shard_map/ppermute | solution.py:43
  214.8 26.0 %collective-permute-start.23 = (bf16[2,64,6912]{2,1,0:T(8,128)(2,1)}, bf16[2,64,6912]{2,1,0:T(8,128)(2,1)S(1)}, u32[]{:S(2)}, u32[]{:S(2)}) collective-permute-start(bf16[2,64,6912]{2,1,0:T(8,128)(2,1)} %get-tuple-element.110), channel_id=1, source_target_pairs={{0,2},{2,0},{4,6},{6,4},{8,10},{10,8},{12,14},{14,12},{16,18},{18,... | collective-permute-start | bytes 5308424 | tf_op jit(solution)/shard_map/ppermute | solution.py:43
  215.4 46.4 %collective-permute-start.26 = (bf16[2,64,6912]{2,1,0:T(8,128)(2,1)}, bf16[2,64,6912]{2,1,0:T(8,128)(2,1)}, u32[]{:S(2)}, u32[]{:S(2)}) collective-permute-start(bf16[2,64,6912]{2,1,0:T(8,128)(2,1)} %get-tuple-element.117), channel_id=1, source_target_pairs={{0,2},{2,0},{4,6},{6,4},{8,10},{10,8},{12,14},{14,12},{16,18},{18,... | collective-permute-start | bytes 5308424 | tf_op jit(solution)/shard_map/ppermute | solution.py:43
  222.3 18.4 %collective-permute-start.24 = (bf16[64,3456]{1,0:T(8,128)(2,1)}, bf16[64,3456]{1,0:T(8,128)(2,1)S(1)}, u32[]{:S(2)}, u32[]{:S(2)}) collective-permute-start(bf16[64,3456]{1,0:T(8,128)(2,1)} %get-tuple-element.104.refs_14_), channel_id=1, source_target_pairs={{0,8},{2,10},{8,16},{10,18},{16,24},{18,26},{24,28},{26,30},{28,20... | collective-permute-start | bytes 1327112 | tf_op jit(solution)/shard_map/ppermute | solution.py:97
  226.5 14.3 %collective-permute-start.25 = (bf16[64,3456]{1,0:T(8,128)(2,1)}, bf16[64,3456]{1,0:T(8,128)(2,1)}, u32[]{:S(2)}, u32[]{:S(2)}) collective-permute-start(bf16[64,3456]{1,0:T(8,128)(2,1)} %get-tuple-element.105.refs_15_), channel_id=1, source_target_pairs={{0,4},{2,6},{8,0},{10,2},{16,8},{18,10},{24,16},{26,18},{28,24},{3... | collective-permute-start | bytes 1327112 | tf_op jit(solution)/shard_map/ppermute | solution.py:97
  228.4 33.3 %collective-permute-start.21 = (bf16[512,1024]{1,0:T(8,128)(2,1)}, bf16[512,1024]{1,0:T(8,128)(2,1)S(1)}, u32[]{:S(2)}, u32[]{:S(2)}) collective-permute-start(bf16[512,1024]{1,0:T(8,128)(2,1)} %held.7), channel_id=1, source_target_pairs={{0,1},{1,0},{2,3},{3,2},{4,5},{5,4},{6,7},{7,6},{8,9},{9,8},{10,11... | collective-permute-start | bytes 3145736 | tf_op jit(solution)/shard_map/ppermute | solution.py:43
  243.1 21.2 %collective-permute-start.27 = (bf16[64,6912]{1,0:T(8,128)(2,1)S(1)}, bf16[64,6912]{1,0:T(8,128)(2,1)S(1)}, u32[]{:S(2)}, u32[]{:S(2)}) collective-permute-start(bf16[64,6912]{1,0:T(8,128)(2,1)S(1)} %get-tuple-element.111.refs_17_), channel_id=1, source_target_pairs={{0,8},{2,10},{8,16},{10,18},{16,24},{18,26},{24,28},{26,30},{28,20... | collective-permute-start | bytes 2654216 | tf_op jit(solution)/shard_map/ppermute | solution.py:97
  245.0 20.8 %collective-permute-start.28 = (bf16[64,6912]{1,0:T(8,128)(2,1)S(1)}, bf16[64,6912]{1,0:T(8,128)(2,1)S(1)}, u32[]{:S(2)}, u32[]{:S(2)}) collective-permute-start(bf16[64,6912]{1,0:T(8,128)(2,1)S(1)} %get-tuple-element.112.refs_18_), channel_id=1, source_target_pairs={{0,4},{2,6},{8,0},{10,2},{16,8},{18,10},{24,16},{26,18},{28,24},{3... | collective-permute-start | bytes 2654216 | tf_op jit(solution)/shard_map/ppermute | solution.py:97
  245.2 41.0 %collective-permute-start.29 = (bf16[2,64,6912]{2,1,0:T(8,128)(2,1)}, bf16[2,64,6912]{2,1,0:T(8,128)(2,1)}, u32[]{:S(2)}, u32[]{:S(2)}) collective-permute-start(bf16[2,64,6912]{2,1,0:T(8,128)(2,1)} %get-tuple-element.123), channel_id=1, source_target_pairs={{0,2},{2,0},{4,6},{6,4},{8,10},{10,8},{12,14},{14,12},{16,18},{18,... | collective-permute-start | bytes 5308424 | tf_op jit(solution)/shard_map/ppermute | solution.py:43
  269.3 20.0 %collective-permute-start.30 = (bf16[64,6912]{1,0:T(8,128)(2,1)S(1)}, bf16[64,6912]{1,0:T(8,128)(2,1)S(1)}, u32[]{:S(2)}, u32[]{:S(2)}) collective-permute-start(bf16[64,6912]{1,0:T(8,128)(2,1)S(1)} %get-tuple-element.118.refs_17_), channel_id=1, source_target_pairs={{0,8},{2,10},{8,16},{10,18},{16,24},{18,26},{24,28},{26,30},{28,20... | collective-permute-start | bytes 2654216 | tf_op jit(solution)/shard_map/ppermute | solution.py:97
  271.1 19.5 %collective-permute-start.31 = (bf16[64,6912]{1,0:T(8,128)(2,1)S(1)}, bf16[64,6912]{1,0:T(8,128)(2,1)S(1)}, u32[]{:S(2)}, u32[]{:S(2)}) collective-permute-start(bf16[64,6912]{1,0:T(8,128)(2,1)S(1)} %get-tuple-element.119.refs_18_), channel_id=1, source_target_pairs={{0,4},{2,6},{8,0},{10,2},{16,8},{18,10},{24,16},{26,18},{28,24},{3... | collective-permute-start | bytes 2654216 | tf_op jit(solution)/shard_map/ppermute | solution.py:97
  294.5 42.3 %collective-permute-start.32 = (bf16[512,1024]{1,0:T(8,128)(2,1)}, bf16[512,1024]{1,0:T(8,128)(2,1)}, u32[]{:S(2)}, u32[]{:S(2)}) collective-permute-start(bf16[512,1024]{1,0:T(8,128)(2,1)} %held.9), channel_id=1, source_target_pairs={{0,1},{1,0},{2,3},{3,2},{4,5},{5,4},{6,7},{7,6},{8,9},{9,8},{10,11... | collective-permute-start | bytes 3145736 | tf_op jit(solution)/shard_map/ppermute | solution.py:43
  303.7 9.5 %collective-permute-start.45 = (bf16[2,64,1536]{2,1,0:T(8,128)(2,1)}, bf16[2,64,1536]{2,1,0:T(8,128)(2,1)S(1)}, u32[]{:S(2)}, u32[]{:S(2)}) collective-permute-start(bf16[2,64,1536]{2,1,0:T(8,128)(2,1)} %get-tuple-element.139), channel_id=1, source_target_pairs={{0,2},{2,0},{4,6},{6,4},{8,10},{10,8},{12,14},{14,12},{16,18},{18,... | collective-permute-start | bytes 1179656 | tf_op jit(solution)/shard_map/ppermute | solution.py:43
  304.2 12.1 %collective-permute-start.44 = (bf16[2,64,1536]{2,1,0:T(8,128)(2,1)}, bf16[2,64,1536]{2,1,0:T(8,128)(2,1)S(1)}, u32[]{:S(2)}, u32[]{:S(2)}) collective-permute-start(bf16[2,64,1536]{2,1,0:T(8,128)(2,1)} %get-tuple-element.137), channel_id=1, source_target_pairs={{0,2},{2,0},{4,6},{6,4},{8,10},{10,8},{12,14},{14,12},{16,18},{18,... | collective-permute-start | bytes 1179656 | tf_op jit(solution)/shard_map/ppermute | solution.py:43
  314.4 7.2 %collective-permute-start.49 = (bf16[64,1536]{1,0:T(8,128)(2,1)S(1)}, bf16[64,1536]{1,0:T(8,128)(2,1)S(1)}, u32[]{:S(2)}, u32[]{:S(2)}) collective-permute-start(bf16[64,1536]{1,0:T(8,128)(2,1)S(1)} %get-tuple-element.144.refs_0_), channel_id=1, source_target_pairs={{0,8},{2,10},{8,16},{10,18},{16,24},{18,26},{24,28},{26,30},{28,20... | collective-permute-start | bytes 589832 | tf_op jit(solution)/shard_map/ppermute | solution.py:97
  315.7 38.1 %collective-permute-start.55 = (bf16[1,64,6912]{2,1,0:T(8,128)(2,1)}, bf16[1,64,6912]{2,1,0:T(8,128)(2,1)S(1)}, u32[]{:S(2)}, u32[]{:S(2)}) collective-permute-start(bf16[1,64,6912]{2,1,0:T(8,128)(2,1)} %get-tuple-element.155), channel_id=1, source_target_pairs={{0,2},{2,0},{4,6},{6,4},{8,10},{10,8},{12,14},{14,12},{16,18},{18,... | collective-permute-start | bytes 2654216 | tf_op jit(solution)/shard_map/ppermute | solution.py:43
  315.7 39.5 %collective-permute-start.56 = (bf16[64,6912]{1,0:T(8,128)(2,1)}, bf16[64,6912]{1,0:T(8,128)(2,1)S(1)}, u32[]{:S(2)}, u32[]{:S(2)}) collective-permute-start(bf16[64,6912]{1,0:T(8,128)(2,1)} %get-tuple-element.125.refs_1_.refs_9_), channel_id=1, source_target_pairs={{0,8},{2,10},{8,16},{10,18},{16,24},{18,26},{24,28},{26,30},{28,20... | collective-permute-start | bytes 2654216 | tf_op jit(solution)/shard_map/ppermute | solution.py:97
  316.4 18.4 %collective-permute-start.43 = (bf16[2,64,1536]{2,1,0:T(8,128)(2,1)}, bf16[2,64,1536]{2,1,0:T(8,128)(2,1)}, u32[]{:S(2)}, u32[]{:S(2)}) collective-permute-start(bf16[2,64,1536]{2,1,0:T(8,128)(2,1)} %get-tuple-element.135), channel_id=1, source_target_pairs={{0,2},{2,0},{4,6},{6,4},{8,10},{10,8},{12,14},{14,12},{16,18},{18,... | collective-permute-start | bytes 1179656 | tf_op jit(solution)/shard_map/ppermute | solution.py:43
  329.0 30.1 %collective-permute-start.57 = (bf16[64,6912]{1,0:T(8,128)(2,1)}, bf16[64,6912]{1,0:T(8,128)(2,1)}, u32[]{:S(2)}, u32[]{:S(2)}) collective-permute-start(bf16[64,6912]{1,0:T(8,128)(2,1)} %get-tuple-element.126.refs_2_.refs_10_), channel_id=1, source_target_pairs={{0,4},{2,6},{8,0},{10,2},{16,8},{18,10},{24,16},{26,18},{28,24},{3... | collective-permute-start | bytes 2654216 | tf_op jit(solution)/shard_map/ppermute | solution.py:97
  334.7 8.9 %collective-permute-start.51 = (bf16[64,1536]{1,0:T(8,128)(2,1)S(1)}, bf16[64,1536]{1,0:T(8,128)(2,1)}, u32[]{:S(2)}, u32[]{:S(2)}) collective-permute-start(bf16[64,1536]{1,0:T(8,128)(2,1)S(1)} %get-tuple-element.146.refs_0_), channel_id=1, source_target_pairs={{0,8},{2,10},{8,16},{10,18},{16,24},{18,26},{24,28},{26,30},{28,20... | collective-permute-start | bytes 589832 | tf_op jit(solution)/shard_map/ppermute | solution.py:97
  336.8 14.5 %collective-permute-start.52 = (bf16[64,1536]{1,0:T(8,128)(2,1)}, bf16[64,1536]{1,0:T(8,128)(2,1)}, u32[]{:S(2)}, u32[]{:S(2)}) collective-permute-start(bf16[64,1536]{1,0:T(8,128)(2,1)} %get-tuple-element.147.refs_1_), channel_id=1, source_target_pairs={{0,4},{2,6},{8,0},{10,2},{16,8},{18,10},{24,16},{26,18},{28,24},{3... | collective-permute-start | bytes 589832 | tf_op jit(solution)/shard_map/ppermute | solution.py:97
  343.6 9.6 %collective-permute-start.33 = (f32[2176]{0:T(1024)S(1)}, f32[2176]{0:T(1024)S(1)}, u32[]{:S(2)}, u32[]{:S(2)}) collective-permute-start(f32[2176]{0:T(1024)S(1)} %concatenate.18), channel_id=1, source_target_pairs={{0,1},{1,0},{2,3},{3,2},{4,5},{5,4},{6,7},{7,6},{8,9},{9,8},{10,11... | collective-permute-start | bytes 26120 | tf_op jit(solution)/shard_map/ppermute | solution.py:68
  351.2 11.9 %collective-permute-start.42 = (bf16[1,64,1536]{2,1,0:T(8,128)(2,1)}, bf16[1,64,1536]{2,1,0:T(8,128)(2,1)}, u32[]{:S(2)}, u32[]{:S(2)}) collective-permute-start(bf16[1,64,1536]{2,1,0:T(8,128)(2,1)} %get-tuple-element.133), channel_id=1, source_target_pairs={{0,2},{2,0},{4,6},{6,4},{8,10},{10,8},{12,14},{14,12},{16,18},{18,... | collective-permute-start | bytes 589832 | tf_op jit(solution)/shard_map/ppermute | solution.py:43
  353.2 9.9 %collective-permute-start.53 = (bf16[64,1536]{1,0:T(8,128)(2,1)}, bf16[64,1536]{1,0:T(8,128)(2,1)S(1)}, u32[]{:S(2)}, u32[]{:S(2)}) collective-permute-start(bf16[64,1536]{1,0:T(8,128)(2,1)} %get-tuple-element.148), channel_id=1, source_target_pairs={{0,8},{2,10},{8,16},{10,18},{16,24},{18,26},{24,28},{26,30},{28,20... | collective-permute-start | bytes 589832 | tf_op jit(solution)/shard_map/ppermute | solution.py:97
  353.9 9.2 %collective-permute-start.54 = (bf16[64,1536]{1,0:T(8,128)(2,1)}, bf16[64,1536]{1,0:T(8,128)(2,1)S(1)}, u32[]{:S(2)}, u32[]{:S(2)}) collective-permute-start(bf16[64,1536]{1,0:T(8,128)(2,1)} %get-tuple-element.149), channel_id=1, source_target_pairs={{0,4},{2,6},{8,0},{10,2},{16,8},{18,10},{24,16},{26,18},{28,24},{3... | collective-permute-start | bytes 589832 | tf_op jit(solution)/shard_map/ppermute | solution.py:97
  355.3 10.4 %collective-permute-start.34 = (f32[2176]{0:T(1024)S(1)}, f32[2176]{0:T(1024)}, u32[]{:S(2)}, u32[]{:S(2)}) collective-permute-start(f32[2176]{0:T(1024)S(1)} %add.168), channel_id=1, source_target_pairs={{0,2},{2,0},{4,6},{6,4},{8,10},{10,8},{12,14},{14,12},{16,18},{18,... | collective-permute-start | bytes 26120 | tf_op jit(solution)/shard_map/ppermute | solution.py:43
  366.4 8.4 %collective-permute-start.41 = (f32[2176]{0:T(1024)S(1)}, f32[2176]{0:T(1024)S(1)}, u32[]{:S(2)}, u32[]{:S(2)}) collective-permute-start(f32[2176]{0:T(1024)S(1)} %add.169), channel_id=1, source_target_pairs={{0,4},{2,6},{8,0},{10,2},{16,8},{18,10},{24,16},{26,18},{28,24},{3... | collective-permute-start | bytes 26120 | tf_op jit(solution)/shard_map/ppermute | solution.py:97
  366.7 8.1 %collective-permute-start.40 = (f32[2176]{0:T(1024)S(1)}, f32[2176]{0:T(1024)S(1)}, u32[]{:S(2)}, u32[]{:S(2)}) collective-permute-start(f32[2176]{0:T(1024)S(1)} %add.169), channel_id=1, source_target_pairs={{0,12},{2,14},{8,4},{10,6},{16,0},{18,2},{24,8},{26,10},{28,16},{3... | collective-permute-start | bytes 26120 | tf_op jit(solution)/shard_map/ppermute | solution.py:97
  366.9 13.1 %collective-permute-start.39 = (f32[2176]{0:T(1024)S(1)}, f32[2176]{0:T(1024)S(1)}, u32[]{:S(2)}, u32[]{:S(2)}) collective-permute-start(f32[2176]{0:T(1024)S(1)} %add.169), channel_id=1, source_target_pairs={{0,20},{2,22},{8,12},{10,14},{16,4},{18,6},{24,0},{26,2},{28,8},{3... | collective-permute-start | bytes 26120 | tf_op jit(solution)/shard_map/ppermute | solution.py:97
  370.2 9.8 %collective-permute-start.38 = (f32[2176]{0:T(1024)S(1)}, f32[2176]{0:T(1024)S(1)}, u32[]{:S(2)}, u32[]{:S(2)}) collective-permute-start(f32[2176]{0:T(1024)S(1)} %add.169), channel_id=1, source_target_pairs={{0,28},{2,30},{8,20},{10,22},{16,12},{18,14},{24,4},{26,6},{28,0},... | collective-permute-start | bytes 26120 | tf_op jit(solution)/shard_map/ppermute | solution.py:97
  371.8 8.2 %collective-permute-start.37 = (f32[2176]{0:T(1024)S(1)}, f32[2176]{0:T(1024)S(1)}, u32[]{:S(2)}, u32[]{:S(2)}) collective-permute-start(f32[2176]{0:T(1024)S(1)} %add.169), channel_id=1, source_target_pairs={{0,24},{2,26},{8,28},{10,30},{16,20},{18,22},{24,12},{26,14},{28,4... | collective-permute-start | bytes 26120 | tf_op jit(solution)/shard_map/ppermute | solution.py:97
  (62 other events, 827.1 us)
Sparse Core Ops, SparseCore 0:
  14.4 123.5 all-gather.1
